TPU v7x, 128 devices: a whole 4x4x4 slice. The times are simulated.
128 devices in a mesh: row: 8 (over x, core), col: 16 (over y, z).
Axes of the slice: x: 4, y: 4, z: 4, core: 2. Of those that a mesh axis runs over, the one named last changes fastest.
Arguments:
- heights: float32 [2048, 4096], P('row', 'col'), may hold values from -2 to 2
- shadow: int32 [2048, 4096], P('row', 'col'), may hold values 0 or 1
- image_tiles: bfloat16 [8192, 256, 256], P(('row', 'col')), may hold values from 0.019897461 to 0.59765625
- image_dest: int32 [8192, 1], P(('row', 'col')), may hold values from 0 to 127; in each aligned block of 64 rows (0 to 63, 64 to 127, ...) at most 2 rows name the same one
- sun_gain: bfloat16 [8192, 4], P(('row', 'col')), may hold values from -1 to 2.5, as said below
- shot_dest: int32 [32768, 1], P(('row', 'col')), may hold values from 0 to 127; in each aligned block of 256 rows (0 to 255, 256 to 511, ...) at most 4 rows name the same one
- shot_pixel: int32 [32768], P(('row', 'col')), may hold values from 0 to 65535
- shot_height: float32 [32768], P(('row', 'col')), may hold values from -2 to 2
Outputs:
- surface: float32 [2048, 4096], P('row', 'col')
Inputs may be any that keep to these rules, and one draw needn't show every extreme that they name: `image_dest`: among one device's 64 image tiles, no tile owner is named more than 2 times. `shot_dest`: among one device's 256 laser shots, no tile owner is named more than 4 times. `sun_gain`: each row is a unit sun direction with elevation between 0.02 and 0.35 radians, followed by a gain between 0.4 and 2.5.
All inputs are finite; a program needn't handle non-finite values. No bound on the sum of `shadow` on one device may be relied on, other than what follows from the above.
Results may differ from a plain program's by a relative error of at most 0.0015.
Values may be sent and summed in bfloat16 or wider, within the bound.
No kernel may reach another device: no remote copies, remote signals or barrier semaphores. Data moves between devices by JAX's collectives and lax.ppermute only.
A program may use at most 256 MiB of HBM per device.

v0:
```python
import jax
import jax.numpy as jnp
from jax import lax
from jax.sharding import PartitionSpec as P

ITERS = 2


sharpness = 8.0
step_size = 0.01
smooth_weight = 2.0
laser_weight = 20.0


def with_halo(value, sides, width):
    for axis, dim in sides:
        devices, length = (lax.axis_size(axis), value.shape[dim])
        up = [(i, (i + 1) % devices) for i in range(devices - 1)]
        down = [(j, i) for i, j in up]
        last = lax.slice_in_dim(value, length - width, length, axis=dim)
        initial = lax.slice_in_dim(value, 0, width, axis=dim)
        before = lax.ppermute(last, axis, up)
        after = lax.ppermute(initial, axis, down)
        value = jnp.concatenate([before, value, after], axis=dim)
    return value


def slot_places(targets, capacity):
    length = targets.shape[0]
    before = jnp.arange(length)[None, :] < jnp.arange(length)[:, None]
    alike = targets[None, :] == targets[:, None]
    order_rank = jnp.sum(jnp.logical_and(before, alike), axis=1)
    return targets * capacity + order_rank


def surface_terms(padded, center):
    slope_x = (padded[1:-1, 2:] - padded[1:-1, :-2]) * 0.5
    slope_y = (padded[2:, 1:-1] - padded[:-2, 1:-1]) * 0.5
    laplace = (
        padded[2:, 1:-1] + padded[:-2, 1:-1] + padded[1:-1, 2:] + padded[1:-1, :-2] - 4.0 * center
    )
    return (slope_x, slope_y, laplace)


def image_terms(slope_x, slope_y, pieces, angles):
    sun_x = angles[:, 0, None, None]
    sun_y = angles[:, 1, None, None]
    sun_z = angles[:, 2, None, None]
    gain = angles[:, 3, None, None]
    inverse = lax.rsqrt(1.0 + slope_x * slope_x + slope_y * slope_y)
    cosine = (sun_z - slope_x * sun_x - slope_y * sun_y) * inverse
    refl = jax.nn.softplus(sharpness * cosine) / sharpness
    sigma = jax.nn.sigmoid(sharpness * cosine)
    along_x = -sun_x * inverse - cosine * slope_x * inverse * inverse
    along_y = -sun_y * inverse - cosine * slope_y * inverse * inverse
    observed = pieces.astype(jnp.float32)
    seen = gain * observed * sigma
    model = gain * gain * refl * sigma
    return (
        seen * along_x,
        seen * along_y,
        model * along_x,
        model * along_y,
        gain * observed * refl,
        gain * gain * refl * refl,
    )


def body(heights, shadow, image_tiles, image_dest, sun_gain, shot_dest, shot_pixel, shot_height):
    row_count = lax.axis_size("row")
    col_count = lax.axis_size("col")
    devices = row_count * col_count
    tile_side = heights.shape[0]
    image_count = image_dest.shape[0]
    image_cap = max(2, 2 * image_count // devices)
    slot_total = devices * image_cap
    places = slot_places(image_dest[:, 0], image_cap)
    send_pixels = (
        jnp.zeros((slot_total, tile_side, tile_side), jnp.bfloat16).at[places].set(image_tiles)
    )
    send_angles = jnp.zeros((slot_total, 4), jnp.bfloat16).at[places].set(sun_gain)
    got_pixels, got_angles = (
        lax.all_to_all(send_pixels, ("row", "col"), split_axis=0, concat_axis=0, tiled=True),
        lax.all_to_all(send_angles, ("row", "col"), split_axis=0, concat_axis=0, tiled=True),
    )
    shot_count = shot_dest.shape[0]
    shot_cap = max(2, 2 * shot_count // devices)
    shot_slots = slot_places(shot_dest[:, 0], shot_cap)
    record = jnp.stack([shot_height, jnp.ones_like(shot_height)], axis=1)
    send_record = jnp.zeros((devices * shot_cap, 2), jnp.float32).at[shot_slots].set(record)
    send_where = jnp.zeros((devices * shot_cap,), jnp.int32).at[shot_slots].set(shot_pixel)
    got_record, got_where = (
        lax.all_to_all(send_record, ("row", "col"), split_axis=0, concat_axis=0, tiled=True),
        lax.all_to_all(send_where, ("row", "col"), split_axis=0, concat_axis=0, tiled=True),
    )
    cells = tile_side * tile_side
    hits = (
        jnp.zeros((cells,), jnp.float32)
        .at[got_where]
        .add(got_record[:, 1])
        .reshape(tile_side, tile_side)
    )
    height_sum = (
        jnp.zeros((cells,), jnp.float32)
        .at[got_where]
        .add(got_record[:, 1] * got_record[:, 0])
        .reshape(tile_side, tile_side)
    )
    lit = 1.0 - shadow.astype(jnp.float32)
    block = 32
    groups = slot_total // block
    grouped_pixels = got_pixels.reshape(groups, block, tile_side, tile_side)
    grouped_angles = got_angles.astype(jnp.float32).reshape(groups, block, 4)
    surface = heights
    for sweep in range(ITERS):
        padded = with_halo(surface, (("row", 0), ("col", 1)), 1)
        slope_x, slope_y, laplace = surface_terms(padded, surface)

        def accumulate(carry, group):
            pieces, angles = group
            terms = image_terms(slope_x, slope_y, pieces, angles)
            return (
                tuple((total + jnp.sum(term, axis=0) for total, term in zip(carry, terms))),
                None,
            )

        start = tuple((jnp.zeros((tile_side, tile_side), jnp.float32) for member in range(6)))
        totals, unused = lax.scan(accumulate, start, (grouped_pixels, grouped_angles))
        obs_x, obs_y, fit_x, fit_y, cross, power = totals
        global_cross, global_power = lax.psum(
            (jnp.sum(lit * cross), jnp.sum(lit * power)), ("row", "col")
        )
        albedo = global_cross / global_power
        grad_x = lit * (albedo * albedo * fit_x - albedo * obs_x)
        grad_y = lit * (albedo * albedo * fit_y - albedo * obs_y)
        rims = with_halo(
            jnp.stack([grad_x, grad_y]).astype(jnp.bfloat16), (("row", 1), ("col", 2)), 1
        ).astype(jnp.float32)
        pad_x = rims[0]
        pad_y = rims[1]
        data = (pad_x[1:-1, :-2] - pad_x[1:-1, 2:]) * 0.5 + (
            pad_y[:-2, 1:-1] - pad_y[2:, 1:-1]
        ) * 0.5
        surface = surface - step_size * (
            data - smooth_weight * laplace + laser_weight * (hits * surface - height_sum)
        )
    return surface


def solution(mesh):
    placed = (
        P("row", "col"),
        P("row", "col"),
        P(("row", "col"), None, None),
        P(("row", "col"), None),
        P(("row", "col"), None),
        P(("row", "col"), None),
        P(("row", "col")),
        P(("row", "col")),
    )
    return jax.shard_map(
        body, mesh=mesh, in_specs=placed, out_specs=P("row", "col"), check_vma=False
    )
```

profile of v0, /device:TPU:1, one launch (start us, length us, event | category | flops | bytes accessed | tf_op | source)
XLA Modules:
  0.0 1150.4 jit_solution(5914371891906477727)
XLA Ops:
  2.4 1.3 scatter_custom_fusion
  3.7 11.5 all-to-all-start
  16.8 1.6 scatter_custom_fusion.2
  19.1 5.6 all-to-all-done
  24.7 4.5 all-to-all-start.2
  29.2 10.9 broadcast_in_dim.7
  40.1 22.2 %scatter_fusion = bf16[256,256,256]{2,1,0:T(8,128)(2,1)} fusion(bf16[256,256,256]{2,1,0:T(8,128)(2,1)} %broadcast_in_dim.7, s32[64]{0:T(128)S(1)} %fusion.41, bf16[64,256,256]{2,1,0:T(8,128)(2,1)} %param.14), kind=kCustom, calls=%fused_computation.1 | custom fusion | bytes 25166080 | tf_op jit(solution)/shard_map/scatter | solution.py:79
  62.3 10.4 all-to-all-start.1
  72.7 3.5 collective-permute-start
  76.2 1.9 collective-permute-start.1
  78.4 1.2 scatter_custom_fusion.3
  79.6 1.5 copy.30
  81.1 466.8 %collective-permute-done = f32[1,256]{1,0:T(1,128)S(1)} collective-permute-done((f32[1,256]{1,0:T(1,128)S(1)}, f32[1,256]{1,0:T(1,128)S(1)}, u32[]{:S(2)}, u32[]{:S(2)}) %collective-permute-start) | collective-permute-done | bytes 1056 | tf_op jit(solution)/shard_map/ppermute | solution.py:22
  548.0 1.3 collective-permute-start.2
  549.3 7.1 collective-permute-start.3
  559.5 55.2 %all-to-all-start.3 = ((f32[128,4,2]{1,2,0:T(2,128)}), f32[128,4,2]{1,2,0:T(2,128)}, u32[]{:S(2)}, u32[]{:S(2)}) async-start(f32[128,4,2]{1,2,0:T(2,128)} %copy.30), calls=%async_computation.3 | async-start | bytes 262144 | tf_op jit(solution)/shard_map/all_to_all | solution.py:93
  614.8 166.7 %while.44 = (s32[]{:T(128)}, f32[256,256]{1,0:T(8,128)S(1)}, f32[256,256]{1,0:T(8,128)S(1)}, f32[256,256]{1,0:T(8,128)S(1)}, f32[256,256]{1,0:T(8,128)S(1)}, /*i...) while((s32[]{:T(128)}, f32[256,256]{1,0:T(8,128)S(1)}, ...), condition=%wide.region_10.11_spmd.clone, body=%wide.region_3.10_spmd.clone.sunk | while | flops 90701952 | bytes 12062497 | solution.py:128
  615.6 18.6 %fusion.51 = (f32[256,256]{1,0:T(8,128)S(1)}, f32[256,256]{1,0:T(8,128)S(1)}, f32[256,256]{1,0:T(8,128)S(1)}, f32[256,256]{1,0:T(8,128)S(1)}, f32[256,256]{1,0:T(8,128)S(1)}, /*index=5*/f32[256,256]{1,0:T(8,128)}) fusion(f32[256,256]{1,0:T(8,128)S(1)} %rsqrt_bitcast_fusion.4, f32[32]{0:T(128)S(1)} %get-tuple-element.754, ...), kind=kLoop, calls=%fused_computation.10.clone.1 | loop fusion | flops 89784320 | bytes 6554500 | tf_op jit(solution)/shard_map/while/body/eval_jaxpr/reduce_sum | solution.py:123
  634.2 1.1 select_add_fusion.20
  636.4 18.6 %fusion.51 = (f32[256,256]{1,0:T(8,128)S(1)}, f32[256,256]{1,0:T(8,128)S(1)}, f32[256,256]{1,0:T(8,128)S(1)}, f32[256,256]{1,0:T(8,128)S(1)}, f32[256,256]{1,0:T(8,128)S(1)}, /*index=5*/f32[256,256]{1,0:T(8,128)}) fusion(f32[256,256]{1,0:T(8,128)S(1)} %rsqrt_bitcast_fusion.4, f32[32]{0:T(128)S(1)} %get-tuple-element.754, ...), kind=kLoop, calls=%fused_computation.10.clone.1 | loop fusion | flops 89784320 | bytes 6554500 | tf_op jit(solution)/shard_map/while/body/eval_jaxpr/reduce_sum | solution.py:123
  655.0 1.1 select_add_fusion.20
  657.2 18.6 %fusion.51 = (f32[256,256]{1,0:T(8,128)S(1)}, f32[256,256]{1,0:T(8,128)S(1)}, f32[256,256]{1,0:T(8,128)S(1)}, f32[256,256]{1,0:T(8,128)S(1)}, f32[256,256]{1,0:T(8,128)S(1)}, /*index=5*/f32[256,256]{1,0:T(8,128)}) fusion(f32[256,256]{1,0:T(8,128)S(1)} %rsqrt_bitcast_fusion.4, f32[32]{0:T(128)S(1)} %get-tuple-element.754, ...), kind=kLoop, calls=%fused_computation.10.clone.1 | loop fusion | flops 89784320 | bytes 6554500 | tf_op jit(solution)/shard_map/while/body/eval_jaxpr/reduce_sum | solution.py:123
  675.9 1.1 select_add_fusion.20
  678.1 18.6 %fusion.51 = (f32[256,256]{1,0:T(8,128)S(1)}, f32[256,256]{1,0:T(8,128)S(1)}, f32[256,256]{1,0:T(8,128)S(1)}, f32[256,256]{1,0:T(8,128)S(1)}, f32[256,256]{1,0:T(8,128)S(1)}, /*index=5*/f32[256,256]{1,0:T(8,128)}) fusion(f32[256,256]{1,0:T(8,128)S(1)} %rsqrt_bitcast_fusion.4, f32[32]{0:T(128)S(1)} %get-tuple-element.754, ...), kind=kLoop, calls=%fused_computation.10.clone.1 | loop fusion | flops 89784320 | bytes 6554500 | tf_op jit(solution)/shard_map/while/body/eval_jaxpr/reduce_sum | solution.py:123
  696.7 1.1 select_add_fusion.20
  698.9 18.6 %fusion.51 = (f32[256,256]{1,0:T(8,128)S(1)}, f32[256,256]{1,0:T(8,128)S(1)}, f32[256,256]{1,0:T(8,128)S(1)}, f32[256,256]{1,0:T(8,128)S(1)}, f32[256,256]{1,0:T(8,128)S(1)}, /*index=5*/f32[256,256]{1,0:T(8,128)}) fusion(f32[256,256]{1,0:T(8,128)S(1)} %rsqrt_bitcast_fusion.4, f32[32]{0:T(128)S(1)} %get-tuple-element.754, ...), kind=kLoop, calls=%fused_computation.10.clone.1 | loop fusion | flops 89784320 | bytes 6554500 | tf_op jit(solution)/shard_map/while/body/eval_jaxpr/reduce_sum | solution.py:123
  717.5 1.1 select_add_fusion.20
  719.7 18.6 %fusion.51 = (f32[256,256]{1,0:T(8,128)S(1)}, f32[256,256]{1,0:T(8,128)S(1)}, f32[256,256]{1,0:T(8,128)S(1)}, f32[256,256]{1,0:T(8,128)S(1)}, f32[256,256]{1,0:T(8,128)S(1)}, /*index=5*/f32[256,256]{1,0:T(8,128)}) fusion(f32[256,256]{1,0:T(8,128)S(1)} %rsqrt_bitcast_fusion.4, f32[32]{0:T(128)S(1)} %get-tuple-element.754, ...), kind=kLoop, calls=%fused_computation.10.clone.1 | loop fusion | flops 89784320 | bytes 6554500 | tf_op jit(solution)/shard_map/while/body/eval_jaxpr/reduce_sum | solution.py:123
  738.4 1.1 select_add_fusion.20
  740.6 18.6 %fusion.51 = (f32[256,256]{1,0:T(8,128)S(1)}, f32[256,256]{1,0:T(8,128)S(1)}, f32[256,256]{1,0:T(8,128)S(1)}, f32[256,256]{1,0:T(8,128)S(1)}, f32[256,256]{1,0:T(8,128)S(1)}, /*index=5*/f32[256,256]{1,0:T(8,128)}) fusion(f32[256,256]{1,0:T(8,128)S(1)} %rsqrt_bitcast_fusion.4, f32[32]{0:T(128)S(1)} %get-tuple-element.754, ...), kind=kLoop, calls=%fused_computation.10.clone.1 | loop fusion | flops 89784320 | bytes 6554500 | tf_op jit(solution)/shard_map/while/body/eval_jaxpr/reduce_sum | solution.py:123
  761.4 18.6 %fusion.51 = (f32[256,256]{1,0:T(8,128)S(1)}, f32[256,256]{1,0:T(8,128)S(1)}, f32[256,256]{1,0:T(8,128)S(1)}, f32[256,256]{1,0:T(8,128)S(1)}, f32[256,256]{1,0:T(8,128)S(1)}, /*index=5*/f32[256,256]{1,0:T(8,128)}) fusion(f32[256,256]{1,0:T(8,128)S(1)} %rsqrt_bitcast_fusion.4, f32[32]{0:T(128)S(1)} %get-tuple-element.754, ...), kind=kLoop, calls=%fused_computation.10.clone.1 | loop fusion | flops 89784320 | bytes 6554500 | tf_op jit(solution)/shard_map/while/body/eval_jaxpr/reduce_sum | solution.py:123
  781.5 1.7 multiply_reduce_fusion.12
  783.3 67.4 %all-reduce.2 = (f32[]{:T(128)}, f32[]{:T(128)}) all-reduce(f32[]{:T(128)} %get-tuple-element.450, f32[]{:T(128)} %get-tuple-element.449), channel_id=1, replica_groups=mesh['row'=8,'col'=16] {'row','col'}, use_global_device_ids=true, to_apply=%region_12.13 | all-reduce | flops 2 | bytes 16 | tf_op jit(solution)/shard_map/psum | solution.py:130
  853.0 2.6 collective-permute-start.4
  855.7 1.9 collective-permute-start.5
  858.7 1.9 collective-permute-done.5
  860.7 2.0 collective-permute-start.6
  862.8 1.3 collective-permute-start.7
  864.1 3.3 scatter_custom_fusion.4
  867.4 3.3 scatter_custom_fusion.5
  871.8 2.2 collective-permute-start.8
  874.1 2.1 collective-permute-start.9
  876.2 2.8 collective-permute-done.9
  879.1 1.3 collective-permute-start.10
  880.4 4.9 collective-permute-start.11
  885.8 1.5 collective-permute-done.11
  888.3 166.6 %while.45 = (s32[]{:T(128)}, f32[256,256]{1,0:T(8,128)S(1)}, f32[256,256]{1,0:T(8,128)S(1)}, f32[256,256]{1,0:T(8,128)S(1)}, f32[256,256]{1,0:T(8,128)S(1)}, /*i...) while((s32[]{:T(128)}, f32[256,256]{1,0:T(8,128)S(1)}, ...), condition=%wide.region_27.28_spmd.clone, body=%wide.region_20.27_spmd.clone.sunk | while | flops 90701952 | bytes 12062497 | solution.py:128
  889.0 18.6 %fusion.52 = (f32[256,256]{1,0:T(8,128)S(1)}, f32[256,256]{1,0:T(8,128)S(1)}, f32[256,256]{1,0:T(8,128)S(1)}, f32[256,256]{1,0:T(8,128)S(1)}, f32[256,256]{1,0:T(8,128)S(1)}, /*index=5*/f32[256,256]{1,0:T(8,128)}) fusion(f32[256,256]{1,0:T(8,128)S(1)} %rsqrt_bitcast_fusion.5, f32[32]{0:T(128)S(1)} %get-tuple-element.786, ...), kind=kLoop, calls=%fused_computation.41.clone.1 | loop fusion | flops 89784320 | bytes 6554500 | tf_op jit(solution)/shard_map/while/body/eval_jaxpr/reduce_sum | solution.py:123
  909.9 18.6 %fusion.52 = (f32[256,256]{1,0:T(8,128)S(1)}, f32[256,256]{1,0:T(8,128)S(1)}, f32[256,256]{1,0:T(8,128)S(1)}, f32[256,256]{1,0:T(8,128)S(1)}, f32[256,256]{1,0:T(8,128)S(1)}, /*index=5*/f32[256,256]{1,0:T(8,128)}) fusion(f32[256,256]{1,0:T(8,128)S(1)} %rsqrt_bitcast_fusion.5, f32[32]{0:T(128)S(1)} %get-tuple-element.786, ...), kind=kLoop, calls=%fused_computation.41.clone.1 | loop fusion | flops 89784320 | bytes 6554500 | tf_op jit(solution)/shard_map/while/body/eval_jaxpr/reduce_sum | solution.py:123
  930.7 18.6 %fusion.52 = (f32[256,256]{1,0:T(8,128)S(1)}, f32[256,256]{1,0:T(8,128)S(1)}, f32[256,256]{1,0:T(8,128)S(1)}, f32[256,256]{1,0:T(8,128)S(1)}, f32[256,256]{1,0:T(8,128)S(1)}, /*index=5*/f32[256,256]{1,0:T(8,128)}) fusion(f32[256,256]{1,0:T(8,128)S(1)} %rsqrt_bitcast_fusion.5, f32[32]{0:T(128)S(1)} %get-tuple-element.786, ...), kind=kLoop, calls=%fused_computation.41.clone.1 | loop fusion | flops 89784320 | bytes 6554500 | tf_op jit(solution)/shard_map/while/body/eval_jaxpr/reduce_sum | solution.py:123
  951.5 18.6 %fusion.52 = (f32[256,256]{1,0:T(8,128)S(1)}, f32[256,256]{1,0:T(8,128)S(1)}, f32[256,256]{1,0:T(8,128)S(1)}, f32[256,256]{1,0:T(8,128)S(1)}, f32[256,256]{1,0:T(8,128)S(1)}, /*index=5*/f32[256,256]{1,0:T(8,128)}) fusion(f32[256,256]{1,0:T(8,128)S(1)} %rsqrt_bitcast_fusion.5, f32[32]{0:T(128)S(1)} %get-tuple-element.786, ...), kind=kLoop, calls=%fused_computation.41.clone.1 | loop fusion | flops 89784320 | bytes 6554500 | tf_op jit(solution)/shard_map/while/body/eval_jaxpr/reduce_sum | solution.py:123
  972.4 18.6 %fusion.52 = (f32[256,256]{1,0:T(8,128)S(1)}, f32[256,256]{1,0:T(8,128)S(1)}, f32[256,256]{1,0:T(8,128)S(1)}, f32[256,256]{1,0:T(8,128)S(1)}, f32[256,256]{1,0:T(8,128)S(1)}, /*index=5*/f32[256,256]{1,0:T(8,128)}) fusion(f32[256,256]{1,0:T(8,128)S(1)} %rsqrt_bitcast_fusion.5, f32[32]{0:T(128)S(1)} %get-tuple-element.786, ...), kind=kLoop, calls=%fused_computation.41.clone.1 | loop fusion | flops 89784320 | bytes 6554500 | tf_op jit(solution)/shard_map/while/body/eval_jaxpr/reduce_sum | solution.py:123
  993.2 18.6 %fusion.52 = (f32[256,256]{1,0:T(8,128)S(1)}, f32[256,256]{1,0:T(8,128)S(1)}, f32[256,256]{1,0:T(8,128)S(1)}, f32[256,256]{1,0:T(8,128)S(1)}, f32[256,256]{1,0:T(8,128)S(1)}, /*index=5*/f32[256,256]{1,0:T(8,128)}) fusion(f32[256,256]{1,0:T(8,128)S(1)} %rsqrt_bitcast_fusion.5, f32[32]{0:T(128)S(1)} %get-tuple-element.786, ...), kind=kLoop, calls=%fused_computation.41.clone.1 | loop fusion | flops 89784320 | bytes 6554500 | tf_op jit(solution)/shard_map/while/body/eval_jaxpr/reduce_sum | solution.py:123
  1014.0 18.6 %fusion.52 = (f32[256,256]{1,0:T(8,128)S(1)}, f32[256,256]{1,0:T(8,128)S(1)}, f32[256,256]{1,0:T(8,128)S(1)}, f32[256,256]{1,0:T(8,128)S(1)}, f32[256,256]{1,0:T(8,128)S(1)}, /*index=5*/f32[256,256]{1,0:T(8,128)}) fusion(f32[256,256]{1,0:T(8,128)S(1)} %rsqrt_bitcast_fusion.5, f32[32]{0:T(128)S(1)} %get-tuple-element.786, ...), kind=kLoop, calls=%fused_computation.41.clone.1 | loop fusion | flops 89784320 | bytes 6554500 | tf_op jit(solution)/shard_map/while/body/eval_jaxpr/reduce_sum | solution.py:123
  1034.9 18.6 %fusion.52 = (f32[256,256]{1,0:T(8,128)S(1)}, f32[256,256]{1,0:T(8,128)S(1)}, f32[256,256]{1,0:T(8,128)S(1)}, f32[256,256]{1,0:T(8,128)S(1)}, f32[256,256]{1,0:T(8,128)S(1)}, /*index=5*/f32[256,256]{1,0:T(8,128)}) fusion(f32[256,256]{1,0:T(8,128)S(1)} %rsqrt_bitcast_fusion.5, f32[32]{0:T(128)S(1)} %get-tuple-element.786, ...), kind=kLoop, calls=%fused_computation.41.clone.1 | loop fusion | flops 89784320 | bytes 6554500 | tf_op jit(solution)/shard_map/while/body/eval_jaxpr/reduce_sum | solution.py:123
  1054.9 1.7 multiply_reduce_fusion.10
  1056.6 71.1 %all-reduce.1 = (f32[]{:T(128)}, f32[]{:T(128)}) all-reduce(f32[]{:T(128)} %get-tuple-element.448, f32[]{:T(128)} %get-tuple-element.447), channel_id=1, replica_groups=mesh['row'=8,'col'=16] {'row','col'}, use_global_device_ids=true, to_apply=%region_29.30 | all-reduce | flops 2 | bytes 16 | tf_op jit(solution)/shard_map/psum | solution.py:130
  1130.1 4.8 collective-permute-start.12
  1134.9 1.9 collective-permute-start.13
  1136.9 3.0 collective-permute-done.13
  1140.0 1.3 collective-permute-start.14
  1141.3 1.3 collective-permute-start.15
  1143.3 3.9 collective-permute-done.15
  1147.5 2.9 fusion.17
  (189 shorter events, 42.9 us)
Async XLA Ops:
  3.7 21.0 %all-to-all-start = ((bf16[128,2,4]{2,1,0:T(2,128)(2,1)}), bf16[128,2,4]{2,1,0:T(2,128)(2,1)S(1)}, u32[]{:S(2)}, u32[]{:S(2)}) async-start(bf16[128,2,4]{2,1,0:T(2,128)(2,1)} %bitcast.3), calls=%async_computation | async-start | bytes 131072 | tf_op jit(solution)/shard_map/all_to_all | solution.py:84
  24.7 37.6 %all-to-all-start.2 = ((s32[128,4,1]{1,2,0:T(1,128)}), s32[128,4,1]{1,2,0:T(1,128)S(1)}, u32[]{:S(2)}, u32[]{:S(2)}) async-start(s32[128,4,1]{1,2,0:T(1,128)} %bitcast.15), calls=%async_computation.2 | async-start | bytes 131072 | tf_op jit(solution)/shard_map/all_to_all | solution.py:94
  62.3 10.4 copy-start.1
  62.3 15.9 %copy-start.8 = (f32[256]{0:T(256)S(1)}, f32[256]{0:T(256)}, u32[]{:S(2)}) copy-start(f32[256]{0:T(256)} %param.19) | copy-start | bytes 3076
  62.3 497.2 %all-to-all-start.1 = ((bf16[256,256,256]{2,1,0:T(8,128)(2,1)}), bf16[256,256,256]{2,1,0:T(8,128)(2,1)}, u32[]{:S(2)}, u32[]{:S(2)}) async-start(bf16[256,256,256]{2,1,0:T(8,128)(2,1)} %scatter_fusion), calls=%async_computation.1 | async-start | bytes 67108864 | tf_op jit(solution)/shard_map/all_to_all | solution.py:83
  72.7 475.2 %collective-permute-start = (f32[1,256]{1,0:T(1,128)S(1)}, f32[1,256]{1,0:T(1,128)S(1)}, u32[]{:S(2)}, u32[]{:S(2)}) collective-permute-start(f32[1,256]{1,0:T(1,128)S(1)} %get-tuple-element.567), channel_id=1, source_target_pairs={{0,16},{16,32},{32,48},{48,64},{64,80},{80,96},{96,112},{1,17},{17... | collective-permute-start | bytes 3080 | tf_op jit(solution)/shard_map/ppermute | solution.py:22
  76.2 471.6 %collective-permute-start.1 = (f32[1,256]{1,0:T(1,128)S(1)}, f32[1,256]{1,0:T(1,128)S(1)}, u32[]{:S(2)}, u32[]{:S(2)}) collective-permute-start(f32[1,256]{1,0:T(1,128)S(1)} %get-tuple-element.568), channel_id=1, source_target_pairs={{16,0},{32,16},{48,32},{64,48},{80,64},{96,80},{112,96},{17,1},{33... | collective-permute-start | bytes 3080 | tf_op jit(solution)/shard_map/ppermute | solution.py:23
  548.0 10.5 collective-permute-start.2
  549.3 9.3 collective-permute-start.3
  558.6 56.2 %copy-start.5 = (f32[258,1]{1,0:T(8,128)}, f32[258,1]{1,0:T(8,128)S(1)}, u32[]{:S(2)}) copy-start(f32[258,1]{1,0:T(8,128)S(1)} %collective-permute-done.3) | copy-start | bytes 3100
  559.5 298.1 %all-to-all-start.3 = ((f32[128,4,2]{1,2,0:T(2,128)}), f32[128,4,2]{1,2,0:T(2,128)}, u32[]{:S(2)}, u32[]{:S(2)}) async-start(f32[128,4,2]{1,2,0:T(2,128)} %copy.30), calls=%async_computation.3 | async-start | bytes 262144 | tf_op jit(solution)/shard_map/all_to_all | solution.py:93
  781.5 89.8 %copy-start.2 = (f32[256,256]{1,0:T(8,128)S(1)}, f32[256,256]{1,0:T(8,128)}, u32[]{:S(2)}) copy-start(f32[256,256]{1,0:T(8,128)} %param.12) | copy-start | bytes 786436
  781.5 89.8 %copy-start.6 = (f32[258,1]{1,0:T(8,128)S(1)}, f32[258,1]{1,0:T(8,128)}, u32[]{:S(2)}) copy-start(f32[258,1]{1,0:T(8,128)} %copy-done.5) | copy-start | bytes 3100
  853.0 5.6 collective-permute-start.4
  855.7 4.9 collective-permute-start.5
  860.7 10.2 collective-permute-start.6
  862.8 8.2 collective-permute-start.7
  870.8 14.9 %copy-start.3 = (f32[256,256]{1,0:T(8,128)}, f32[256,256]{1,0:T(8,128)S(1)}, u32[]{:S(2)}) copy-start(f32[256,256]{1,0:T(8,128)S(1)} %reshape.155) | copy-start | bytes 786436
  870.9 14.4 %copy-start.4 = (f32[256,256]{1,0:T(8,128)}, f32[256,256]{1,0:T(8,128)S(1)}, u32[]{:S(2)}) copy-start(f32[256,256]{1,0:T(8,128)S(1)} %reshape.154) | copy-start | bytes 786436
  871.8 16.5 %copy-start = (f32[256,256]{1,0:T(8,128)}, f32[256,256]{1,0:T(8,128)S(1)}, u32[]{:S(2)}) copy-start(f32[256,256]{1,0:T(8,128)S(1)} %fusion.23) | copy-start | bytes 786436
  871.8 4.3 collective-permute-start.8
  874.1 4.9 collective-permute-start.9
  879.1 6.7 collective-permute-start.10
  880.4 6.9 collective-permute-start.11
  887.3 1.0 copy-start.7
  1130.1 6.7 collective-permute-start.12
  1134.9 4.9 collective-permute-start.13
  1140.0 3.3 collective-permute-start.14
  1141.3 5.8 collective-permute-start.15
where the time goes:
time: 1150 us
  waiting for transfers between devices  486 us (42%)
  other arithmetic  344 us (30%)
  blocking collectives  139 us (12%)
  starting transfers between devices  123 us (11%)
  local copies, waits for them, and re-layouts  54.4 us (5%)
    ppermute x8, waiting for transfers between devices, with_halo(): before = lax.ppermute(last, axis, up)  469 us
    reduce_sum x16, other arithmetic, accumulate(): jnp.sum(term, axis=0)  298 us
    psum x2, blocking collectives, body(): lax.psum((jnp.sum(lit * cross), jnp.sum(lit * power)), ('row', 'col'))  139 us
    all_to_all x1, starting transfers between devices, body(): lax.all_to_all(send_record, ('row', 'col'), split_axis=0, concat_axis=0,...  55.2 us
    ppermute x8, starting transfers between devices, with_halo(): before = lax.ppermute(last, axis, up)  28.5 us
  transfers between devices with their start and end apart: 20, of which 9 were waited for; matrix products, arithmetic and copies ran while one was open for 19% of the time, Pallas kernels for 0%

commit v1 on v0

v1 whole, which is shorter than its diff:
```python
import functools

import jax
import jax.numpy as jnp
from jax import lax
from jax.experimental import pallas as pl
from jax.experimental.pallas import tpu as pltpu
from jax.sharding import PartitionSpec as P

ITERS = 2

sharpness = 8.0
step_size = 0.01
smooth_weight = 2.0
laser_weight = 20.0

AXES = ("row", "col")
DEVICES = 128
N_COL = 16
TILE = 256
IMG = 64
SLAB = 512
LANES = 128
PIX_ROWS = IMG * SLAB // LANES
EXTRA = 24
REPLY = 32
SHOT_CAP = 4
F32 = jnp.float32
BF16 = jnp.bfloat16


def exchange(value):
    return lax.all_to_all(value, AXES, split_axis=0, concat_axis=0, tiled=True)


def pieces_of(value, count):
    out = []
    for member in range(count):
        head = lax.reduce_precision(value, 8, 7)
        out.append(head.astype(BF16))
        value = value - head
    return out


def edges(value):
    out = []
    for axis, dim in (("row", 0), ("col", 1)):
        devices, length = (lax.axis_size(axis), value.shape[dim])
        up = [(i, (i + 1) % devices) for i in range(devices - 1)]
        down = [(j, i) for i, j in up]
        last = lax.slice_in_dim(value, length - 1, length, axis=dim)
        first = lax.slice_in_dim(value, 0, 1, axis=dim)
        out.append(lax.ppermute(last, axis, up))
        out.append(lax.ppermute(first, axis, down))
    return out


def laplacian(value, rims):
    above, below, left, right = rims
    tall = jnp.concatenate([above, value, below], axis=0)
    wide = jnp.concatenate([left, value, right], axis=1)
    return tall[2:] + tall[:-2] + wide[:, 2:] + wide[:, :-2] - 4.0 * value


def total_of(terms):
    return (terms[0].astype(F32) + terms[1].astype(F32)) + terms[2].astype(F32)


def own_albedo(cross, power):
    return jnp.where(power > 0.0, cross / jnp.where(power > 0.0, power, 1.0), 0.0)


PACK_ROWS = 16


def pack_kernel(images_ref, extra_ref, out_ref):
    side = 16 * PACK_ROWS
    to = lax.broadcasted_iota(jnp.int32, (side, side), 0)
    source = lax.broadcasted_iota(jnp.int32, (side, side), 1)
    move = jnp.where((to % 16) * 16 + to // 16 == source, 1.0, 0.0).astype(BF16)
    for group in range(IMG // 16):
        block = images_ref[group * 16 : group * 16 + 16].reshape(side, TILE)
        turned = jnp.dot(move, block, preferred_element_type=F32).astype(BF16)
        for r in range(PACK_ROWS):
            for half in range(TILE // LANES):
                quarter = (r % 2) * 2 + half
                place = quarter * IMG + group * 16
                out_ref[r // 2, place : place + 16, :] = turned[
                    r * 16 : r * 16 + 16, half * LANES : half * LANES + LANES
                ]
    out_ref[:, PIX_ROWS : PIX_ROWS + EXTRA, :] = extra_ref[...]


def pack(images, extra):
    per_step = PACK_ROWS * TILE // SLAB
    return pl.pallas_call(
        pack_kernel,
        grid=(DEVICES // per_step,),
        in_specs=[
            pl.BlockSpec((IMG, PACK_ROWS, TILE), lambda s: (0, s, 0)),
            pl.BlockSpec((per_step, EXTRA, LANES), lambda s: (s, 0, 0)),
        ],
        out_specs=pl.BlockSpec((per_step, PIX_ROWS + EXTRA, LANES), lambda s: (s, 0, 0)),
        out_shape=jax.ShapeDtypeStruct((DEVICES, PIX_ROWS + EXTRA, LANES), BF16),
        compiler_params=pltpu.CompilerParams(vmem_limit_bytes=48 * 1024 * 1024),
    )(images, extra)


SUM_SRC = 8
SUM_IMG = SUM_SRC * IMG


def sum_kernel(meta_ref, pixels_ref, normal_ref, sums_ref, plain_ref):
    @pl.when(pl.program_id(0) == 0)
    def start():
        sums_ref[...] = jnp.zeros_like(sums_ref)
        plain_ref[...] = jnp.zeros_like(plain_ref)

    meta = meta_ref[...]
    cols = meta.T
    lane = lax.broadcasted_iota(jnp.int32, (SUM_IMG, DEVICES), 1).astype(F32)
    hot = lane == cols[:, 0:1]
    pick = jnp.concatenate(
        [jnp.where(hot, cols[:, j : j + 1], 0.0).astype(BF16) for j in (1, 2, 3)] * 2, axis=1
    )
    sub = lax.broadcasted_iota(jnp.int32, (DEVICES, SUM_IMG), 0).astype(F32)
    hot_t = sub == meta[0:1, :]
    pick_t = jnp.concatenate(
        [jnp.where(hot_t, meta[j : j + 1, :], 0.0).astype(BF16) for j in (1, 2, 3)], axis=0
    )
    ones_t = jnp.where(hot_t, 1.0, 0.0).astype(BF16)
    gain = cols[:, 4:5]

    half_angle = jnp.dot(pick, normal_ref[...], preferred_element_type=F32)
    bend = jnp.tanh(half_angle)
    rest = 0.5 - 0.5 * bend
    refl = jnp.log(rest) * (gain * (-1.0 / sharpness))
    sigma = (0.5 + 0.5 * bend) * gain
    seen = jnp.concatenate(
        [
            pixels_ref[:, q * IMG : q * IMG + IMG, :].reshape(SUM_IMG, LANES)
            for q in range(SLAB // LANES)
        ],
        axis=1,
    ).astype(F32)
    weighted = jnp.concatenate([(seen * sigma).astype(BF16), (refl * sigma).astype(BF16)], axis=1)
    squares = jnp.concatenate([(seen * refl).astype(BF16), (refl * refl).astype(BF16)], axis=1)
    sums_ref[...] += jnp.dot(pick_t, weighted, preferred_element_type=F32)
    plain_ref[...] += jnp.dot(ones_t, squares, preferred_element_type=F32)


def image_sums(meta, pixels, normals):
    return pl.pallas_call(
        sum_kernel,
        grid=(DEVICES // SUM_SRC,),
        in_specs=[
            pl.BlockSpec((8, SUM_IMG), lambda s: (0, s)),
            pl.BlockSpec((SUM_SRC, PIX_ROWS + EXTRA, LANES), lambda s: (s, 0, 0)),
            pl.BlockSpec((6 * DEVICES, SLAB), lambda s: (0, 0)),
        ],
        out_specs=[
            pl.BlockSpec((3 * DEVICES, 2 * SLAB), lambda s: (0, 0)),
            pl.BlockSpec((DEVICES, 2 * SLAB), lambda s: (0, 0)),
        ],
        out_shape=[
            jax.ShapeDtypeStruct((3 * DEVICES, 2 * SLAB), F32),
            jax.ShapeDtypeStruct((DEVICES, 2 * SLAB), F32),
        ],
        compiler_params=pltpu.CompilerParams(vmem_limit_bytes=56 * 1024 * 1024),
    )(meta, pixels, normals)


def shift_tiles(value, count):
    pad = jnp.zeros((abs(count),) + value.shape[1:], value.dtype)
    if count > 0:
        return jnp.concatenate([pad, value[:-count]], axis=0)
    return jnp.concatenate([value[-count:], pad], axis=0)


def central_x(value):
    column = lax.broadcasted_iota(jnp.int32, (DEVICES, 1), 0) % N_COL
    before = jnp.where(column == 0, 0.0, shift_tiles(value[:, -1:], 1))
    after = jnp.where(column == N_COL - 1, 0.0, shift_tiles(value[:, :1], -1))
    wide = jnp.concatenate([before, value, after], axis=1)
    return wide[:, 2:] - wide[:, :-2]


def slab_slopes(rows, me):
    top = jnp.where(me == 0, shift_tiles(rows[0], N_COL), rows[0])
    bottom = jnp.where(me == DEVICES - 1, shift_tiles(rows[3], -N_COL), rows[3])
    slope_x = jnp.concatenate([central_x(rows[1]), central_x(rows[2])], axis=1) * 0.5
    slope_y = jnp.concatenate([rows[2] - top, bottom - rows[1]], axis=1) * 0.5
    return slope_x, slope_y


def slab_pass(rows, lit, meta, pixels, me):
    slope_x, slope_y = slab_slopes(rows, me)
    inverse = lax.rsqrt(1.0 + slope_x * slope_x + slope_y * slope_y)
    scale = 0.5 * sharpness
    normals = jnp.concatenate(
        [-slope_x * inverse * scale, -slope_y * inverse * scale, inverse * scale], axis=0
    )
    sums, plain = image_sums(meta, pixels, jnp.concatenate(pieces_of(normals, 2), axis=0))
    cross = pieces_of(jnp.sum(lit * plain[:, :SLAB]), 3)
    power = pieces_of(jnp.sum(lit * plain[:, SLAB:]), 3)
    guess = own_albedo(total_of(cross), total_of(power))
    fields = []
    for part in range(2):
        by_x, by_y, by_z = (
            sums[j * DEVICES : (j + 1) * DEVICES, part * SLAB : (part + 1) * SLAB] for j in range(3)
        )
        turned = (by_z - slope_x * by_x - slope_y * by_y) * inverse * inverse * inverse
        grad_x = -lit * (by_x * inverse + slope_x * turned)
        grad_y = -lit * (by_y * inverse + slope_y * turned)
        across = jnp.concatenate([central_x(grad_x[:, :TILE]), central_x(grad_x[:, TILE:])], axis=1)
        halo = jnp.where(
            me == 0, shift_tiles(grad_y[:, :TILE], -N_COL), shift_tiles(grad_y[:, TILE:], N_COL)
        )
        fields.append(jnp.concatenate([across * (-0.5), grad_y, halo], axis=1))
    seen, model = fields
    scalars = jnp.broadcast_to(jnp.stack(cross + power)[None, :], (DEVICES, 6))
    flat = jnp.concatenate(
        [model.astype(BF16)]
        + pieces_of(guess * model - seen, 2)
        + [scalars, jnp.zeros((DEVICES, 2 * LANES - 6), BF16)],
        axis=1,
    )
    return flat.reshape(DEVICES, REPLY, LANES)


def owner_data(got):
    flat = got.reshape(DEVICES, REPLY * LANES).astype(F32)
    width = 2 * SLAB + TILE
    terms = flat[:, 3 * width : 3 * width + 6]
    cross = terms[:, 0:1] + terms[:, 1:2] + terms[:, 2:3]
    power = terms[:, 3:4] + terms[:, 4:5] + terms[:, 5:6]
    guess = own_albedo(cross, power)
    albedo = jnp.sum(cross) / jnp.sum(power)
    model = flat[:, :width]
    misfit = flat[:, width : 2 * width] + flat[:, 2 * width : 3 * width]
    grad = albedo * misfit + albedo * (albedo - guess) * model
    across = grad[:, :SLAB].reshape(TILE, TILE)
    along = grad[:, SLAB : 2 * SLAB].reshape(TILE, TILE)
    halo = grad[:, 2 * SLAB :]
    tall = jnp.concatenate([halo[-1:], along, halo[:1]], axis=0)
    return across + (tall[:-2] - tall[2:]) * 0.5


def slab_rows(surface):
    tall = jnp.concatenate([surface[-1:], surface, surface[:1]], axis=0)
    four = jnp.stack([tall[j : j + TILE : 2] for j in range(4)], axis=1).reshape(DEVICES, 8, LANES)
    return jnp.concatenate(pieces_of(four, 2), axis=1)


def shot_sums(slots):
    cell = lax.broadcasted_iota(jnp.int32, (1, TILE), 1).astype(F32)
    present = slots[:, 4:5]
    in_row = jnp.where(slots[:, 0:1] == cell, 1.0, 0.0)
    in_col = jnp.where(slots[:, 1:2] == cell, 1.0, 0.0).astype(BF16)
    left = jnp.concatenate([in_row * slots[:, j : j + 1] * present for j in (4, 2, 3)], axis=1)
    both = lax.dot_general(
        left.astype(BF16), in_col, (((0,), (0,)), ((), ())), preferred_element_type=F32
    )
    return both[:TILE], both[TILE : 2 * TILE] + both[2 * TILE :]


def shot_slots(shot_dest, shot_pixel, shot_height):
    count = shot_dest.shape[0]
    target = shot_dest[:, 0]
    before = jnp.arange(count)[None, :] < jnp.arange(count)[:, None]
    alike = target[None, :] == target[:, None]
    rank = jnp.sum(jnp.logical_and(before, alike), axis=1)
    place = target * SHOT_CAP + rank
    slots = jnp.arange(DEVICES * SHOT_CAP)[:, None] == place[None, :]
    high, low = pieces_of(shot_height, 2)
    record = jnp.stack(
        [
            (shot_pixel // TILE).astype(BF16),
            (shot_pixel % TILE).astype(BF16),
            high,
            low,
            jnp.ones_like(high),
        ],
        axis=1,
    )
    got = jnp.dot(slots.astype(BF16), record, preferred_element_type=F32).astype(BF16)
    return got.reshape(DEVICES, SHOT_CAP * 5)


def body(heights, shadow, image_tiles, image_dest, sun_gain, shot_dest, shot_pixel, shot_height):
    me = lax.axis_index("row") * N_COL + lax.axis_index("col")
    lit = 1.0 - shadow.astype(F32)
    rims = edges(heights)

    def fan(value):
        return jnp.broadcast_to(value[None], (DEVICES,) + value.shape)

    dest = image_dest[:, 0].astype(BF16)
    shots = shot_slots(shot_dest, shot_pixel, shot_height)
    extra = jnp.concatenate(
        [
            slab_rows(heights),
            lit.astype(BF16).reshape(DEVICES, 4, LANES),
            fan(jnp.concatenate([dest, jnp.zeros_like(dest)])[None]),
            fan(sun_gain.T.reshape(2, LANES)),
            jnp.pad(shots, ((0, 0), (0, LANES - shots.shape[1])))[:, None, :],
        ],
        axis=1,
    )
    pixels = exchange(pack(image_tiles, extra))
    extra = pixels[:, PIX_ROWS:, :]
    meta = jnp.stack(
        [
            extra[:, 20, :IMG],
            extra[:, 21, :IMG],
            extra[:, 21, IMG:],
            extra[:, 22, :IMG],
            extra[:, 22, IMG:],
        ]
    ).astype(F32)
    meta = jnp.pad(meta.reshape(5, DEVICES * IMG), ((0, 3), (0, 0)))
    slab_lit = extra[:, 16:20, :].reshape(DEVICES, SLAB).astype(F32)
    around = extra[:, 0:16, :]
    slots = extra[:, 23, : SHOT_CAP * 5].reshape(DEVICES * SHOT_CAP, 5).astype(F32)
    hits, height_sum = shot_sums(slots)
    surface = heights
    for sweep in range(ITERS):
        if sweep > 0:
            around = exchange(slab_rows(surface))
            rims = edges(surface)
        fine = (around[:, :8].astype(F32) + around[:, 8:].astype(F32)).reshape(DEVICES, 4, TILE)
        rows = [fine[:, j] for j in range(4)]
        got = exchange(slab_pass(rows, slab_lit, meta, pixels, me))
        data = owner_data(got)
        laplace = laplacian(surface, rims)
        surface = surface - step_size * (
            data - smooth_weight * laplace + laser_weight * (hits * surface - height_sum)
        )
    return surface


def solution(mesh):
    placed = (
        P("row", "col"),
        P("row", "col"),
        P(("row", "col"), None, None),
        P(("row", "col"), None),
        P(("row", "col"), None),
        P(("row", "col"), None),
        P(("row", "col")),
        P(("row", "col")),
    )
    return jax.shard_map(
        body, mesh=mesh, in_specs=placed, out_specs=P("row", "col"), check_vma=False
    )
```

time: 1150 us -> 355 us (0.31)
  waiting for transfers between devices: 486 us -> 126 us
  other arithmetic: 344 us -> 24 us
  blocking collectives: 139 us -> 18.1 us
  Pallas kernels: 0 us -> 80.4 us
  starting transfers between devices: 123 us -> 47.7 us
  local copies, waits for them, and re-layouts: 54.4 us -> 26.6 us
  between operations: 3.24 us -> 28.4 us
    ppermute x16 -> x8, waiting for transfers between devices: 481 us -> 0.02 us  [the longest x4 0.01 us: edges(): out.append(lax.ppermute(first, axis, down))]
    reduce_sum x20 -> x5, other arithmetic: 303 us -> 7.04 us  [the longest x2 5.21 us: slab_pass(): cross = pieces_of(jnp.sum(lit * plain[:, :SLAB]), 3)]
    psum x2 -> x0, blocking collectives: 139 us -> none  [body(): lax.psum((jnp.sum(lit * cross), jnp.sum(lit * power)), ('row', 'col'))]
    all_to_all x4 -> x3, waiting for transfers between devices: 5.6 us -> 126 us  [exchange(): return lax.all_to_all(value, AXES, split_axis=0, concat_axis=0, tiled=True)]
    pallas_call x0 -> x3, Pallas kernels: none -> 80.4 us  [the longest x2 66.2 us: image_sums(): pl.pallas_call(sum_kernel, grid=(DEVICES // SUM_SRC,), in_specs=[pl.Block...]
    all_to_all x4 -> x3, starting transfers between devices: 81.6 us -> 24.5 us  [exchange(): return lax.all_to_all(value, AXES, split_axis=0, concat_axis=0, tiled=True)]
    scatter x4 -> x0, local copies, waits for them, and re-layouts: 26.3 us -> none  [the longest x1 22.2 us: body(): jnp.zeros((slot_total, tile_side, tile_side), jnp.bfloat16).at[places]]
    add x48 -> x5, other arithmetic: 22.7 us -> 1.43 us  [the longest x2 1.15 us: body(): around[:, :8].astype(F32) + around[:, 8:].astype(F32)]
  transfers between devices with their start and end apart: 20 -> 11, of which waited for: 9 -> 3; matrix products, arithmetic and copies ran while one was open for 19% -> 8% of each run, Pallas kernels for 0% -> 9%
where the time goes in v1:
time: 355 us; the launch traced here: 353 us
  waiting for transfers between devices  126 us (35%)
  Pallas kernels  80.4 us (23%)
  starting transfers between devices  47.7 us (13%)
  between operations  28.4 us (8%)
  local copies, waits for them, and re-layouts  26.6 us (7%)
  other arithmetic  24 us (7%)
  blocking collectives  18.1 us (5%)
    all_to_all x3, waiting for transfers between devices, exchange(): return lax.all_to_all(value, AXES, split_axis=0, concat_axis=0, tiled=True)  126 us
    pallas_call x2, Pallas kernels, image_sums(): pl.pallas_call(sum_kernel, grid=(DEVICES // SUM_SRC,), in_specs=[pl.Block...  66.2 us
    all_to_all x3, starting transfers between devices, exchange(): return lax.all_to_all(value, AXES, split_axis=0, concat_axis=0, tiled=True)  24.5 us
    all_to_all x1, blocking collectives, exchange(): return lax.all_to_all(value, AXES, split_axis=0, concat_axis=0, tiled=True)  18.1 us
    ppermute x4, starting transfers between devices, edges(): out.append(lax.ppermute(last, axis, up))  14.5 us
    pallas_call x1, Pallas kernels, pack(): pl.pallas_call(pack_kernel, grid=(DEVICES // per_step,), in_specs=[pl.Blo...  14.2 us
    ppermute x4, starting transfers between devices, edges(): out.append(lax.ppermute(first, axis, down))  8.72 us
    unnamed x66, local copies, waits for them, and re-layouts  8.1 us
  transfers between devices with their start and end apart: 11, of which 3 were waited for; matrix products, arithmetic and copies ran while one was open for 8% of the time, Pallas kernels for 9%

profile of v1, /device:TPU:1, one launch (start us, length us, event | category | flops | bytes accessed | tf_op | source)
XLA Modules:
  0.0 353.1 jit_solution(9745858199985078750)
XLA Ops:
  0.0 0.7 fusion.154
  0.7 1.0 pad_maximum_fusion.33
  2.1 1.0 slice.667
  3.2 0.3 copy.96
  3.5 0.2 reshape.791
  5.1 0.7 concatenate.502.extra_ref
  5.8 14.2 %shard_map.82 = bf16[128,280,128]{2,1,0:T(8,128)(2,1)} custom-call(bf16[64,256,256]{2,1,0:T(8,128)(2,1)} %images_ref.1, bf16[128,24,128]{2,1,0:T(8,128)(2,1)S(1)} %concatenate.502.extra_ref), custom_call_target="tpu_custom_call" | custom-call | tf_op jit(solution)/shard_map/pallas_call | solution.py:96
  20.0 11.9 %all-to-all-start = ((bf16[128,280,128]{2,1,0:T(8,128)(2,1)}), bf16[128,280,128]{2,1,0:T(8,128)(2,1)}, u32[]{:S(2)}, u32[]{:S(2)}) async-start(bf16[128,280,128]{2,1,0:T(8,128)(2,1)} %shard_map.82), calls=%async_computation | async-start | bytes 18350080 | tf_op jit(solution)/shard_map/all_to_all | solution.py:33
  31.9 3.0 collective-permute-start
  35.0 2.5 collective-permute-start.1
  37.5 111.3 %all-to-all-done.pixels_ref = bf16[128,280,128]{2,1,0:T(8,128)(2,1)} async-done(((bf16[128,280,128]{2,1,0:T(8,128)(2,1)}), bf16[128,280,128]{2,1,0:T(8,128)(2,1)}, u32[]{:S(2)}, u32[]{:S(2)}) %all-to-all-start) | async-done | bytes 9175072 | tf_op jit(solution)/shard_map/all_to_all | solution.py:33
  148.8 1.1 convert_add_fusion.1
  149.9 0.2 copy.99
  151.2 2.9 slice_reduce_fusion.5
  154.6 0.2 stack.115
  154.8 0.7 pad_convert_fusion.meta_ref
  156.2 0.9 pad_maximum_fusion.1.normal_ref
  157.1 1.0 slice_convert_fusion
  158.1 33.1 %shard_map.83 = (f32[384,1024]{1,0:T(8,128)}, f32[128,1024]{1,0:T(8,128)}) custom-call(f32[8,8192]{1,0:T(8,128)} %pad_convert_fusion.meta_ref, bf16[128,280,128]{2,1,0:T(8,128)(2,1)} %all-to-all-done.pixels_ref, bf16[768,512]{1,0:T(8,128)(2,1)} %pad_maximum_fusion.1.normal_ref), custom_call_target="tpu_custom_call" | custom-call | tf_op jit(solution)/shard_map/pallas_call | solution.py:153
  191.3 2.6 fusion.31
  203.6 0.3 add_multiply_fusion.5
  207.8 1.4 stack.122
  209.2 0.8 concatenate.541
  210.0 1.2 copy.131
  211.2 8.3 %all-to-all-start.1 = ((bf16[128,32,128]{2,1,0:T(8,128)(2,1)}), bf16[128,32,128]{2,1,0:T(8,128)(2,1)S(1)}, u32[]{:S(2)}, u32[]{:S(2)}) async-start(bf16[128,32,128]{2,1,0:T(8,128)(2,1)} %bitcast.42), calls=%async_computation.1 | async-start | bytes 2097152 | tf_op jit(solution)/shard_map/all_to_all | solution.py:33
  219.5 0.7 fusion.155
  220.3 1.3 collective-permute-start.2
  221.6 4.7 %collective-permute-start.3 = (f32[256,1]{1,0:T(8,128)}, f32[256,1]{1,0:T(8,128)}, u32[]{:S(2)}, u32[]{:S(2)}) collective-permute-start(f32[256,1]{1,0:T(8,128)} %get-tuple-element.122), channel_id=1, source_target_pairs={{0,1},{1,2},{2,3},{3,4},{4,5},{5,6},{6,7},{7,8},{8,9},{9,10},{10,1... | collective-permute-start | bytes 3080 | tf_op jit(solution)/shard_map/ppermute | solution.py:53
  226.3 1.2 fusion.112
  227.6 0.7 slice_reduce_fusion
  228.3 0.3 fusion.23
  228.6 1.4 fusion.4
  230.0 8.4 %all-to-all-done.1 = bf16[128,32,128]{2,1,0:T(8,128)(2,1)S(1)} async-done(((bf16[128,32,128]{2,1,0:T(8,128)(2,1)}), bf16[128,32,128]{2,1,0:T(8,128)(2,1)S(1)}, u32[]{:S(2)}, u32[]{:S(2)}) %all-to-all-start.1) | async-done | bytes 1048608 | tf_op jit(solution)/shard_map/all_to_all | solution.py:33
  238.4 0.4 copy.159
  238.8 0.8 fusion.128
  241.0 0.2 fusion.118
  241.6 0.7 copy-done.4
  242.3 0.3 copy-done.5
  242.6 1.2 fusion.52
  244.7 0.4 copy.107
  245.2 18.1 %all_to_all.20 = bf16[128,16,128]{2,1,0:T(8,128)(2,1)S(1)} all-to-all(bf16[128,16,128]{2,1,0:T(8,128)(2,1)S(1)} %copy.107), channel_id=1, replica_groups=mesh['row'=8,'col'=16] {'row','col'}, dimensions={0} | all-to-all | bytes 1048576 | tf_op jit(solution)/shard_map/all_to_all | solution.py:33
  263.3 0.2 copy.122
  263.5 0.2 copy.123
  265.5 0.9 pad_maximum_fusion.3.normal_ref
  266.4 33.1 %shard_map.84 = (f32[384,1024]{1,0:T(8,128)}, f32[128,1024]{1,0:T(8,128)}) custom-call(f32[8,8192]{1,0:T(8,128)} %pad_convert_fusion.meta_ref, bf16[128,280,128]{2,1,0:T(8,128)(2,1)} %all-to-all-done.pixels_ref, bf16[768,512]{1,0:T(8,128)(2,1)} %pad_maximum_fusion.3.normal_ref), custom_call_target="tpu_custom_call" | custom-call | tf_op jit(solution)/shard_map/pallas_call | solution.py:153
  299.5 2.6 fusion.33
  311.7 0.8 fusion.140
  312.4 0.7 fusion.141
  313.2 2.0 add_multiply_fusion
  318.9 1.4 stack.134
  320.3 0.8 concatenate.589
  321.2 1.2 copy.133
  322.4 4.3 %all-to-all-start.3 = ((bf16[128,32,128]{2,1,0:T(8,128)(2,1)}), bf16[128,32,128]{2,1,0:T(8,128)(2,1)S(1)}, u32[]{:S(2)}, u32[]{:S(2)}) async-start(bf16[128,32,128]{2,1,0:T(8,128)(2,1)} %bitcast.46), calls=%async_computation.3 | async-start | bytes 2097152 | tf_op jit(solution)/shard_map/all_to_all | solution.py:33
  326.7 3.1 collective-permute-start.4
  329.8 2.4 collective-permute-start.5
  332.3 0.8 fusion.147
  333.0 1.3 collective-permute-start.6
  334.3 4.8 %collective-permute-start.7 = (f32[256,1]{1,0:T(8,128)}, f32[256,1]{1,0:T(8,128)}, u32[]{:S(2)}, u32[]{:S(2)}) collective-permute-start(f32[256,1]{1,0:T(8,128)} %get-tuple-element.100), channel_id=1, source_target_pairs={{0,1},{1,2},{2,3},{3,4},{4,5},{5,6},{6,7},{7,8},{8,9},{9,10},{10,1... | collective-permute-start | bytes 3080 | tf_op jit(solution)/shard_map/ppermute | solution.py:53
  339.1 6.6 %all-to-all-done.3 = bf16[128,32,128]{2,1,0:T(8,128)(2,1)S(1)} async-done(((bf16[128,32,128]{2,1,0:T(8,128)(2,1)}), bf16[128,32,128]{2,1,0:T(8,128)(2,1)S(1)}, u32[]{:S(2)}, u32[]{:S(2)}) %all-to-all-start.3) | async-done | bytes 1048608 | tf_op jit(solution)/shard_map/all_to_all | solution.py:33
  345.7 1.0 copy-done.2
  346.8 1.6 copy.158
  348.4 0.8 fusion.130
  350.6 0.2 fusion.117
  351.2 1.9 fusion.40
  (193 shorter events, 9.2 us)
Async XLA Ops:
  3.1 0.7 copy-start.20
  3.1 0.8 copy-start.21
  3.1 0.8 copy-start.19
  3.5 1.3 copy-start.14
  3.5 1.4 copy-start.23
  3.5 1.4 copy-start.22
  20.0 128.8 %all-to-all-start = ((bf16[128,280,128]{2,1,0:T(8,128)(2,1)}), bf16[128,280,128]{2,1,0:T(8,128)(2,1)}, u32[]{:S(2)}, u32[]{:S(2)}) async-start(bf16[128,280,128]{2,1,0:T(8,128)(2,1)} %shard_map.82), calls=%async_computation | async-start | bytes 18350080 | tf_op jit(solution)/shard_map/all_to_all | solution.py:33
  31.9 209.7 %collective-permute-start = (f32[1,256]{1,0:T(1,128)S(1)}, f32[1,256]{1,0:T(1,128)S(1)}, u32[]{:S(2)}, u32[]{:S(2)}) collective-permute-start(f32[1,256]{1,0:T(1,128)S(1)} %get-tuple-element.119), channel_id=1, source_target_pairs={{16,0},{32,16},{48,32},{64,48},{80,64},{96,80},{112,96},{17,1},{33... | collective-permute-start | bytes 3080 | tf_op jit(solution)/shard_map/ppermute | solution.py:54
  35.0 206.6 %collective-permute-start.1 = (f32[1,256]{1,0:T(1,128)S(1)}, f32[1,256]{1,0:T(1,128)S(1)}, u32[]{:S(2)}, u32[]{:S(2)}) collective-permute-start(f32[1,256]{1,0:T(1,128)S(1)} %get-tuple-element.120), channel_id=1, source_target_pairs={{0,16},{16,32},{32,48},{48,64},{64,80},{80,96},{96,112},{1,17},{17... | collective-permute-start | bytes 3080 | tf_op jit(solution)/shard_map/ppermute | solution.py:53
  191.3 12.3 %copy-start.1 = (f32[384,1024]{1,0:T(8,128)S(1)}, f32[384,1024]{1,0:T(8,128)}, u32[]{:S(2)}) copy-start(f32[384,1024]{1,0:T(8,128)} %get-tuple-element.9) | copy-start | bytes 4718596
  209.2 2.0 copy-start.10
  211.2 8.3 %copy-start.3 = (f32[256,256]{1,0:T(8,128)S(1)}, f32[256,256]{1,0:T(8,128)}, u32[]{:S(2)}) copy-start(f32[256,256]{1,0:T(8,128)} %param.8) | copy-start | bytes 786436
  211.2 27.2 %all-to-all-start.1 = ((bf16[128,32,128]{2,1,0:T(8,128)(2,1)}), bf16[128,32,128]{2,1,0:T(8,128)(2,1)S(1)}, u32[]{:S(2)}, u32[]{:S(2)}) async-start(bf16[128,32,128]{2,1,0:T(8,128)(2,1)} %bitcast.42), calls=%async_computation.1 | async-start | bytes 2097152 | tf_op jit(solution)/shard_map/all_to_all | solution.py:33
  220.3 21.3 %collective-permute-start.2 = (f32[256,1]{1,0:T(8,128)}, f32[256,1]{1,0:T(8,128)S(1)}, u32[]{:S(2)}, u32[]{:S(2)}) collective-permute-start(f32[256,1]{1,0:T(8,128)} %get-tuple-element.121), channel_id=1, source_target_pairs={{1,0},{2,1},{3,2},{4,3},{5,4},{6,5},{7,6},{8,7},{9,8},{10,9},{11,1... | collective-permute-start | bytes 3080 | tf_op jit(solution)/shard_map/ppermute | solution.py:54
  221.6 20.0 %collective-permute-start.3 = (f32[256,1]{1,0:T(8,128)}, f32[256,1]{1,0:T(8,128)}, u32[]{:S(2)}, u32[]{:S(2)}) collective-permute-start(f32[256,1]{1,0:T(8,128)} %get-tuple-element.122), channel_id=1, source_target_pairs={{0,1},{1,2},{2,3},{3,4},{4,5},{5,6},{6,7},{7,8},{8,9},{9,10},{10,1... | collective-permute-start | bytes 3080 | tf_op jit(solution)/shard_map/ppermute | solution.py:53
  241.4 1.0 copy-start.4
  241.4 1.2 copy-start.5
  265.1 34.3 %copy-start.7 = (f32[128,256]{1,0:T(8,128)}, f32[128,256]{1,0:T(8,128)S(1)}, u32[]{:S(2)}) copy-start(f32[128,256]{1,0:T(8,128)S(1)} %fusion.70) | copy-start | bytes 393220
  265.2 34.3 %copy-start.8 = (f32[128,256]{1,0:T(8,128)}, f32[128,256]{1,0:T(8,128)S(1)}, u32[]{:S(2)}) copy-start(f32[128,256]{1,0:T(8,128)S(1)} %fusion.79) | copy-start | bytes 393220
  265.2 34.3 %copy-start.9 = (f32[128,256]{1,0:T(8,128)}, f32[128,256]{1,0:T(8,128)S(1)}, u32[]{:S(2)}) copy-start(f32[128,256]{1,0:T(8,128)S(1)} %fusion.78) | copy-start | bytes 393220
  299.5 13.7 %copy-start = (f32[384,1024]{1,0:T(8,128)S(1)}, f32[384,1024]{1,0:T(8,128)}, u32[]{:S(2)}) copy-start(f32[384,1024]{1,0:T(8,128)} %get-tuple-element.11) | copy-start | bytes 4718596
  315.2 2.6 copy-start.6
  315.2 2.7 copy-start.17
  315.2 2.7 copy-start.18
  315.2 2.7 copy-start.15
  315.2 2.7 copy-start.16
  315.2 2.7 copy-start.13
  315.2 2.9 copy-start.12
  318.7 1.6 copy-start.11
  322.4 23.3 %all-to-all-start.3 = ((bf16[128,32,128]{2,1,0:T(8,128)(2,1)}), bf16[128,32,128]{2,1,0:T(8,128)(2,1)S(1)}, u32[]{:S(2)}, u32[]{:S(2)}) async-start(bf16[128,32,128]{2,1,0:T(8,128)(2,1)} %bitcast.46), calls=%async_computation.3 | async-start | bytes 2097152 | tf_op jit(solution)/shard_map/all_to_all | solution.py:33
  326.7 24.5 %collective-permute-start.4 = (f32[1,256]{1,0:T(1,128)S(1)}, f32[1,256]{1,0:T(1,128)S(1)}, u32[]{:S(2)}, u32[]{:S(2)}) collective-permute-start(f32[1,256]{1,0:T(1,128)S(1)} %get-tuple-element.97), channel_id=1, source_target_pairs={{16,0},{32,16},{48,32},{64,48},{80,64},{96,80},{112,96},{17,1},{33... | collective-permute-start | bytes 3080 | tf_op jit(solution)/shard_map/ppermute | solution.py:54
  329.8 21.4 %collective-permute-start.5 = (f32[1,256]{1,0:T(1,128)S(1)}, f32[1,256]{1,0:T(1,128)S(1)}, u32[]{:S(2)}, u32[]{:S(2)}) collective-permute-start(f32[1,256]{1,0:T(1,128)S(1)} %get-tuple-element.98), channel_id=1, source_target_pairs={{0,16},{16,32},{32,48},{48,64},{64,80},{80,96},{96,112},{1,17},{17... | collective-permute-start | bytes 3080 | tf_op jit(solution)/shard_map/ppermute | solution.py:53
  333.0 18.2 %collective-permute-start.6 = (f32[256,1]{1,0:T(8,128)}, f32[256,1]{1,0:T(8,128)S(1)}, u32[]{:S(2)}, u32[]{:S(2)}) collective-permute-start(f32[256,1]{1,0:T(8,128)} %get-tuple-element.99), channel_id=1, source_target_pairs={{1,0},{2,1},{3,2},{4,3},{5,4},{6,5},{7,6},{8,7},{9,8},{10,9},{11,1... | collective-permute-start | bytes 3080 | tf_op jit(solution)/shard_map/ppermute | solution.py:54
  334.3 16.9 %collective-permute-start.7 = (f32[256,1]{1,0:T(8,128)}, f32[256,1]{1,0:T(8,128)}, u32[]{:S(2)}, u32[]{:S(2)}) collective-permute-start(f32[256,1]{1,0:T(8,128)} %get-tuple-element.100), channel_id=1, source_target_pairs={{0,1},{1,2},{2,3},{3,4},{4,5},{5,6},{6,7},{7,8},{8,9},{9,10},{10,1... | collective-permute-start | bytes 3080 | tf_op jit(solution)/shard_map/ppermute | solution.py:53
  345.7 1.0 copy-start.2

commit v2 on v1

v2 whole, which is shorter than its diff:
```python
import functools

import jax
import jax.numpy as jnp
from jax import lax
from jax.experimental import pallas as pl
from jax.experimental.pallas import tpu as pltpu
from jax.sharding import PartitionSpec as P

sharpness = 8.0
step_size = 0.01
smooth_weight = 2.0
laser_weight = 20.0

AXES = ("row", "col")
DEVICES = 128
N_COL = 16
TILE = 256
IMG = 64
SLAB = 512
LANES = 128
PIX_ROWS = IMG * SLAB // LANES
EXTRA = 24
REPLY = 32
SHOT_CAP = 4
LOG_2 = 0.6931471805599453
F32 = jnp.float32
BF16 = jnp.bfloat16


def exchange(value):
    return lax.all_to_all(value, AXES, split_axis=0, concat_axis=0, tiled=True)


def edges(value):
    out = []
    for axis, dim in (("row", 0), ("col", 1)):
        devices, length = (lax.axis_size(axis), value.shape[dim])
        up = [(i, (i + 1) % devices) for i in range(devices - 1)]
        down = [(j, i) for i, j in up]
        last = lax.slice_in_dim(value, length - 1, length, axis=dim)
        first = lax.slice_in_dim(value, 0, 1, axis=dim)
        out.append(lax.ppermute(last, axis, up))
        out.append(lax.ppermute(first, axis, down))
    return out


def own_albedo(cross, power):
    return jnp.where(power > 0.0, cross / jnp.where(power > 0.0, power, 1.0), 0.0)


PACK_ROWS = 64


def swap_matrix():
    to = lax.broadcasted_iota(jnp.int32, (256, 256), 0)
    source = lax.broadcasted_iota(jnp.int32, (256, 256), 1)
    return jnp.where((to % 16) * 16 + to // 16 == source, 1.0, 0.0).astype(BF16)


def iota_of(shape, dim):
    return lax.broadcasted_iota(jnp.int32, shape, dim)


def two_terms(value):
    head = value.astype(BF16)
    return head, (value - head.astype(F32)).astype(BF16)


def swapped(swap, pieces):
    turned = jnp.dot(swap, jnp.concatenate(pieces, axis=0), preferred_element_type=F32)
    return turned.astype(BF16).reshape(16, 16, LANES)


def around_pieces(even, odd):
    four = (pltpu.roll(odd, 1, 0), even, odd, pltpu.roll(even, DEVICES - 1, 0))
    terms = [two_terms(item) for item in four]
    return [
        terms[r][term][:, half * LANES : half * LANES + LANES]
        for term in range(2)
        for r in range(4)
        for half in range(2)
    ]


def shot_rows(shots):
    count = shots.shape[1]
    target, pixel, height = shots[0:1], shots[1:2], shots[2:3]
    head = height.astype(BF16).astype(F32)
    grid_row = jnp.floor(pixel * (1.0 / TILE))
    pair = jnp.floor(grid_row * 0.5)
    columns = jnp.concatenate(
        [
            target,
            (grid_row - 2.0 * pair) * DEVICES + pair,
            pixel - TILE * grid_row,
            head,
            height - head,
            jnp.ones_like(height),
            jnp.zeros((2, count), F32),
        ],
        axis=0,
    ).T
    alike = columns[:, 0:1] == target
    before = iota_of((count, count), 0) < iota_of((count, count), 1)
    rank = jnp.sum(jnp.where(jnp.logical_and(alike, before), 1.0, 0.0), axis=0, keepdims=True)
    lane = iota_of((count, LANES), 1)
    record = jnp.zeros((count, LANES), F32)
    for member in range(5):
        record = jnp.where(lane % 5 == member, columns[:, member + 1 : member + 2], record)
    owned = iota_of((DEVICES, count), 0).astype(F32) == target
    rows = jnp.zeros((DEVICES, LANES), F32)
    for slot in range(SHOT_CAP):
        chosen = jnp.where(jnp.logical_and(owned, rank == slot), 1.0, 0.0).astype(BF16)
        held = jnp.where(lane // 5 == slot, record, 0.0).astype(BF16)
        rows = rows + jnp.dot(chosen, held, preferred_element_type=F32)
    return rows.astype(BF16)


def pack_kernel(images_ref, heights_ref, shadow_ref, table_ref, shots_ref, out_ref, split_ref, extra_ref, halves_ref):
    step = pl.program_id(0)
    swap = swap_matrix()

    @pl.when(step == 0)
    def start():
        tiles = []
        for source, kind in ((heights_ref, 0), (shadow_ref, 1)):
            parts = []
            for half in range(2):
                lanes = slice(half * LANES, half * LANES + LANES)
                block = source[:, lanes]
                halves_ref[kind * 2 + half] = block if kind == 0 else 1.0 - block.astype(F32)
            for side in range(2):
                parts.append(
                    jnp.concatenate(
                        [halves_ref[kind * 2 + half, pl.ds(side, DEVICES, 2), :] for half in range(2)],
                        axis=1,
                    )
                )
            tiles.append(parts)
        (even, odd), (lit_even, lit_odd) = tiles
        split_ref[:DEVICES] = even
        split_ref[DEVICES:] = odd
        first = around_pieces(even, odd)
        lit = jnp.concatenate([lit_even, lit_odd], axis=1).astype(BF16)
        table = table_ref[...].astype(BF16)
        second = [lit[:, j * LANES : j * LANES + LANES] for j in range(4)]
        second += [jnp.broadcast_to(table[j : j + 1], (DEVICES, LANES)) for j in range(3)]
        second += [shot_rows(shots_ref[...])] + [jnp.zeros((DEVICES, LANES), BF16)] * 8
        for group in range(DEVICES // 16):
            span = slice(group * 16, group * 16 + 16)
            extra_ref[span, 0:16] = swapped(swap, [item[span] for item in first])
            extra_ref[span, 16:32] = swapped(swap, [item[span] for item in second])

    for band in range(PACK_ROWS // 16):
        for group in range(IMG // 16):
            block = images_ref[group * 16 : group * 16 + 16, band * 16 : band * 16 + 16]
            turned = jnp.dot(
                swap, block.reshape(256, TILE), preferred_element_type=F32
            ).astype(BF16)
            for r in range(16):
                for half in range(TILE // LANES):
                    place = ((r % 2) * 2 + half) * IMG + group * 16
                    out_ref[band * 8 + r // 2, place : place + 16, :] = turned[
                        r * 16 : r * 16 + 16, half * LANES : half * LANES + LANES
                    ]
    per_step = PACK_ROWS // 2
    here = pl.ds(pl.multiple_of(step * per_step, per_step), per_step)
    out_ref[:, PIX_ROWS : PIX_ROWS + EXTRA, :] = extra_ref[here, 0:EXTRA, :]


def pack(images, heights, shadow, table, shots):
    per_step = PACK_ROWS // 2
    whole = lambda s: (0, 0)
    return pl.pallas_call(
        pack_kernel,
        grid=(DEVICES // per_step,),
        in_specs=[
            pl.BlockSpec((IMG, PACK_ROWS, TILE), lambda s: (0, s, 0)),
            pl.BlockSpec((TILE, TILE), whole),
            pl.BlockSpec((TILE, TILE), whole),
            pl.BlockSpec((8, LANES), whole),
            pl.BlockSpec((8, TILE), whole),
        ],
        out_specs=[
            pl.BlockSpec((per_step, PIX_ROWS + EXTRA, LANES), lambda s: (s, 0, 0)),
            pl.BlockSpec((TILE, TILE), whole),
        ],
        out_shape=[
            jax.ShapeDtypeStruct((DEVICES, PIX_ROWS + EXTRA, LANES), BF16),
            jax.ShapeDtypeStruct((TILE, TILE), F32),
        ],
        scratch_shapes=[
            pltpu.VMEM((DEVICES, 32, LANES), BF16),
            pltpu.VMEM((4, TILE, LANES), F32),
        ],
        compiler_params=pltpu.CompilerParams(vmem_limit_bytes=48 * 1024 * 1024),
    )(images, heights, shadow, table, shots)


SUM_SRC = 16
SUM_IMG = SUM_SRC * IMG
HALF_SRC = SUM_SRC // 2
HALF_IMG = SUM_IMG // 2
CHUNKS = 4
WIDTH = 2 * SLAB + TILE


def sideways(value):
    lane = iota_of(value.shape, 1)
    column = iota_of(value.shape, 0) % N_COL
    before = pltpu.roll(value, 1, 1)
    first = jnp.where(column == 0, 0.0, pltpu.roll(before, 1, 0))
    after = pltpu.roll(value, TILE - 1, 1)
    last = jnp.where(column == N_COL - 1, 0.0, pltpu.roll(after, DEVICES - 1, 0))
    return jnp.where(lane == 0, first, before), jnp.where(lane == TILE - 1, last, after)


def central_x(value):
    before, after = sideways(value)
    return after - before


def shift_tiles(value, count):
    pad = jnp.zeros((abs(count),) + value.shape[1:], value.dtype)
    if count > 0:
        return jnp.concatenate([pad, value[:-count]], axis=0)
    return jnp.concatenate([value[-count:], pad], axis=0)


def slab_normals(me, around_ref, lit_ref, normal_ref, slopes_ref, rows_ref):
    swap = swap_matrix()
    for group in range(DEVICES // 16):
        span = slice(group * 16, group * 16 + 16)
        turned = jnp.dot(
            swap, around_ref[span].reshape(256, LANES), preferred_element_type=F32
        )
        fine = turned[:128] + turned[128:]
        for r in range(4):
            for half in range(2):
                at = (2 * r + half) * 16
                rows_ref[r, span, half * LANES : half * LANES + LANES] = fine[at : at + 16]
    rows = [rows_ref[r] for r in range(4)]
    top = jnp.where(me == 0, shift_tiles(rows[0], N_COL), rows[0])
    bottom = jnp.where(me == DEVICES - 1, shift_tiles(rows[3], -N_COL), rows[3])
    slope_x = jnp.concatenate([central_x(rows[1]), central_x(rows[2])], axis=1) * 0.5
    slope_y = jnp.concatenate([rows[2] - top, bottom - rows[1]], axis=1) * 0.5
    inverse = lax.rsqrt(1.0 + slope_x * slope_x + slope_y * slope_y)
    slopes_ref[0], slopes_ref[1], slopes_ref[2] = slope_x, slope_y, inverse
    scale = 0.5 * sharpness
    x_head, x_tail = two_terms(-slope_x * inverse * scale)
    y_head, y_tail = two_terms(-slope_y * inverse * scale)
    steep = ((inverse - 1.0) * scale).astype(BF16)
    flat = jnp.where(lit_ref[...] > 0.5, scale, -2048.0).astype(BF16)
    for place, item in enumerate((x_head, y_head, x_tail, y_tail, steep, flat)):
        normal_ref[place * DEVICES : (place + 1) * DEVICES] = item


def slab_reply(me, lit_ref, slopes_ref, sums_ref, plain_ref, reply_ref):
    lit = lit_ref[...]
    slope_x, slope_y, inverse = slopes_ref[0], slopes_ref[1], slopes_ref[2]
    cube = inverse * inverse * inverse
    lane = iota_of((16, LANES), 1)
    scalars = jnp.zeros((16, LANES), BF16)
    totals = []
    for part in range(2):
        value = jnp.sum(plain_ref[:, part * SLAB : (part + 1) * SLAB], keepdims=True)
        total = jnp.zeros((1, 1), F32)
        for term in range(3):
            head = value.astype(BF16).astype(F32)
            scalars = jnp.where(lane == part * 3 + term, head, scalars.astype(F32)).astype(BF16)
            value = value - head
            total = total + head
        totals.append(total)
    guess = own_albedo(totals[0], totals[1])
    fields = []
    for part in range(2):
        by_x, by_y, by_z = (
            sums_ref[j * DEVICES : (j + 1) * DEVICES, part * SLAB : (part + 1) * SLAB]
            for j in range(3)
        )
        turned = (by_z - slope_x * by_x - slope_y * by_y) * cube
        grad_x = -lit * (by_x * inverse + slope_x * turned)
        grad_y = -lit * (by_y * inverse + slope_y * turned)
        across = jnp.concatenate([central_x(grad_x[:, :TILE]), central_x(grad_x[:, TILE:])], axis=1)
        halo = jnp.where(
            me == 0, shift_tiles(grad_y[:, :TILE], -N_COL), shift_tiles(grad_y[:, TILE:], N_COL)
        )
        fields.append(jnp.concatenate([across * (-0.5), grad_y, halo], axis=1))
    seen, model = fields
    head, tail = two_terms(guess * model - seen)
    flat = jnp.concatenate([model.astype(BF16), head, tail], axis=1)
    swap = swap_matrix()
    for group in range(DEVICES // 16):
        span = slice(group * 16, group * 16 + 16)
        pieces = [flat[span, j * LANES : (j + 1) * LANES] for j in range(30)]
        pieces = pieces + [scalars, jnp.zeros((16, LANES), BF16)]
        for part in range(2):
            block = jnp.concatenate(pieces[part * 16 : part * 16 + 16], axis=0)
            turned = jnp.dot(swap, block, preferred_element_type=F32).astype(BF16)
            reply_ref[span, part * 16 : part * 16 + 16, :] = turned.reshape(16, 16, LANES)


def sum_kernel(
    me_ref, meta_ref, pixels_ref, around_ref, lit_ref, reply_ref,
    normal_ref, slopes_ref, rows_ref, sums_ref, plain_ref, first_w, second_w, first_p, second_p,
):
    step = pl.program_id(0)
    me = me_ref[0]

    @pl.when(step == 0)
    def start():
        sums_ref[...] = jnp.zeros_like(sums_ref)
        plain_ref[...] = jnp.zeros_like(plain_ref)
        second_w[...] = jnp.zeros_like(second_w)
        second_p[...] = jnp.zeros_like(second_p)
        slab_normals(me, around_ref, lit_ref, normal_ref, slopes_ref, rows_ref)

    def front(side, w_ref, p_ref):
        meta = meta_ref[:, side * HALF_IMG : (side + 1) * HALF_IMG]
        cols = meta.T
        hot = iota_of((HALF_IMG, DEVICES), 1).astype(F32) == cols[:, 0:1]
        sun = [jnp.where(hot, cols[:, j : j + 1], 0.0).astype(BF16) for j in (1, 2, 3)]
        pick = jnp.concatenate([sun[0], sun[1], sun[0], sun[1], sun[2], sun[2]], axis=1)
        hot_t = iota_of((DEVICES, HALF_IMG), 0).astype(F32) == meta[0:1, :]
        for j in range(3):
            p_ref[j * DEVICES : (j + 1) * DEVICES] = jnp.where(
                hot_t, meta[j + 1 : j + 2, :], 0.0
            ).astype(BF16)
        count, images = (HALF_SRC // CHUNKS, HALF_IMG // CHUNKS)
        for chunk in range(CHUNKS):
            span = slice(chunk * images, (chunk + 1) * images)
            src = slice(side * HALF_SRC + chunk * count, side * HALF_SRC + (chunk + 1) * count)
            half_angle = jnp.dot(pick[span], normal_ref[...], preferred_element_type=F32)
            gain = cols[span, 4:5]
            bend = jnp.tanh(half_angle)
            refl = (jnp.log(1.0 - bend) - LOG_2) * (gain * (-1.0 / sharpness))
            sigma = bend * (gain * 0.5) + gain * 0.5
            seen = jnp.concatenate(
                [
                    pixels_ref[src, q * IMG : q * IMG + IMG, :].reshape(images, LANES)
                    for q in range(SLAB // LANES)
                ],
                axis=1,
            ).astype(F32)
            w_ref[span, :SLAB] = (seen * sigma).astype(BF16)
            w_ref[span, SLAB:] = (refl * sigma).astype(BF16)
            plain_ref[:, :SLAB] += jnp.sum((seen * refl).reshape(-1, 8, SLAB), axis=0)
            plain_ref[:, SLAB:] += jnp.sum((refl * refl).reshape(-1, 8, SLAB), axis=0)

    def back(w_ref, p_ref):
        sums_ref[...] += jnp.dot(p_ref[...], w_ref[...], preferred_element_type=F32)

    back(second_w, second_p)
    front(0, first_w, first_p)
    back(first_w, first_p)
    front(1, second_w, second_p)

    @pl.when(step == pl.num_programs(0) - 1)
    def finish():
        back(second_w, second_p)
        slab_reply(me, lit_ref, slopes_ref, sums_ref, plain_ref, reply_ref)


def slab_pass(me, meta, pixels, around, lit):
    return pl.pallas_call(
        sum_kernel,
        grid=(DEVICES // SUM_SRC,),
        in_specs=[
            pl.BlockSpec(memory_space=pltpu.SMEM),
            pl.BlockSpec((8, SUM_IMG), lambda s: (0, s)),
            pl.BlockSpec((SUM_SRC, PIX_ROWS + EXTRA, LANES), lambda s: (s, 0, 0)),
            pl.BlockSpec((DEVICES, 16, LANES), lambda s: (0, 0, 0)),
            pl.BlockSpec((DEVICES, SLAB), lambda s: (0, 0)),
        ],
        out_specs=pl.BlockSpec((DEVICES, REPLY, LANES), lambda s: (0, 0, 0)),
        out_shape=jax.ShapeDtypeStruct((DEVICES, REPLY, LANES), BF16),
        scratch_shapes=[
            pltpu.VMEM((6 * DEVICES, SLAB), BF16),
            pltpu.VMEM((3, DEVICES, SLAB), F32),
            pltpu.VMEM((4, DEVICES, TILE), F32),
            pltpu.VMEM((3 * DEVICES, 2 * SLAB), F32),
            pltpu.VMEM((8, 2 * SLAB), F32),
            pltpu.VMEM((HALF_IMG, 2 * SLAB), BF16),
            pltpu.VMEM((HALF_IMG, 2 * SLAB), BF16),
            pltpu.VMEM((3 * DEVICES, HALF_IMG), BF16),
            pltpu.VMEM((3 * DEVICES, HALF_IMG), BF16),
        ],
        compiler_params=pltpu.CompilerParams(vmem_limit_bytes=48 * 1024 * 1024),
    )(me, meta, pixels, around, lit)


def owner_kernel(final, *refs):
    got_ref, surface_ref, hits_ref, height_ref, ends_ref, sides_ref = refs[:6]
    outs, (model_ref, misfit_ref, scalar_ref, mixed_ref) = refs[6:-4], refs[-4:]
    swap = swap_matrix()
    for group in range(DEVICES // 16):
        span = slice(group * 16, group * 16 + 16)
        rows = []
        for part in range(2):
            block = got_ref[span, part * 16 : part * 16 + 16, :].reshape(256, LANES)
            turned = jnp.dot(swap, block, preferred_element_type=F32)
            rows += [turned[j * 16 : j * 16 + 16] for j in range(16)]
        for j in range(10):
            model_ref[j, span] = rows[j]
            misfit_ref[j, span] = rows[10 + j] + rows[20 + j]
        scalar_ref[span] = rows[30]
    scalars = scalar_ref[...]
    cross = scalars[:, 0:1] + scalars[:, 1:2] + scalars[:, 2:3]
    power = scalars[:, 3:4] + scalars[:, 4:5] + scalars[:, 5:6]
    albedo = jnp.sum(cross, keepdims=True) / jnp.sum(power, keepdims=True)
    rest = albedo * (albedo - own_albedo(cross, power))

    def grad(j):
        return jnp.concatenate(
            [albedo * misfit_ref[i] + rest * model_ref[i] for i in (j, j + 1)], axis=1
        )

    row = iota_of((DEVICES, TILE), 0)
    lane = iota_of((DEVICES, TILE), 1)
    along_even, along_odd, halo = grad(4), grad(6), grad(8)
    before = jnp.where(row == 0, pltpu.roll(halo, 1, 0), pltpu.roll(along_odd, 1, 0))
    after = jnp.where(
        row == DEVICES - 1,
        pltpu.roll(halo, DEVICES - 1, 0),
        pltpu.roll(along_even, DEVICES - 1, 0),
    )
    data = (grad(0) + (before - along_odd) * 0.5, grad(2) + (along_even - after) * 0.5)
    old = (surface_ref[:DEVICES], surface_ref[DEVICES:])
    above = jnp.where(row == 0, ends_ref[0:1], pltpu.roll(old[1], 1, 0))
    below = jnp.where(row == DEVICES - 1, ends_ref[1:2], pltpu.roll(old[0], DEVICES - 1, 0))
    vertical = (above + old[1], old[0] + below)
    new = []
    for part in range(2):
        span = slice(part * DEVICES, (part + 1) * DEVICES)
        left = jnp.where(lane == 0, sides_ref[span, 0:1], pltpu.roll(old[part], 1, 1))
        right = jnp.where(
            lane == TILE - 1, sides_ref[span, 1:2], pltpu.roll(old[part], TILE - 1, 1)
        )
        laplace = vertical[part] + left + right - 4.0 * old[part]
        laser = hits_ref[span] * old[part] - height_ref[span]
        new.append(
            old[part]
            - step_size * (data[part] - smooth_weight * laplace + laser_weight * laser)
        )
    if final:
        for part in range(2):
            for half in range(2):
                lanes = slice(half * LANES, half * LANES + LANES)
                mixed_ref[pl.ds(half * TILE + part, DEVICES, 2), :] = new[part][:, lanes]
        for half in range(2):
            outs[0][:, half * LANES : half * LANES + LANES] = mixed_ref[
                half * TILE : half * TILE + TILE
            ]
        return
    outs[0][:DEVICES], outs[0][DEVICES:] = new[0], new[1]
    pieces = around_pieces(new[0], new[1])
    for group in range(DEVICES // 16):
        span = slice(group * 16, group * 16 + 16)
        outs[1][span] = swapped(swap, [item[span] for item in pieces])


def owner_update(final, got, surface, hits, height_sum, rims):
    above, below, left, right = rims
    ends = jnp.concatenate([above, below], axis=0)
    sides = jnp.concatenate([left, right], axis=1)
    out_shape = [jax.ShapeDtypeStruct((TILE, TILE), F32)]
    if not final:
        out_shape.append(jax.ShapeDtypeStruct((DEVICES, 16, LANES), BF16))
    return pl.pallas_call(
        functools.partial(owner_kernel, final),
        out_shape=out_shape,
        scratch_shapes=[
            pltpu.VMEM((10, DEVICES, LANES), F32),
            pltpu.VMEM((10, DEVICES, LANES), F32),
            pltpu.VMEM((DEVICES, LANES), F32),
            pltpu.VMEM((2 * TILE, LANES), F32),
        ],
        compiler_params=pltpu.CompilerParams(vmem_limit_bytes=32 * 1024 * 1024),
    )(got, surface, hits, height_sum, ends, sides)


def shot_sums(slots):
    cell = lax.broadcasted_iota(jnp.int32, (1, TILE), 1).astype(F32)
    present = slots[:, 4:5]
    in_row = jnp.where(slots[:, 0:1] == cell, 1.0, 0.0)
    in_col = jnp.where(slots[:, 1:2] == cell, 1.0, 0.0).astype(BF16)
    left = jnp.concatenate([in_row * slots[:, j : j + 1] * present for j in (4, 2, 3)], axis=1)
    both = lax.dot_general(
        left.astype(BF16), in_col, (((0,), (0,)), ((), ())), preferred_element_type=F32
    )
    return both[:TILE], both[TILE : 2 * TILE] + both[2 * TILE :]


def body(heights, shadow, image_tiles, image_dest, sun_gain, shot_dest, shot_pixel, shot_height):
    me = (lax.axis_index("row") * N_COL + lax.axis_index("col")).astype(jnp.int32)[None]
    dest = image_dest[:, 0].astype(F32)
    table = jnp.concatenate([dest, jnp.zeros_like(dest), sun_gain.astype(F32).T.reshape(-1)])
    table = jnp.pad(table.reshape(3, LANES), ((0, 5), (0, 0)))
    shots = jnp.stack([shot_dest[:, 0].astype(F32), shot_pixel.astype(F32), shot_height])
    shots = jnp.pad(shots, ((0, 5), (0, 0)))
    packed, surface = pack(image_tiles, heights, shadow, table, shots)
    rims = edges(surface)
    pixels = exchange(packed)
    extra = pixels[:, PIX_ROWS:, :]
    meta = jnp.stack(
        [
            extra[:, 20, :IMG],
            extra[:, 21, :IMG],
            extra[:, 21, IMG:],
            extra[:, 22, :IMG],
            extra[:, 22, IMG:],
        ]
    ).astype(F32)
    meta = jnp.pad(meta.reshape(5, DEVICES * IMG), ((0, 3), (0, 0)))
    slab_lit = extra[:, 16:20, :].reshape(DEVICES, SLAB).astype(F32)
    around = extra[:, 0:16, :]
    slots = extra[:, 23, : SHOT_CAP * 5].reshape(DEVICES * SHOT_CAP, 5).astype(F32)
    hits, height_sum = shot_sums(slots)
    reply = slab_pass(me, meta, pixels, around, slab_lit)
    got = exchange(reply)
    surface, around = owner_update(False, got, surface, hits, height_sum, rims)
    around = exchange(around)
    rims = edges(surface)
    got = exchange(slab_pass(me, meta, pixels, around, slab_lit))
    return owner_update(True, got, surface, hits, height_sum, rims)[0]


def solution(mesh):
    placed = (
        P("row", "col"),
        P("row", "col"),
        P(("row", "col"), None, None),
        P(("row", "col"), None),
        P(("row", "col"), None),
        P(("row", "col"), None),
        P(("row", "col")),
        P(("row", "col")),
    )
    return jax.shard_map(
        body, mesh=mesh, in_specs=placed, out_specs=P("row", "col"), check_vma=False
    )
```

time: 355 us -> 275 us (0.77)
  between operations: 28.4 us -> 0.27 us
  local copies, waits for them, and re-layouts: 26.6 us -> 7.8 us
  other arithmetic: 24 us -> 6.25 us
  Pallas kernels: 80.4 us -> 64.9 us
  waiting for transfers between devices: 126 us -> 131 us
    all_to_all x3, waiting for transfers between devices: 126 us -> 49.7 us  [exchange(): return lax.all_to_all(value, AXES, split_axis=0, concat_axis=0, tiled=True)]
    ppermute x4, waiting for transfers between devices: 0.01 us -> 75.3 us  [edges(): out.append(lax.ppermute(last, axis, up))]
    pallas_call x2 -> x4, Pallas kernels: 66.2 us -> 55.2 us  [the longest x2 51.4 us: slab_pass(): pl.pallas_call(sum_kernel, grid=(DEVICES // SUM_SRC,), in_specs=[pl.Block...]
    reduce_sum x5 -> x0, other arithmetic: 7.04 us -> none  [the longest x2 5.21 us: slab_pass(): cross = pieces_of(jnp.sum(lit * plain[:, :SLAB]), 3)]
    unnamed x66 -> x5, local copies, waits for them, and re-layouts: 8.1 us -> 1.92 us
    ppermute x4, waiting for transfers between devices: 0.01 us -> 5.81 us  [edges(): out.append(lax.ppermute(first, axis, down))]
    slice x37 -> x5, local copies, waits for them, and re-layouts: 6.68 us -> 1.29 us  [the longest x1 1.1 us: body(): around = extra[:, 0:16, :]]
    sub x18 -> x0, other arithmetic: 4.98 us -> none  [the longest x2 3.08 us: body(): surface - step_size * (data - smooth_weight * laplace + laser_weight * (h...]
  transfers between devices with their start and end apart: 11 -> 11, of which waited for: 3 -> 7; matrix products, arithmetic and copies ran while one was open for 8% -> 3% of each run, Pallas kernels for 9% -> 9%
where the time goes in v2:
time: 275 us; the launch traced here: 274 us
  waiting for transfers between devices  131 us (48%)
  Pallas kernels  64.9 us (24%)
  starting transfers between devices  45.5 us (17%)
  blocking collectives  18 us (7%)
  local copies, waits for them, and re-layouts  7.8 us (3%)
  other arithmetic  6.25 us (2%)
    ppermute x4, waiting for transfers between devices, edges(): out.append(lax.ppermute(last, axis, up))  75.3 us
    pallas_call x2, Pallas kernels, slab_pass(): pl.pallas_call(sum_kernel, grid=(DEVICES // SUM_SRC,), in_specs=[pl.Block...  51.4 us
    all_to_all x3, waiting for transfers between devices, exchange(): return lax.all_to_all(value, AXES, split_axis=0, concat_axis=0, tiled=True)  49.7 us
    all_to_all x3, starting transfers between devices, exchange(): return lax.all_to_all(value, AXES, split_axis=0, concat_axis=0, tiled=True)  25.1 us
    all_to_all x1, blocking collectives, exchange(): return lax.all_to_all(value, AXES, split_axis=0, concat_axis=0, tiled=True)  18 us
    ppermute x4, starting transfers between devices, edges(): out.append(lax.ppermute(last, axis, up))  14 us
    pallas_call x1, Pallas kernels, pack(): pl.pallas_call(pack_kernel, grid=(DEVICES // per_step,), in_specs=[pl.Blo...  9.76 us
    ppermute x4, starting transfers between devices, edges(): out.append(lax.ppermute(first, axis, down))  6.43 us
  transfers between devices with their start and end apart: 11, of which 7 were waited for; matrix products, arithmetic and copies ran while one was open for 3% of the time, Pallas kernels for 9%

profile of v2, /device:TPU:1, one launch (start us, length us, event | category | flops | bytes accessed | tf_op | source)
XLA Modules:
  0.0 274.0 jit_solution(3809200470298672334)
XLA Ops:
  0.0 0.7 convert_bitcast_fusion
  0.7 0.1 reshape.46
  0.8 0.7 convert_bitcast_fusion.2
  1.4 0.1 maximum_bitcast_fusion
  1.5 0.7 convert_element_type.60
  2.2 0.7 convert_bitcast_fusion.1
  2.9 0.7 select_maximum_fusion.shots_ref
  3.6 0.0 copy-start
  3.6 0.9 copy-done
  4.5 0.0 copy-start.1
  4.5 0.9 copy-done.1
  5.5 9.8 %shard_map.82 = (bf16[128,280,128]{2,1,0:T(8,128)(2,1)}, f32[256,256]{1,0:T(8,128)S(1)}) custom-call(bf16[64,256,256]{2,1,0:T(8,128)(2,1)} %images_ref.1, f32[256,256]{1,0:T(8,128)S(1)} %copy-done, s32[256,256]{1,0:T(8,128)S(1)} %copy-done.1, f32[8,128]{1,0:T(8,128)S(1)} %pad.14.table_ref, f32[8,256]{1,0:T(8,128)S(1)} %select_maximum_fusion.shots_ref), custom_call_target="tpu_custom_call" | custom-call | tf_op jit(solution)/shard_map/pallas_call | solution.py:175
  15.2 11.9 %all-to-all-start = ((bf16[128,280,128]{2,1,0:T(8,128)(2,1)}), bf16[128,280,128]{2,1,0:T(8,128)(2,1)}, u32[]{:S(2)}, u32[]{:S(2)}) async-start(bf16[128,280,128]{2,1,0:T(8,128)(2,1)} %get-tuple-element.9), calls=%async_computation | async-start | bytes 18350080 | tf_op jit(solution)/shard_map/all_to_all | solution.py:32
  27.1 0.1 fusion.22
  27.2 3.4 %collective-permute-start.2 = (f32[256,1]{1,0:T(8,128)S(1)}, f32[256,1]{1,0:T(8,128)S(1)}, u32[]{:S(2)}, u32[]{:S(2)}) collective-permute-start(f32[256,1]{1,0:T(8,128)S(1)} %get-tuple-element.29), channel_id=1, source_target_pairs={{0,1},{1,2},{2,3},{3,4},{4,5},{5,6},{6,7},{7,8},{8,9},{9,10},{10,1... | collective-permute-start | bytes 3080 | tf_op jit(solution)/shard_map/ppermute | solution.py:43
  30.7 1.3 collective-permute-start.3
  32.0 3.6 %collective-permute-start = (f32[1,256]{1,0:T(1,128)S(1)}, f32[1,256]{1,0:T(1,128)S(1)}, u32[]{:S(2)}, u32[]{:S(2)}) collective-permute-start(f32[1,256]{1,0:T(1,128)S(1)} %get-tuple-element.31), channel_id=1, source_target_pairs={{0,16},{16,32},{32,48},{48,64},{64,80},{80,96},{96,112},{1,17},{17... | collective-permute-start | bytes 3080 | tf_op jit(solution)/shard_map/ppermute | solution.py:43
  35.6 1.9 collective-permute-start.1
  37.6 73.0 %collective-permute-done.2 = f32[256,1]{1,0:T(8,128)S(1)} collective-permute-done((f32[256,1]{1,0:T(8,128)S(1)}, f32[256,1]{1,0:T(8,128)S(1)}, u32[]{:S(2)}, u32[]{:S(2)}) %collective-permute-start.2) | collective-permute-done | bytes 1056 | tf_op jit(solution)/shard_map/ppermute | solution.py:43
  110.5 0.0 collective-permute-done.3
  110.5 0.1 pad_maximum_fusion.refs_5_
  110.7 33.1 %all-to-all-done.pixels_ref = bf16[128,280,128]{2,1,0:T(8,128)(2,1)} async-done(((bf16[128,280,128]{2,1,0:T(8,128)(2,1)}), bf16[128,280,128]{2,1,0:T(8,128)(2,1)}, u32[]{:S(2)}, u32[]{:S(2)}) %all-to-all-start) | async-done | bytes 9175072 | tf_op jit(solution)/shard_map/all_to_all | solution.py:32
  143.8 3.0 %slice_reduce_fusion.5 = (bf16[128,64]{1,0:T(8,128)(2,1)S(1)}, bf16[128,64]{1,0:T(8,128)(2,1)S(1)}, bf16[128,64]{1,0:T(8,128)(2,1)S(1)}, bf16[128,64]{1,0:T(8,128)(2,1)S(1)}, bf16[128,64]{1,0:T(8,128)(2,1)S(1)}) fusion(bf16[128,280,128]{2,1,0:T(8,128)(2,1)} %all-to-all-done.pixels_ref), kind=kLoop, calls=%fused_computation.33 | loop fusion | bytes 163840 | tf_op jit(solution)/shard_map/slice | solution.py:512
  146.8 0.1 stack.26
  146.9 0.1 stack.27
  147.0 0.1 stack.28
  147.0 0.1 stack.29
  147.1 0.1 stack.30
  147.2 0.2 stack.31
  147.5 1.0 slice_convert_fusion
  148.5 1.1 slice.111.around_ref
  149.6 25.7 %shard_map.83 = bf16[128,32,128]{2,1,0:T(8,128)(2,1)} custom-call(s32[1]{0:T(128)} %bitcast.me_ref, f32[8,8192]{1,0:T(8,128)S(1)} %pad_convert_fusion.meta_ref, bf16[128,280,128]{2,1,0:T(8,128)(2,1)} %all-to-all-done.pixels_ref, bf16[128,16,128]{2,1,0:T(8,128)(2,1)S(1)} %slice.111.around_ref, f32[128,512]{1,0:T(8,128)S(1)} %bitcast.15), custom_call_target="tpu_custom_call" | custom-call | tf_op jit(solution)/shard_map/pallas_call | solution.py:366
  175.3 9.0 %all-to-all-start.1 = ((bf16[128,32,128]{2,1,0:T(8,128)(2,1)}), bf16[128,32,128]{2,1,0:T(8,128)(2,1)S(1)}, u32[]{:S(2)}, u32[]{:S(2)}) async-start(bf16[128,32,128]{2,1,0:T(8,128)(2,1)} %shard_map.83), calls=%async_computation.1 | async-start | bytes 2097152 | tf_op jit(solution)/shard_map/all_to_all | solution.py:32
  184.3 0.0 collective-permute-done
  184.3 0.0 collective-permute-done.1
  184.3 1.2 fusion.16
  185.5 0.1 reshape.48
  185.6 0.7 slice_reduce_fusion
  186.4 0.3 fusion.7
  186.7 0.5 fusion
  187.2 0.1 slice_add_fusion
  187.3 15.9 %all-to-all-done.1.refs_0_ = bf16[128,32,128]{2,1,0:T(8,128)(2,1)S(1)} async-done(((bf16[128,32,128]{2,1,0:T(8,128)(2,1)}), bf16[128,32,128]{2,1,0:T(8,128)(2,1)S(1)}, u32[]{:S(2)}, u32[]{:S(2)}) %all-to-all-start.1) | async-done | bytes 1048608 | tf_op jit(solution)/shard_map/all_to_all | solution.py:32
  203.2 1.8 shard_map.84
  205.0 18.0 %all_to_all.20.around_ref = bf16[128,16,128]{2,1,0:T(8,128)(2,1)S(1)} all-to-all(bf16[128,16,128]{2,1,0:T(8,128)(2,1)S(1)} %get-tuple-element.11), channel_id=1, replica_groups=mesh['row'=8,'col'=16] {'row','col'}, dimensions={0} | all-to-all | bytes 1048576 | tf_op jit(solution)/shard_map/all_to_all | solution.py:32
  223.0 25.7 %shard_map.85 = bf16[128,32,128]{2,1,0:T(8,128)(2,1)} custom-call(s32[1]{0:T(128)} %bitcast.me_ref, f32[8,8192]{1,0:T(8,128)S(1)} %pad_convert_fusion.meta_ref, bf16[128,280,128]{2,1,0:T(8,128)(2,1)} %all-to-all-done.pixels_ref, bf16[128,16,128]{2,1,0:T(8,128)(2,1)S(1)} %all_to_all.20.around_ref, f32[128,512]{1,0:T(8,128)S(1)} %bitcast.16), custom_call_target="tpu_custom_call" | custom-call | tf_op jit(solution)/shard_map/pallas_call | solution.py:366
  248.7 4.2 %all-to-all-start.3 = ((bf16[128,32,128]{2,1,0:T(8,128)(2,1)}), bf16[128,32,128]{2,1,0:T(8,128)(2,1)S(1)}, u32[]{:S(2)}, u32[]{:S(2)}) async-start(bf16[128,32,128]{2,1,0:T(8,128)(2,1)} %shard_map.85), calls=%async_computation.3 | async-start | bytes 2097152 | tf_op jit(solution)/shard_map/all_to_all | solution.py:32
  253.0 3.5 %collective-permute-start.4 = (f32[1,256]{1,0:T(1,128)S(1)}, f32[1,256]{1,0:T(1,128)S(1)}, u32[]{:S(2)}, u32[]{:S(2)}) collective-permute-start(f32[1,256]{1,0:T(1,128)S(1)} %get-tuple-element.27), channel_id=1, source_target_pairs={{0,16},{16,32},{32,48},{48,64},{64,80},{80,96},{96,112},{1,17},{17... | collective-permute-start | bytes 3080 | tf_op jit(solution)/shard_map/ppermute | solution.py:43
  256.5 1.9 collective-permute-start.5
  258.5 0.1 fusion.20
  258.6 3.4 %collective-permute-start.6 = (f32[256,1]{1,0:T(8,128)S(1)}, f32[256,1]{1,0:T(8,128)S(1)}, u32[]{:S(2)}, u32[]{:S(2)}) collective-permute-start(f32[256,1]{1,0:T(8,128)S(1)} %get-tuple-element.25), channel_id=1, source_target_pairs={{0,1},{1,2},{2,3},{3,4},{4,5},{5,6},{6,7},{7,8},{8,9},{9,10},{10,1... | collective-permute-start | bytes 3080 | tf_op jit(solution)/shard_map/ppermute | solution.py:43
  261.9 1.3 collective-permute-start.7
  263.2 0.0 collective-permute-done.4
  263.2 2.9 %collective-permute-done.5 = f32[1,256]{1,0:T(1,128)S(1)} collective-permute-done((f32[1,256]{1,0:T(1,128)S(1)}, f32[1,256]{1,0:T(1,128)S(1)}, u32[]{:S(2)}, u32[]{:S(2)}) %collective-permute-start.5) | collective-permute-done | bytes 1056 | tf_op jit(solution)/shard_map/ppermute | solution.py:44
  266.2 2.3 collective-permute-done.6
  268.5 2.9 %collective-permute-done.7 = f32[256,1]{1,0:T(8,128)S(1)} collective-permute-done((f32[256,1]{1,0:T(8,128)S(1)}, f32[256,1]{1,0:T(8,128)S(1)}, u32[]{:S(2)}, u32[]{:S(2)}) %collective-permute-start.7) | collective-permute-done | bytes 1056 | tf_op jit(solution)/shard_map/ppermute | solution.py:44
  271.3 0.1 pad_maximum_fusion.1.refs_5_
  271.4 0.6 all-to-all-done.3.refs_0_
  272.0 2.0 shard_map.86
  (9 shorter events, 0.1 us)
Async XLA Ops:
  3.6 0.9 copy-start
  4.5 0.9 copy-start.1
  15.2 128.6 %all-to-all-start = ((bf16[128,280,128]{2,1,0:T(8,128)(2,1)}), bf16[128,280,128]{2,1,0:T(8,128)(2,1)}, u32[]{:S(2)}, u32[]{:S(2)}) async-start(bf16[128,280,128]{2,1,0:T(8,128)(2,1)} %get-tuple-element.9), calls=%async_computation | async-start | bytes 18350080 | tf_op jit(solution)/shard_map/all_to_all | solution.py:32
  27.2 83.3 %collective-permute-start.2 = (f32[256,1]{1,0:T(8,128)S(1)}, f32[256,1]{1,0:T(8,128)S(1)}, u32[]{:S(2)}, u32[]{:S(2)}) collective-permute-start(f32[256,1]{1,0:T(8,128)S(1)} %get-tuple-element.29), channel_id=1, source_target_pairs={{0,1},{1,2},{2,3},{3,4},{4,5},{5,6},{6,7},{7,8},{8,9},{9,10},{10,1... | collective-permute-start | bytes 3080 | tf_op jit(solution)/shard_map/ppermute | solution.py:43
  30.7 79.9 %collective-permute-start.3 = (f32[256,1]{1,0:T(8,128)S(1)}, f32[256,1]{1,0:T(8,128)S(1)}, u32[]{:S(2)}, u32[]{:S(2)}) collective-permute-start(f32[256,1]{1,0:T(8,128)S(1)} %get-tuple-element.30), channel_id=1, source_target_pairs={{1,0},{2,1},{3,2},{4,3},{5,4},{6,5},{7,6},{8,7},{9,8},{10,9},{11,1... | collective-permute-start | bytes 3080 | tf_op jit(solution)/shard_map/ppermute | solution.py:44
  32.0 152.3 %collective-permute-start = (f32[1,256]{1,0:T(1,128)S(1)}, f32[1,256]{1,0:T(1,128)S(1)}, u32[]{:S(2)}, u32[]{:S(2)}) collective-permute-start(f32[1,256]{1,0:T(1,128)S(1)} %get-tuple-element.31), channel_id=1, source_target_pairs={{0,16},{16,32},{32,48},{48,64},{64,80},{80,96},{96,112},{1,17},{17... | collective-permute-start | bytes 3080 | tf_op jit(solution)/shard_map/ppermute | solution.py:43
  35.6 148.7 %collective-permute-start.1 = (f32[1,256]{1,0:T(1,128)S(1)}, f32[1,256]{1,0:T(1,128)S(1)}, u32[]{:S(2)}, u32[]{:S(2)}) collective-permute-start(f32[1,256]{1,0:T(1,128)S(1)} %get-tuple-element.32), channel_id=1, source_target_pairs={{16,0},{32,16},{48,32},{64,48},{80,64},{96,80},{112,96},{17,1},{33... | collective-permute-start | bytes 3080 | tf_op jit(solution)/shard_map/ppermute | solution.py:44
  175.3 27.9 %all-to-all-start.1 = ((bf16[128,32,128]{2,1,0:T(8,128)(2,1)}), bf16[128,32,128]{2,1,0:T(8,128)(2,1)S(1)}, u32[]{:S(2)}, u32[]{:S(2)}) async-start(bf16[128,32,128]{2,1,0:T(8,128)(2,1)} %shard_map.83), calls=%async_computation.1 | async-start | bytes 2097152 | tf_op jit(solution)/shard_map/all_to_all | solution.py:32
  248.7 23.3 %all-to-all-start.3 = ((bf16[128,32,128]{2,1,0:T(8,128)(2,1)}), bf16[128,32,128]{2,1,0:T(8,128)(2,1)S(1)}, u32[]{:S(2)}, u32[]{:S(2)}) async-start(bf16[128,32,128]{2,1,0:T(8,128)(2,1)} %shard_map.85), calls=%async_computation.3 | async-start | bytes 2097152 | tf_op jit(solution)/shard_map/all_to_all | solution.py:32
  253.0 10.3 %collective-permute-start.4 = (f32[1,256]{1,0:T(1,128)S(1)}, f32[1,256]{1,0:T(1,128)S(1)}, u32[]{:S(2)}, u32[]{:S(2)}) collective-permute-start(f32[1,256]{1,0:T(1,128)S(1)} %get-tuple-element.27), channel_id=1, source_target_pairs={{0,16},{16,32},{32,48},{48,64},{64,80},{80,96},{96,112},{1,17},{17... | collective-permute-start | bytes 3080 | tf_op jit(solution)/shard_map/ppermute | solution.py:43
  256.5 9.6 %collective-permute-start.5 = (f32[1,256]{1,0:T(1,128)S(1)}, f32[1,256]{1,0:T(1,128)S(1)}, u32[]{:S(2)}, u32[]{:S(2)}) collective-permute-start(f32[1,256]{1,0:T(1,128)S(1)} %get-tuple-element.28), channel_id=1, source_target_pairs={{16,0},{32,16},{48,32},{64,48},{80,64},{96,80},{112,96},{17,1},{33... | collective-permute-start | bytes 3080 | tf_op jit(solution)/shard_map/ppermute | solution.py:44
  258.6 9.9 %collective-permute-start.6 = (f32[256,1]{1,0:T(8,128)S(1)}, f32[256,1]{1,0:T(8,128)S(1)}, u32[]{:S(2)}, u32[]{:S(2)}) collective-permute-start(f32[256,1]{1,0:T(8,128)S(1)} %get-tuple-element.25), channel_id=1, source_target_pairs={{0,1},{1,2},{2,3},{3,4},{4,5},{5,6},{6,7},{7,8},{8,9},{9,10},{10,1... | collective-permute-start | bytes 3080 | tf_op jit(solution)/shard_map/ppermute | solution.py:43
  261.9 9.4 %collective-permute-start.7 = (f32[256,1]{1,0:T(8,128)S(1)}, f32[256,1]{1,0:T(8,128)S(1)}, u32[]{:S(2)}, u32[]{:S(2)}) collective-permute-start(f32[256,1]{1,0:T(8,128)S(1)} %get-tuple-element.26), channel_id=1, source_target_pairs={{1,0},{2,1},{3,2},{4,3},{5,4},{6,5},{7,6},{8,7},{9,8},{10,9},{11,1... | collective-permute-start | bytes 3080 | tf_op jit(solution)/shard_map/ppermute | solution.py:44

commit v3 on v2

--- a/solution.py
+++ b/solution.py
@@ -19,9 +19,10 @@
 IMG = 64
 SLAB = 512
 LANES = 128
-PIX_ROWS = IMG * SLAB // LANES
+QUARTERS = SLAB // LANES
+PARTS = ((0, 48), (48, 16))
 EXTRA = 24
-REPLY = 32
+REPLY = 24
 SHOT_CAP = 4
 LOG_2 = 0.6931471805599453
 F32 = jnp.float32
@@ -52,10 +53,10 @@
 PACK_ROWS = 64
 
 
-def swap_matrix():
-    to = lax.broadcasted_iota(jnp.int32, (256, 256), 0)
-    source = lax.broadcasted_iota(jnp.int32, (256, 256), 1)
-    return jnp.where((to % 16) * 16 + to // 16 == source, 1.0, 0.0).astype(BF16)
+def swap_matrix(blocks=16, rows=16):
+    to = lax.broadcasted_iota(jnp.int32, (blocks * rows, blocks * rows), 0)
+    source = lax.broadcasted_iota(jnp.int32, (blocks * rows, blocks * rows), 1)
+    return jnp.where((to % blocks) * rows + to // blocks == source, 1.0, 0.0).astype(BF16)
 
 
 def iota_of(shape, dim):
@@ -69,7 +70,7 @@
 
 def swapped(swap, pieces):
     turned = jnp.dot(swap, jnp.concatenate(pieces, axis=0), preferred_element_type=F32)
-    return turned.astype(BF16).reshape(16, 16, LANES)
+    return turned.astype(BF16).reshape(16, len(pieces), LANES)
 
 
 def around_pieces(even, odd):
@@ -117,7 +118,30 @@
     return rows.astype(BF16)
 
 
-def pack_kernel(images_ref, heights_ref, shadow_ref, table_ref, shots_ref, out_ref, split_ref, extra_ref, halves_ref):
+def pack_images(swap, images_ref, out_ref):
+    count = images_ref.shape[0]
+    for band in range(PACK_ROWS // 16):
+        for group in range(count // 16):
+            block = images_ref[group * 16 : group * 16 + 16, band * 16 : band * 16 + 16]
+            turned = jnp.dot(
+                swap, block.reshape(256, TILE), preferred_element_type=F32
+            ).astype(BF16)
+            for r in range(16):
+                for half in range(TILE // LANES):
+                    place = ((r % 2) * 2 + half) * count + group * 16
+                    out_ref[band * 8 + r // 2, place : place + 16, :] = turned[
+                        r * 16 : r * 16 + 16, half * LANES : half * LANES + LANES
+                    ]
+
+
+def pack_rest_kernel(images_ref, out_ref):
+    pack_images(swap_matrix(), images_ref, out_ref)
+
+
+def pack_kernel(
+    images_ref, heights_ref, shadow_ref, table_ref, shots_ref,
+    out_ref, split_ref, extra_ref, halves_ref,
+):
     step = pl.program_id(0)
     swap = swap_matrix()
 
@@ -152,57 +176,62 @@
             extra_ref[span, 0:16] = swapped(swap, [item[span] for item in first])
             extra_ref[span, 16:32] = swapped(swap, [item[span] for item in second])
 
-    for band in range(PACK_ROWS // 16):
-        for group in range(IMG // 16):
-            block = images_ref[group * 16 : group * 16 + 16, band * 16 : band * 16 + 16]
-            turned = jnp.dot(
-                swap, block.reshape(256, TILE), preferred_element_type=F32
-            ).astype(BF16)
-            for r in range(16):
-                for half in range(TILE // LANES):
-                    place = ((r % 2) * 2 + half) * IMG + group * 16
-                    out_ref[band * 8 + r // 2, place : place + 16, :] = turned[
-                        r * 16 : r * 16 + 16, half * LANES : half * LANES + LANES
-                    ]
+    pack_images(swap, images_ref, out_ref)
     per_step = PACK_ROWS // 2
     here = pl.ds(pl.multiple_of(step * per_step, per_step), per_step)
-    out_ref[:, PIX_ROWS : PIX_ROWS + EXTRA, :] = extra_ref[here, 0:EXTRA, :]
+    pixel_rows = QUARTERS * images_ref.shape[0]
+    out_ref[:, pixel_rows : pixel_rows + EXTRA, :] = extra_ref[here, 0:EXTRA, :]
 
 
 def pack(images, heights, shadow, table, shots):
     per_step = PACK_ROWS // 2
+    count = PARTS[0][1]
+    rows = QUARTERS * count + EXTRA
     whole = lambda s: (0, 0)
     return pl.pallas_call(
         pack_kernel,
         grid=(DEVICES // per_step,),
         in_specs=[
-            pl.BlockSpec((IMG, PACK_ROWS, TILE), lambda s: (0, s, 0)),
+            pl.BlockSpec((count, PACK_ROWS, TILE), lambda s: (0, s, 0)),
             pl.BlockSpec((TILE, TILE), whole),
             pl.BlockSpec((TILE, TILE), whole),
             pl.BlockSpec((8, LANES), whole),
             pl.BlockSpec((8, TILE), whole),
         ],
         out_specs=[
-            pl.BlockSpec((per_step, PIX_ROWS + EXTRA, LANES), lambda s: (s, 0, 0)),
+            pl.BlockSpec((per_step, rows, LANES), lambda s: (s, 0, 0)),
             pl.BlockSpec((TILE, TILE), whole),
         ],
         out_shape=[
-            jax.ShapeDtypeStruct((DEVICES, PIX_ROWS + EXTRA, LANES), BF16),
+            jax.ShapeDtypeStruct((DEVICES, rows, LANES), BF16),
             jax.ShapeDtypeStruct((TILE, TILE), F32),
         ],
         scratch_shapes=[
             pltpu.VMEM((DEVICES, 32, LANES), BF16),
             pltpu.VMEM((4, TILE, LANES), F32),
         ],
-        compiler_params=pltpu.CompilerParams(vmem_limit_bytes=48 * 1024 * 1024),
+        compiler_params=pltpu.CompilerParams(vmem_limit_bytes=58 * 1024 * 1024),
     )(images, heights, shadow, table, shots)
 
 
-SUM_SRC = 16
-SUM_IMG = SUM_SRC * IMG
-HALF_SRC = SUM_SRC // 2
-HALF_IMG = SUM_IMG // 2
-CHUNKS = 4
+def pack_rest(images):
+    per_step = PACK_ROWS // 2
+    start, count = PARTS[1]
+    rows = QUARTERS * count
+    return pl.pallas_call(
+        pack_rest_kernel,
+        grid=(DEVICES // per_step,),
+        in_specs=[pl.BlockSpec((count, PACK_ROWS, TILE), lambda s: (start // count, s, 0))],
+        out_specs=pl.BlockSpec((per_step, rows, LANES), lambda s: (s, 0, 0)),
+        out_shape=jax.ShapeDtypeStruct((DEVICES, rows, LANES), BF16),
+        compiler_params=pltpu.CompilerParams(vmem_limit_bytes=58 * 1024 * 1024),
+        cost_estimate=pl.CostEstimate(
+            flops=2 * 256 * TILE * TILE * count, bytes_accessed=4 * TILE * TILE * count, transcendentals=0
+        ),
+    )(images)
+
+
+SUM_SRC = (32, 64)
 WIDTH = 2 * SLAB + TILE
 
 
@@ -288,49 +317,38 @@
         )
         fields.append(jnp.concatenate([across * (-0.5), grad_y, halo], axis=1))
     seen, model = fields
-    head, tail = two_terms(guess * model - seen)
-    flat = jnp.concatenate([model.astype(BF16), head, tail], axis=1)
-    swap = swap_matrix()
+    flat = jnp.concatenate([model.astype(BF16), (guess * model - seen).astype(BF16)], axis=1)
+    swap, short_swap = swap_matrix(), swap_matrix(8, 16)
     for group in range(DEVICES // 16):
         span = slice(group * 16, group * 16 + 16)
-        pieces = [flat[span, j * LANES : (j + 1) * LANES] for j in range(30)]
-        pieces = pieces + [scalars, jnp.zeros((16, LANES), BF16)]
-        for part in range(2):
-            block = jnp.concatenate(pieces[part * 16 : part * 16 + 16], axis=0)
-            turned = jnp.dot(swap, block, preferred_element_type=F32).astype(BF16)
-            reply_ref[span, part * 16 : part * 16 + 16, :] = turned.reshape(16, 16, LANES)
-
-
-def sum_kernel(
-    me_ref, meta_ref, pixels_ref, around_ref, lit_ref, reply_ref,
-    normal_ref, slopes_ref, rows_ref, sums_ref, plain_ref, first_w, second_w, first_p, second_p,
-):
-    step = pl.program_id(0)
-    me = me_ref[0]
-
-    @pl.when(step == 0)
-    def start():
-        sums_ref[...] = jnp.zeros_like(sums_ref)
-        plain_ref[...] = jnp.zeros_like(plain_ref)
-        second_w[...] = jnp.zeros_like(second_w)
-        second_p[...] = jnp.zeros_like(second_p)
-        slab_normals(me, around_ref, lit_ref, normal_ref, slopes_ref, rows_ref)
+        pieces = [flat[span, j * LANES : (j + 1) * LANES] for j in range(20)]
+        pieces = pieces + [scalars] + [jnp.zeros((16, LANES), BF16)] * 3
+        reply_ref[span, 0:16, :] = swapped(swap, pieces[:16])
+        reply_ref[span, 16:24, :] = swapped(short_swap, pieces[16:])
+
+
+def sum_images(part, meta_ref, pixels_ref, normal_ref, sums_ref, plain_ref, work):
+    first_w, second_w, first_p, second_p = work
+    count = PARTS[part][1]
+    half_src = SUM_SRC[part] // 2
+    half_img = half_src * count
 
     def front(side, w_ref, p_ref):
-        meta = meta_ref[:, side * HALF_IMG : (side + 1) * HALF_IMG]
+        meta = meta_ref[:, side * half_img : (side + 1) * half_img]
         cols = meta.T
-        hot = iota_of((HALF_IMG, DEVICES), 1).astype(F32) == cols[:, 0:1]
+        hot = iota_of((half_img, DEVICES), 1).astype(F32) == cols[:, 0:1]
         sun = [jnp.where(hot, cols[:, j : j + 1], 0.0).astype(BF16) for j in (1, 2, 3)]
         pick = jnp.concatenate([sun[0], sun[1], sun[0], sun[1], sun[2], sun[2]], axis=1)
-        hot_t = iota_of((DEVICES, HALF_IMG), 0).astype(F32) == meta[0:1, :]
+        hot_t = iota_of((DEVICES, half_img), 0).astype(F32) == meta[0:1, :]
         for j in range(3):
             p_ref[j * DEVICES : (j + 1) * DEVICES] = jnp.where(
                 hot_t, meta[j + 1 : j + 2, :], 0.0
             ).astype(BF16)
-        count, images = (HALF_SRC // CHUNKS, HALF_IMG // CHUNKS)
-        for chunk in range(CHUNKS):
+        chunks = half_img // (192 if count == 48 else 128)
+        few, images = (half_src // chunks, half_img // chunks)
+        for chunk in range(chunks):
             span = slice(chunk * images, (chunk + 1) * images)
-            src = slice(side * HALF_SRC + chunk * count, side * HALF_SRC + (chunk + 1) * count)
+            src = slice(side * half_src + chunk * few, side * half_src + (chunk + 1) * few)
             half_angle = jnp.dot(pick[span], normal_ref[...], preferred_element_type=F32)
             gain = cols[span, 4:5]
             bend = jnp.tanh(half_angle)
@@ -338,8 +356,8 @@
             sigma = bend * (gain * 0.5) + gain * 0.5
             seen = jnp.concatenate(
                 [
-                    pixels_ref[src, q * IMG : q * IMG + IMG, :].reshape(images, LANES)
-                    for q in range(SLAB // LANES)
+                    pixels_ref[src, q * count : q * count + count, :].reshape(images, LANES)
+                    for q in range(QUARTERS)
                 ],
                 axis=1,
             ).astype(F32)
@@ -351,60 +369,125 @@
     def back(w_ref, p_ref):
         sums_ref[...] += jnp.dot(p_ref[...], w_ref[...], preferred_element_type=F32)
 
+    @pl.when(pl.program_id(0) == 0)
+    def start():
+        second_w[...] = jnp.zeros_like(second_w)
+        second_p[...] = jnp.zeros_like(second_p)
+
     back(second_w, second_p)
     front(0, first_w, first_p)
     back(first_w, first_p)
     front(1, second_w, second_p)
 
-    @pl.when(step == pl.num_programs(0) - 1)
+    @pl.when(pl.program_id(0) == pl.num_programs(0) - 1)
     def finish():
         back(second_w, second_p)
-        slab_reply(me, lit_ref, slopes_ref, sums_ref, plain_ref, reply_ref)
-
-
-def slab_pass(me, meta, pixels, around, lit):
+
+
+def first_kernel(
+    me_ref, meta_ref, pixels_ref, around_ref, lit_ref,
+    sums_ref, plain_ref, normal_ref, slopes_ref, rows_ref, *work,
+):
+    @pl.when(pl.program_id(0) == 0)
+    def start():
+        sums_ref[...] = jnp.zeros_like(sums_ref)
+        plain_ref[...] = jnp.zeros_like(plain_ref)
+        slab_normals(me_ref[0], around_ref, lit_ref, normal_ref, slopes_ref, rows_ref)
+
+    sum_images(0, meta_ref, pixels_ref, normal_ref, sums_ref, plain_ref, work)
+
+
+def second_kernel(
+    me_ref, meta_ref, pixels_ref, around_ref, lit_ref, sums_in, plain_in,
+    reply_ref, sums_ref, plain_ref, normal_ref, slopes_ref, rows_ref, *work,
+):
+    @pl.when(pl.program_id(0) == 0)
+    def start():
+        sums_ref[...] = sums_in[...]
+        plain_ref[...] = plain_in[...]
+        slab_normals(me_ref[0], around_ref, lit_ref, normal_ref, slopes_ref, rows_ref)
+
+    sum_images(1, meta_ref, pixels_ref, normal_ref, sums_ref, plain_ref, work)
+
+    @pl.when(pl.program_id(0) == pl.num_programs(0) - 1)
+    def finish():
+        slab_reply(me_ref[0], lit_ref, slopes_ref, sums_ref, plain_ref, reply_ref)
+
+
+SUMS = ((3 * DEVICES, 2 * SLAB), F32)
+PLAIN = ((8, 2 * SLAB), F32)
+NORMALS = ((6 * DEVICES, SLAB), BF16)
+SLOPES = ((3, DEVICES, SLAB), F32)
+ROWS = ((4, DEVICES, TILE), F32)
+
+
+def kept(shape):
+    return pl.BlockSpec(shape, lambda s: (0,) * len(shape))
+
+
+def sum_call(part, kernel, inputs, specs, outs, scratch):
+    count, sources = PARTS[part][1], SUM_SRC[part]
+    half = sources * count // 2
+    rows = QUARTERS * count + (EXTRA if part == 0 else 0)
+    cells = DEVICES * count * SLAB
     return pl.pallas_call(
-        sum_kernel,
-        grid=(DEVICES // SUM_SRC,),
+        kernel,
+        grid=(DEVICES // sources,),
         in_specs=[
             pl.BlockSpec(memory_space=pltpu.SMEM),
-            pl.BlockSpec((8, SUM_IMG), lambda s: (0, s)),
-            pl.BlockSpec((SUM_SRC, PIX_ROWS + EXTRA, LANES), lambda s: (s, 0, 0)),
-            pl.BlockSpec((DEVICES, 16, LANES), lambda s: (0, 0, 0)),
-            pl.BlockSpec((DEVICES, SLAB), lambda s: (0, 0)),
-        ],
-        out_specs=pl.BlockSpec((DEVICES, REPLY, LANES), lambda s: (0, 0, 0)),
-        out_shape=jax.ShapeDtypeStruct((DEVICES, REPLY, LANES), BF16),
-        scratch_shapes=[
-            pltpu.VMEM((6 * DEVICES, SLAB), BF16),
-            pltpu.VMEM((3, DEVICES, SLAB), F32),
-            pltpu.VMEM((4, DEVICES, TILE), F32),
-            pltpu.VMEM((3 * DEVICES, 2 * SLAB), F32),
-            pltpu.VMEM((8, 2 * SLAB), F32),
-            pltpu.VMEM((HALF_IMG, 2 * SLAB), BF16),
-            pltpu.VMEM((HALF_IMG, 2 * SLAB), BF16),
-            pltpu.VMEM((3 * DEVICES, HALF_IMG), BF16),
-            pltpu.VMEM((3 * DEVICES, HALF_IMG), BF16),
-        ],
-        compiler_params=pltpu.CompilerParams(vmem_limit_bytes=48 * 1024 * 1024),
-    )(me, meta, pixels, around, lit)
+            pl.BlockSpec((8, sources * count), lambda s: (0, s)),
+            pl.BlockSpec((sources, rows, LANES), lambda s: (s, 0, 0)),
+        ]
+        + specs,
+        out_specs=[kept(shape) for shape, dtype in outs],
+        out_shape=[jax.ShapeDtypeStruct(shape, dtype) for shape, dtype in outs],
+        scratch_shapes=[pltpu.VMEM(shape, dtype) for shape, dtype in scratch]
+        + [pltpu.VMEM((half, 2 * SLAB), BF16)] * 2
+        + [pltpu.VMEM((3 * DEVICES, half), BF16)] * 2,
+        compiler_params=pltpu.CompilerParams(vmem_limit_bytes=44 * 1024 * 1024),
+        cost_estimate=pl.CostEstimate(
+            flops=2 * 12 * DEVICES * cells, bytes_accessed=4 * cells, transcendentals=2 * cells
+        ),
+    )(*inputs)
+
+
+def first_sums(me, meta, pixels, around, lit):
+    return sum_call(
+        0,
+        first_kernel,
+        (me, meta, pixels, around, lit),
+        [kept((DEVICES, 16, LANES)), kept((DEVICES, SLAB))],
+        (SUMS, PLAIN),
+        (NORMALS, SLOPES, ROWS),
+    )
+
+
+def second_sums(me, meta, pixels, around, lit, sums, plain):
+    return sum_call(
+        1,
+        second_kernel,
+        (me, meta, pixels, around, lit, sums, plain),
+        [kept((DEVICES, 16, LANES)), kept((DEVICES, SLAB)), kept(SUMS[0]), kept(PLAIN[0])],
+        (((DEVICES, REPLY, LANES), BF16),),
+        (SUMS, PLAIN, NORMALS, SLOPES, ROWS),
+    )[0]
 
 
 def owner_kernel(final, *refs):
     got_ref, surface_ref, hits_ref, height_ref, ends_ref, sides_ref = refs[:6]
     outs, (model_ref, misfit_ref, scalar_ref, mixed_ref) = refs[6:-4], refs[-4:]
-    swap = swap_matrix()
+    swap, short_swap = swap_matrix(), swap_matrix(16, 8)
     for group in range(DEVICES // 16):
         span = slice(group * 16, group * 16 + 16)
         rows = []
-        for part in range(2):
-            block = got_ref[span, part * 16 : part * 16 + 16, :].reshape(256, LANES)
-            turned = jnp.dot(swap, block, preferred_element_type=F32)
-            rows += [turned[j * 16 : j * 16 + 16] for j in range(16)]
+        for matrix, start, count in ((swap, 0, 16), (short_swap, 16, 8)):
+            block = got_ref[span, start : start + count, :].reshape(16 * count, LANES)
+            turned = jnp.dot(matrix, block, preferred_element_type=F32)
+            rows += [turned[j * 16 : j * 16 + 16] for j in range(count)]
         for j in range(10):
             model_ref[j, span] = rows[j]
-            misfit_ref[j, span] = rows[10 + j] + rows[20 + j]
-        scalar_ref[span] = rows[30]
+            misfit_ref[j, span] = rows[10 + j]
+        scalar_ref[span] = rows[20]
     scalars = scalar_ref[...]
     cross = scalars[:, 0:1] + scalars[:, 1:2] + scalars[:, 2:3]
     power = scalars[:, 3:4] + scalars[:, 4:5] + scalars[:, 5:6]
@@ -501,28 +584,30 @@
     shots = jnp.pad(shots, ((0, 5), (0, 0)))
     packed, surface = pack(image_tiles, heights, shadow, table, shots)
     rims = edges(surface)
-    pixels = exchange(packed)
-    extra = pixels[:, PIX_ROWS:, :]
-    meta = jnp.stack(
-        [
-            extra[:, 20, :IMG],
-            extra[:, 21, :IMG],
-            extra[:, 21, IMG:],
-            extra[:, 22, :IMG],
-            extra[:, 22, IMG:],
+    pixels = (exchange(packed), exchange(pack_rest(image_tiles)))
+    extra = pixels[0][:, QUARTERS * PARTS[0][1] :, :]
+    metas = []
+    for start, count in PARTS:
+        lists = [
+            extra[:, row, at + start : at + start + count]
+            for row, at in ((20, 0), (21, 0), (21, IMG), (22, 0), (22, IMG))
         ]
-    ).astype(F32)
-    meta = jnp.pad(meta.reshape(5, DEVICES * IMG), ((0, 3), (0, 0)))
+        meta = jnp.stack(lists).astype(F32).reshape(5, DEVICES * count)
+        metas.append(jnp.pad(meta, ((0, 3), (0, 0))))
     slab_lit = extra[:, 16:20, :].reshape(DEVICES, SLAB).astype(F32)
     around = extra[:, 0:16, :]
     slots = extra[:, 23, : SHOT_CAP * 5].reshape(DEVICES * SHOT_CAP, 5).astype(F32)
     hits, height_sum = shot_sums(slots)
-    reply = slab_pass(me, meta, pixels, around, slab_lit)
-    got = exchange(reply)
+
+    def slab_pass(around):
+        begun = first_sums(me, metas[0], pixels[0], around, slab_lit)
+        return second_sums(me, metas[1], pixels[1], around, slab_lit, *begun)
+
+    got = exchange(slab_pass(around))
     surface, around = owner_update(False, got, surface, hits, height_sum, rims)
     around = exchange(around)
     rims = edges(surface)
-    got = exchange(slab_pass(me, meta, pixels, around, slab_lit))
+    got = exchange(slab_pass(around))
     return owner_update(True, got, surface, hits, height_sum, rims)[0]
 
 

time: 275 us -> 261 us (0.949)
  waiting for transfers between devices: 131 us -> 92.9 us
  starting transfers between devices: 45.5 us -> 54.9 us
  local copies, waits for them, and re-layouts: 7.8 us -> 15.6 us
  Pallas kernels: 64.9 us -> 68.5 us
    ppermute x4, waiting for transfers between devices: 75.3 us -> 0.01 us  [edges(): out.append(lax.ppermute(last, axis, up))]
    ppermute x4, waiting for transfers between devices: 5.81 us -> 70.8 us  [edges(): out.append(lax.ppermute(first, axis, down))]
    all_to_all x3 -> x4, waiting for transfers between devices: 49.7 us -> 22.1 us  [exchange(): return lax.all_to_all(value, AXES, split_axis=0, concat_axis=0, tiled=True)]
    all_to_all x3 -> x4, starting transfers between devices: 25.1 us -> 32.9 us  [exchange(): return lax.all_to_all(value, AXES, split_axis=0, concat_axis=0, tiled=True)]
    pallas_call x2 -> x5, Pallas kernels: 51.4 us -> 56.6 us  [the longest x4 52.3 us: sum_call(): pl.pallas_call(kernel, grid=(DEVICES // sources,), in_specs=[pl.BlockSpec...]
    unnamed x5 -> x29, local copies, waits for them, and re-layouts: 1.92 us -> 6.02 us
  transfers between devices with their start and end apart: 11 -> 12, of which waited for: 7 -> 6; matrix products, arithmetic and copies ran while one was open for 3% -> 5% of each run, Pallas kernels for 9% -> 9%
where the time goes in v3:
time: 261 us; the launch traced here: 257 us
  waiting for transfers between devices  92.9 us (36%)
  Pallas kernels  68.5 us (26%)
  starting transfers between devices  54.9 us (21%)
  blocking collectives  17.8 us (7%)
  local copies, waits for them, and re-layouts  15.6 us (6%)
  other arithmetic  6.85 us (3%)
    ppermute x4, waiting for transfers between devices, edges(): out.append(lax.ppermute(first, axis, down))  70.8 us
    pallas_call x4, Pallas kernels, sum_call(): pl.pallas_call(kernel, grid=(DEVICES // sources,), in_specs=[pl.BlockSpec...  52.3 us
    all_to_all x4, starting transfers between devices, exchange(): return lax.all_to_all(value, AXES, split_axis=0, concat_axis=0, tiled=True)  32.9 us
    all_to_all x4, waiting for transfers between devices, exchange(): return lax.all_to_all(value, AXES, split_axis=0, concat_axis=0, tiled=True)  22.1 us
    all_to_all x1, blocking collectives, exchange(): return lax.all_to_all(value, AXES, split_axis=0, concat_axis=0, tiled=True)  17.8 us
    ppermute x4, starting transfers between devices, edges(): out.append(lax.ppermute(last, axis, up))  13.2 us
    ppermute x4, starting transfers between devices, edges(): out.append(lax.ppermute(first, axis, down))  8.74 us
    pallas_call x1, Pallas kernels, pack(): pl.pallas_call(pack_kernel, grid=(DEVICES // per_step,), in_specs=[pl.Blo...  8.61 us
  transfers between devices with their start and end apart: 12, of which 6 were waited for; matrix products, arithmetic and copies ran while one was open for 5% of the time, Pallas kernels for 9%

profile of v3, /device:TPU:1, one launch (start us, length us, event | category | flops | bytes accessed | tf_op | source)
XLA Modules:
  0.0 257.5 jit_solution(2052612635681744328)
XLA Ops:
  0.0 0.7 convert_bitcast_fusion
  0.7 0.1 reshape.57
  0.8 0.7 convert_bitcast_fusion.2
  1.5 0.6 pad.20.table_ref
  2.1 0.7 convert_element_type.64
  2.8 0.7 convert_bitcast_fusion.1
  3.5 1.3 select_maximum_fusion.shots_ref
  4.7 8.6 %shard_map.82 = (bf16[128,216,128]{2,1,0:T(8,128)(2,1)}, f32[256,256]{1,0:T(8,128)}) custom-call(bf16[64,256,256]{2,1,0:T(8,128)(2,1)} %images_ref.3, f32[256,256]{1,0:T(8,128)} %heights_ref.1, s32[256,256]{1,0:T(8,128)} %shadow_ref.1, f32[8,128]{1,0:T(8,128)} %pad.20.table_ref, f32[8,256]{1,0:T(8,128)} %select_maximum_fusion.shots_ref), custom_call_target="tpu_custom_call" | custom-call | tf_op jit(solution)/shard_map/pallas_call | solution.py:191
  13.4 11.9 %all-to-all-start = ((bf16[128,216,128]{2,1,0:T(8,128)(2,1)}), bf16[128,216,128]{2,1,0:T(8,128)(2,1)}, u32[]{:S(2)}, u32[]{:S(2)}) async-start(bf16[128,216,128]{2,1,0:T(8,128)(2,1)} %get-tuple-element.13), calls=%async_computation | async-start | bytes 14155776 | tf_op jit(solution)/shard_map/all_to_all | solution.py:33
  25.3 3.0 %collective-permute-start.1 = (f32[1,256]{1,0:T(1,128)S(1)}, f32[1,256]{1,0:T(1,128)S(1)}, u32[]{:S(2)}, u32[]{:S(2)}) collective-permute-start(f32[1,256]{1,0:T(1,128)S(1)} %get-tuple-element.45), channel_id=1, source_target_pairs={{16,0},{32,16},{48,32},{64,48},{80,64},{96,80},{112,96},{17,1},{33... | collective-permute-start | bytes 3080 | tf_op jit(solution)/shard_map/ppermute | solution.py:45
  28.3 2.5 collective-permute-start
  30.9 0.1 fusion.22
  31.0 1.3 collective-permute-start.3
  32.3 4.0 %collective-permute-start.2 = (f32[256,1]{1,0:T(8,128)S(1)}, f32[256,1]{1,0:T(8,128)S(1)}, u32[]{:S(2)}, u32[]{:S(2)}) collective-permute-start(f32[256,1]{1,0:T(8,128)S(1)} %get-tuple-element.42), channel_id=1, source_target_pairs={{0,1},{1,2},{2,3},{3,4},{4,5},{5,6},{6,7},{7,8},{8,9},{9,10},{10,1... | collective-permute-start | bytes 3080 | tf_op jit(solution)/shard_map/ppermute | solution.py:44
  36.3 4.3 %shard_map.83 = bf16[128,64,128]{2,1,0:T(8,128)(2,1)} custom-call(bf16[64,256,256]{2,1,0:T(8,128)(2,1)} %images_ref.3), custom_call_target="tpu_custom_call" | custom-call | flops 536870912 | bytes 4194304 | tf_op jit(solution)/shard_map/pallas_call | solution.py:221
  40.7 66.3 %collective-permute-done.1 = f32[1,256]{1,0:T(1,128)S(1)} collective-permute-done((f32[1,256]{1,0:T(1,128)S(1)}, f32[1,256]{1,0:T(1,128)S(1)}, u32[]{:S(2)}, u32[]{:S(2)}) %collective-permute-start.1) | collective-permute-done | bytes 1056 | tf_op jit(solution)/shard_map/ppermute | solution.py:45
  107.0 0.1 pad_maximum_fusion.refs_5_
  107.1 7.1 %all-to-all-done.pixels_ref = bf16[128,216,128]{2,1,0:T(8,128)(2,1)} async-done(((bf16[128,216,128]{2,1,0:T(8,128)(2,1)}), bf16[128,216,128]{2,1,0:T(8,128)(2,1)}, u32[]{:S(2)}, u32[]{:S(2)}) %all-to-all-start) | async-done | bytes 7077920 | tf_op jit(solution)/shard_map/all_to_all | solution.py:33
  114.2 7.8 %all-to-all-start.1 = ((bf16[128,64,128]{2,1,0:T(8,128)(2,1)}), bf16[128,64,128]{2,1,0:T(8,128)(2,1)S(1)}, u32[]{:S(2)}, u32[]{:S(2)}) async-start(bf16[128,64,128]{2,1,0:T(8,128)(2,1)} %shard_map.83), calls=%async_computation.1 | async-start | bytes 4194304 | tf_op jit(solution)/shard_map/all_to_all | solution.py:33
  122.0 1.0 slice_convert_fusion
  123.0 2.8 %slice_reduce_fusion.10 = (bf16[128,16]{1,0:T(8,128)(2,1)S(1)}, bf16[128,16]{1,0:T(8,128)(2,1)S(1)}, bf16[128,16]{1,0:T(8,128)(2,1)S(1)}, bf16[128,16]{1,0:T(8,128)(2,1)S(1)}, bf16[128,16]{1,0:T(8,128)(2,1)S(1)}) fusion(bf16[128,216,128]{2,1,0:T(8,128)(2,1)} %all-to-all-done.pixels_ref), kind=kLoop, calls=%fused_computation.38 | loop fusion | bytes 40960 | tf_op jit(solution)/shard_map/slice | solution.py:592
  125.8 0.1 stack.39
  125.9 0.1 stack.40
  126.0 0.1 stack.41
  126.1 0.1 stack.42
  126.2 0.1 stack.43
  126.3 2.7 %slice_reduce_fusion.5 = (bf16[128,48]{1,0:T(8,128)(2,1)S(1)}, bf16[128,48]{1,0:T(8,128)(2,1)S(1)}, bf16[128,48]{1,0:T(8,128)(2,1)S(1)}, bf16[128,48]{1,0:T(8,128)(2,1)S(1)}, bf16[128,48]{1,0:T(8,128)(2,1)S(1)}) fusion(bf16[128,216,128]{2,1,0:T(8,128)(2,1)} %all-to-all-done.pixels_ref), kind=kLoop, calls=%fused_computation.33 | loop fusion | bytes 122880 | tf_op jit(solution)/shard_map/slice | solution.py:592
  129.0 0.1 stack.45
  129.1 0.1 stack.46
  129.2 0.1 stack.47
  129.3 0.1 stack.48
  129.4 0.1 stack.49
  129.6 0.2 stack.50
  129.8 1.1 slice.136.around_ref
  130.9 18.6 %shard_map.84 = (f32[384,1024]{1,0:T(8,128)S(1)}, f32[8,1024]{1,0:T(8,128)S(1)}) custom-call(s32[1]{0:T(128)} %bitcast.me_ref, f32[8,6144]{1,0:T(8,128)S(1)} %pad_convert_fusion.meta_ref, bf16[128,216,128]{2,1,0:T(8,128)(2,1)} %all-to-all-done.pixels_ref, bf16[128,16,128]{2,1,0:T(8,128)(2,1)S(1)} %slice.136.around_ref, f32[128,512]{1,0:T(8,128)S(1)} %bitcast.15), custom_call_target="tpu_custom_call" | custom-call | flops 9663676416 | bytes 12582912 | tf_op jit(solution)/shard_map/pallas_call | solution.py:433
  149.6 1.2 copy-done.12
  150.7 0.7 all-to-all-done.1.pixels_ref
  151.5 1.4 copy-done.13
  152.9 7.5 %shard_map.85 = bf16[128,24,128]{2,1,0:T(8,128)(2,1)S(1)} custom-call(s32[1]{0:T(128)} %bitcast.me_ref, f32[8,2048]{1,0:T(8,128)S(1)} %pad_convert_fusion.1.meta_ref, bf16[128,64,128]{2,1,0:T(8,128)(2,1)S(1)} %all-to-all-done.1.pixels_ref, bf16[128,16,128]{2,1,0:T(8,128)(2,1)S(1)} %slice.136.around_ref, f32[128,512]{1,0:T(8,128)S(1)} %bitcast.16, ...), custom_call_target="tpu_custom_call" | custom-call | flops 3221225472 | bytes 4194304 | tf_op jit(solution)/shard_map/pallas_call | solution.py:433
  160.4 0.9 copy-done.5
  161.3 9.0 %all-to-all-start.2 = ((bf16[128,24,128]{2,1,0:T(8,128)(2,1)}), bf16[128,24,128]{2,1,0:T(8,128)(2,1)S(1)}, u32[]{:S(2)}, u32[]{:S(2)}) async-start(bf16[128,24,128]{2,1,0:T(8,128)(2,1)} %copy-done.5), calls=%async_computation.2 | async-start | bytes 1572864 | tf_op jit(solution)/shard_map/all_to_all | solution.py:33
  170.4 1.2 fusion.16
  171.5 0.1 reshape.59
  171.7 0.7 slice_reduce_fusion
  172.4 0.3 fusion.7
  172.7 0.5 fusion
  173.3 13.5 %all-to-all-done.2.refs_0_ = bf16[128,24,128]{2,1,0:T(8,128)(2,1)S(1)} async-done(((bf16[128,24,128]{2,1,0:T(8,128)(2,1)}), bf16[128,24,128]{2,1,0:T(8,128)(2,1)S(1)}, u32[]{:S(2)}, u32[]{:S(2)}) %all-to-all-start.2) | async-done | bytes 786464 | tf_op jit(solution)/shard_map/all_to_all | solution.py:33
  186.8 0.9 copy-done.3
  187.8 1.6 shard_map.86
  189.3 0.7 copy-done
  190.0 17.8 %all_to_all.25.around_ref = bf16[128,16,128]{2,1,0:T(8,128)(2,1)S(1)} all-to-all(bf16[128,16,128]{2,1,0:T(8,128)(2,1)S(1)} %get-tuple-element.17), channel_id=1, replica_groups=mesh['row'=8,'col'=16] {'row','col'}, dimensions={0} | all-to-all | bytes 1048576 | tf_op jit(solution)/shard_map/all_to_all | solution.py:33
  207.8 18.6 %shard_map.87 = (f32[384,1024]{1,0:T(8,128)S(1)}, f32[8,1024]{1,0:T(8,128)S(1)}) custom-call(s32[1]{0:T(128)} %bitcast.me_ref, f32[8,6144]{1,0:T(8,128)S(1)} %copy-done.9, bf16[128,216,128]{2,1,0:T(8,128)(2,1)} %all-to-all-done.pixels_ref, bf16[128,16,128]{2,1,0:T(8,128)(2,1)S(1)} %all_to_all.25.around_ref, f32[128,512]{1,0:T(8,128)S(1)} %bitcast.17), custom_call_target="tpu_custom_call" | custom-call | flops 9663676416 | bytes 12582912 | tf_op jit(solution)/shard_map/pallas_call | solution.py:433
  226.4 7.6 %shard_map.88 = bf16[128,24,128]{2,1,0:T(8,128)(2,1)S(1)} custom-call(s32[1]{0:T(128)} %bitcast.me_ref, f32[8,2048]{1,0:T(8,128)S(1)} %copy-done.11, bf16[128,64,128]{2,1,0:T(8,128)(2,1)S(1)} %all-to-all-done.1.pixels_ref, bf16[128,16,128]{2,1,0:T(8,128)(2,1)S(1)} %all_to_all.25.around_ref, f32[128,512]{1,0:T(8,128)S(1)} %bitcast.18, ...), custom_call_target="tpu_custom_call" | custom-call | flops 3221225472 | bytes 4194304 | tf_op jit(solution)/shard_map/pallas_call | solution.py:433
  234.0 0.9 copy-done.4
  234.9 4.2 %all-to-all-start.4 = ((bf16[128,24,128]{2,1,0:T(8,128)(2,1)}), bf16[128,24,128]{2,1,0:T(8,128)(2,1)S(1)}, u32[]{:S(2)}, u32[]{:S(2)}) async-start(bf16[128,24,128]{2,1,0:T(8,128)(2,1)} %copy-done.4), calls=%async_computation.4 | async-start | bytes 1572864 | tf_op jit(solution)/shard_map/all_to_all | solution.py:33
  239.1 3.1 %collective-permute-start.5 = (f32[1,256]{1,0:T(1,128)S(1)}, f32[1,256]{1,0:T(1,128)S(1)}, u32[]{:S(2)}, u32[]{:S(2)}) collective-permute-start(f32[1,256]{1,0:T(1,128)S(1)} %get-tuple-element.41), channel_id=1, source_target_pairs={{16,0},{32,16},{48,32},{64,48},{80,64},{96,80},{112,96},{17,1},{33... | collective-permute-start | bytes 3080 | tf_op jit(solution)/shard_map/ppermute | solution.py:45
  242.2 2.4 collective-permute-start.4
  244.7 0.1 fusion.20
  244.8 1.3 collective-permute-start.7
  246.1 4.2 %collective-permute-start.6 = (f32[256,1]{1,0:T(8,128)S(1)}, f32[256,1]{1,0:T(8,128)S(1)}, u32[]{:S(2)}, u32[]{:S(2)}) collective-permute-start(f32[256,1]{1,0:T(8,128)S(1)} %get-tuple-element.38), channel_id=1, source_target_pairs={{0,1},{1,2},{2,3},{3,4},{4,5},{5,6},{6,7},{7,8},{8,9},{9,10},{10,1... | collective-permute-start | bytes 3080 | tf_op jit(solution)/shard_map/ppermute | solution.py:44
  250.3 4.5 %collective-permute-done.7 = f32[256,1]{1,0:T(8,128)S(1)} collective-permute-done((f32[256,1]{1,0:T(8,128)S(1)}, f32[256,1]{1,0:T(8,128)S(1)}, u32[]{:S(2)}, u32[]{:S(2)}) %collective-permute-start.7) | collective-permute-done | bytes 1056 | tf_op jit(solution)/shard_map/ppermute | solution.py:45
  254.8 0.1 pad_maximum_fusion.1.refs_5_
  254.9 0.8 all-to-all-done.4.refs_0_
  255.7 1.8 shard_map.89
  (40 shorter events, 0.3 us)
Async XLA Ops:
  13.4 11.9 %copy-start.2 = (f32[256,256]{1,0:T(8,128)S(1)}, f32[256,256]{1,0:T(8,128)}, u32[]{:S(2)}) copy-start(f32[256,256]{1,0:T(8,128)} %get-tuple-element.16.refs_1_) | copy-start | bytes 786436
  13.4 100.8 %all-to-all-start = ((bf16[128,216,128]{2,1,0:T(8,128)(2,1)}), bf16[128,216,128]{2,1,0:T(8,128)(2,1)}, u32[]{:S(2)}, u32[]{:S(2)}) async-start(bf16[128,216,128]{2,1,0:T(8,128)(2,1)} %get-tuple-element.13), calls=%async_computation | async-start | bytes 14155776 | tf_op jit(solution)/shard_map/all_to_all | solution.py:33
  25.3 81.7 %collective-permute-start.1 = (f32[1,256]{1,0:T(1,128)S(1)}, f32[1,256]{1,0:T(1,128)S(1)}, u32[]{:S(2)}, u32[]{:S(2)}) collective-permute-start(f32[1,256]{1,0:T(1,128)S(1)} %get-tuple-element.45), channel_id=1, source_target_pairs={{16,0},{32,16},{48,32},{64,48},{80,64},{96,80},{112,96},{17,1},{33... | collective-permute-start | bytes 3080 | tf_op jit(solution)/shard_map/ppermute | solution.py:45
  28.3 78.6 %collective-permute-start = (f32[1,256]{1,0:T(1,128)S(1)}, f32[1,256]{1,0:T(1,128)S(1)}, u32[]{:S(2)}, u32[]{:S(2)}) collective-permute-start(f32[1,256]{1,0:T(1,128)S(1)} %get-tuple-element.44), channel_id=1, source_target_pairs={{0,16},{16,32},{32,48},{48,64},{64,80},{80,96},{96,112},{1,17},{17... | collective-permute-start | bytes 3080 | tf_op jit(solution)/shard_map/ppermute | solution.py:44
  31.0 76.0 %collective-permute-start.3 = (f32[256,1]{1,0:T(8,128)S(1)}, f32[256,1]{1,0:T(8,128)S(1)}, u32[]{:S(2)}, u32[]{:S(2)}) collective-permute-start(f32[256,1]{1,0:T(8,128)S(1)} %get-tuple-element.43), channel_id=1, source_target_pairs={{1,0},{2,1},{3,2},{4,3},{5,4},{6,5},{7,6},{8,7},{9,8},{10,9},{11,1... | collective-permute-start | bytes 3080 | tf_op jit(solution)/shard_map/ppermute | solution.py:45
  32.3 74.7 %collective-permute-start.2 = (f32[256,1]{1,0:T(8,128)S(1)}, f32[256,1]{1,0:T(8,128)S(1)}, u32[]{:S(2)}, u32[]{:S(2)}) collective-permute-start(f32[256,1]{1,0:T(8,128)S(1)} %get-tuple-element.42), channel_id=1, source_target_pairs={{0,1},{1,2},{2,3},{3,4},{4,5},{5,6},{6,7},{7,8},{8,9},{9,10},{10,1... | collective-permute-start | bytes 3080 | tf_op jit(solution)/shard_map/ppermute | solution.py:44
  114.2 37.3 %all-to-all-start.1 = ((bf16[128,64,128]{2,1,0:T(8,128)(2,1)}), bf16[128,64,128]{2,1,0:T(8,128)(2,1)S(1)}, u32[]{:S(2)}, u32[]{:S(2)}) async-start(bf16[128,64,128]{2,1,0:T(8,128)(2,1)} %shard_map.83), calls=%async_computation.1 | async-start | bytes 4194304 | tf_op jit(solution)/shard_map/all_to_all | solution.py:33
  126.3 25.2 %copy-start.6 = (f32[16,8,4,128]{3,1,2,0:T(8,128)}, f32[16,8,4,128]{3,1,2,0:T(8,128)S(1)}, u32[]{:S(2)}) copy-start(f32[16,8,4,128]{3,1,2,0:T(8,128)S(1)} %copy.17) | copy-start | bytes 786436
  130.9 20.6 %copy-start.10 = (f32[8,2048]{1,0:T(8,128)}, f32[8,2048]{1,0:T(8,128)S(1)}, u32[]{:S(2)}) copy-start(f32[8,2048]{1,0:T(8,128)S(1)} %pad_convert_fusion.1.meta_ref) | copy-start | bytes 196612
  130.9 18.6 %copy-start.8 = (f32[8,6144]{1,0:T(8,128)}, f32[8,6144]{1,0:T(8,128)S(1)}, u32[]{:S(2)}) copy-start(f32[8,6144]{1,0:T(8,128)S(1)} %pad_convert_fusion.meta_ref) | copy-start | bytes 589828
  149.6 1.2 copy-start.12
  151.5 1.4 copy-start.13
  160.4 0.9 copy-start.5
  161.3 25.5 %all-to-all-start.2 = ((bf16[128,24,128]{2,1,0:T(8,128)(2,1)}), bf16[128,24,128]{2,1,0:T(8,128)(2,1)S(1)}, u32[]{:S(2)}, u32[]{:S(2)}) async-start(bf16[128,24,128]{2,1,0:T(8,128)(2,1)} %copy-done.5), calls=%async_computation.2 | async-start | bytes 1572864 | tf_op jit(solution)/shard_map/all_to_all | solution.py:33
  186.8 1.0 copy-start.3
  187.8 20.0 %copy-start.7 = (f32[16,8,4,128]{3,1,2,0:T(8,128)S(1)}, f32[16,8,4,128]{3,1,2,0:T(8,128)}, u32[]{:S(2)}) copy-start(f32[16,8,4,128]{3,1,2,0:T(8,128)} %copy-done.6) | copy-start | bytes 786436
  187.8 20.0 %copy-start.9 = (f32[8,6144]{1,0:T(8,128)S(1)}, f32[8,6144]{1,0:T(8,128)}, u32[]{:S(2)}) copy-start(f32[8,6144]{1,0:T(8,128)} %copy-done.8) | copy-start | bytes 589828
  189.3 0.7 copy-start
  207.8 18.6 %copy-start.11 = (f32[8,2048]{1,0:T(8,128)S(1)}, f32[8,2048]{1,0:T(8,128)}, u32[]{:S(2)}) copy-start(f32[8,2048]{1,0:T(8,128)} %copy-done.10) | copy-start | bytes 196612
  226.4 12.7 %copy-start.1 = (f32[256,256]{1,0:T(8,128)S(1)}, f32[256,256]{1,0:T(8,128)}, u32[]{:S(2)}) copy-start(f32[256,256]{1,0:T(8,128)} %copy-done) | copy-start | bytes 786436
  234.0 0.9 copy-start.4
  234.9 20.8 %all-to-all-start.4 = ((bf16[128,24,128]{2,1,0:T(8,128)(2,1)}), bf16[128,24,128]{2,1,0:T(8,128)(2,1)S(1)}, u32[]{:S(2)}, u32[]{:S(2)}) async-start(bf16[128,24,128]{2,1,0:T(8,128)(2,1)} %copy-done.4), calls=%async_computation.4 | async-start | bytes 1572864 | tf_op jit(solution)/shard_map/all_to_all | solution.py:33
  239.1 11.2 %collective-permute-start.5 = (f32[1,256]{1,0:T(1,128)S(1)}, f32[1,256]{1,0:T(1,128)S(1)}, u32[]{:S(2)}, u32[]{:S(2)}) collective-permute-start(f32[1,256]{1,0:T(1,128)S(1)} %get-tuple-element.41), channel_id=1, source_target_pairs={{16,0},{32,16},{48,32},{64,48},{80,64},{96,80},{112,96},{17,1},{33... | collective-permute-start | bytes 3080 | tf_op jit(solution)/shard_map/ppermute | solution.py:45
  242.2 8.1 %collective-permute-start.4 = (f32[1,256]{1,0:T(1,128)S(1)}, f32[1,256]{1,0:T(1,128)S(1)}, u32[]{:S(2)}, u32[]{:S(2)}) collective-permute-start(f32[1,256]{1,0:T(1,128)S(1)} %get-tuple-element.40), channel_id=1, source_target_pairs={{0,16},{16,32},{32,48},{48,64},{64,80},{80,96},{96,112},{1,17},{17... | collective-permute-start | bytes 3080 | tf_op jit(solution)/shard_map/ppermute | solution.py:44
  244.8 10.0 %collective-permute-start.7 = (f32[256,1]{1,0:T(8,128)S(1)}, f32[256,1]{1,0:T(8,128)S(1)}, u32[]{:S(2)}, u32[]{:S(2)}) collective-permute-start(f32[256,1]{1,0:T(8,128)S(1)} %get-tuple-element.39), channel_id=1, source_target_pairs={{1,0},{2,1},{3,2},{4,3},{5,4},{6,5},{7,6},{8,7},{9,8},{10,9},{11,1... | collective-permute-start | bytes 3080 | tf_op jit(solution)/shard_map/ppermute | solution.py:45
  246.1 8.7 %collective-permute-start.6 = (f32[256,1]{1,0:T(8,128)S(1)}, f32[256,1]{1,0:T(8,128)S(1)}, u32[]{:S(2)}, u32[]{:S(2)}) collective-permute-start(f32[256,1]{1,0:T(8,128)S(1)} %get-tuple-element.38), channel_id=1, source_target_pairs={{0,1},{1,2},{2,3},{3,4},{4,5},{5,6},{6,7},{7,8},{8,9},{9,10},{10,1... | collective-permute-start | bytes 3080 | tf_op jit(solution)/shard_map/ppermute | solution.py:44

commit v4 on v3

--- a/solution.py
+++ b/solution.py
@@ -84,9 +84,8 @@
     ]
 
 
-def shot_rows(shots):
-    count = shots.shape[1]
-    target, pixel, height = shots[0:1], shots[1:2], shots[2:3]
+def shot_rows(target, pixel, height):
+    count = target.shape[1]
     head = height.astype(BF16).astype(F32)
     grid_row = jnp.floor(pixel * (1.0 / TILE))
     pair = jnp.floor(grid_row * 0.5)
@@ -139,7 +138,7 @@
 
 
 def pack_kernel(
-    images_ref, heights_ref, shadow_ref, table_ref, shots_ref,
+    images_ref, heights_ref, shadow_ref, dest_ref, sun_ref, shot_dest_ref, pixel_ref, shot_height_ref,
     out_ref, split_ref, extra_ref, halves_ref,
 ):
     step = pl.program_id(0)
@@ -167,10 +166,17 @@
         split_ref[DEVICES:] = odd
         first = around_pieces(even, odd)
         lit = jnp.concatenate([lit_even, lit_odd], axis=1).astype(BF16)
-        table = table_ref[...].astype(BF16)
+        sun = sun_ref[...].astype(F32)
+        dest = dest_ref[...].astype(F32)
+        table = [
+            jnp.concatenate([dest, jnp.zeros_like(dest)], axis=1),
+            jnp.concatenate([sun[0:1], sun[1:2]], axis=1),
+            jnp.concatenate([sun[2:3], sun[3:4]], axis=1),
+        ]
         second = [lit[:, j * LANES : j * LANES + LANES] for j in range(4)]
-        second += [jnp.broadcast_to(table[j : j + 1], (DEVICES, LANES)) for j in range(3)]
-        second += [shot_rows(shots_ref[...])] + [jnp.zeros((DEVICES, LANES), BF16)] * 8
+        second += [jnp.broadcast_to(item, (DEVICES, LANES)).astype(BF16) for item in table]
+        shots = (shot_dest_ref[...].astype(F32), pixel_ref[...].astype(F32), shot_height_ref[...])
+        second += [shot_rows(*shots)] + [jnp.zeros((DEVICES, LANES), BF16)] * 8
         for group in range(DEVICES // 16):
             span = slice(group * 16, group * 16 + 16)
             extra_ref[span, 0:16] = swapped(swap, [item[span] for item in first])
@@ -183,7 +189,7 @@
     out_ref[:, pixel_rows : pixel_rows + EXTRA, :] = extra_ref[here, 0:EXTRA, :]
 
 
-def pack(images, heights, shadow, table, shots):
+def pack(images, heights, shadow, *small):
     per_step = PACK_ROWS // 2
     count = PARTS[0][1]
     rows = QUARTERS * count + EXTRA
@@ -195,9 +201,8 @@
             pl.BlockSpec((count, PACK_ROWS, TILE), lambda s: (0, s, 0)),
             pl.BlockSpec((TILE, TILE), whole),
             pl.BlockSpec((TILE, TILE), whole),
-            pl.BlockSpec((8, LANES), whole),
-            pl.BlockSpec((8, TILE), whole),
-        ],
+        ]
+        + [pl.BlockSpec(item.shape, whole) for item in small],
         out_specs=[
             pl.BlockSpec((per_step, rows, LANES), lambda s: (s, 0, 0)),
             pl.BlockSpec((TILE, TILE), whole),
@@ -211,7 +216,7 @@
             pltpu.VMEM((4, TILE, LANES), F32),
         ],
         compiler_params=pltpu.CompilerParams(vmem_limit_bytes=58 * 1024 * 1024),
-    )(images, heights, shadow, table, shots)
+    )(images, heights, shadow, *small)
 
 
 def pack_rest(images):
@@ -232,6 +237,7 @@
 
 
 SUM_SRC = (32, 64)
+STEPS = (DEVICES // 32, DEVICES // 64)
 WIDTH = 2 * SLAB + TILE
 
 
@@ -327,7 +333,7 @@
         reply_ref[span, 16:24, :] = swapped(short_swap, pieces[16:])
 
 
-def sum_images(part, meta_ref, pixels_ref, normal_ref, sums_ref, plain_ref, work):
+def sum_images(part, step, steps, meta_ref, pixels_ref, normal_ref, sums_ref, plain_ref, work):
     first_w, second_w, first_p, second_p = work
     count = PARTS[part][1]
     half_src = SUM_SRC[part] // 2
@@ -352,7 +358,7 @@
             half_angle = jnp.dot(pick[span], normal_ref[...], preferred_element_type=F32)
             gain = cols[span, 4:5]
             bend = jnp.tanh(half_angle)
-            refl = (jnp.log(1.0 - bend) - LOG_2) * (gain * (-1.0 / sharpness))
+            refl = (jnp.log2(1.0 - bend) - 1.0) * (gain * (-LOG_2 / sharpness))
             sigma = bend * (gain * 0.5) + gain * 0.5
             seen = jnp.concatenate(
                 [
@@ -369,7 +375,7 @@
     def back(w_ref, p_ref):
         sums_ref[...] += jnp.dot(p_ref[...], w_ref[...], preferred_element_type=F32)
 
-    @pl.when(pl.program_id(0) == 0)
+    @pl.when(step == 0)
     def start():
         second_w[...] = jnp.zeros_like(second_w)
         second_p[...] = jnp.zeros_like(second_p)
@@ -379,7 +385,7 @@
     back(first_w, first_p)
     front(1, second_w, second_p)
 
-    @pl.when(pl.program_id(0) == pl.num_programs(0) - 1)
+    @pl.when(step == steps - 1)
     def finish():
         back(second_w, second_p)
 
@@ -394,7 +400,9 @@
         plain_ref[...] = jnp.zeros_like(plain_ref)
         slab_normals(me_ref[0], around_ref, lit_ref, normal_ref, slopes_ref, rows_ref)
 
-    sum_images(0, meta_ref, pixels_ref, normal_ref, sums_ref, plain_ref, work)
+    sum_images(
+        0, pl.program_id(0), STEPS[0], meta_ref, pixels_ref, normal_ref, sums_ref, plain_ref, work
+    )
 
 
 def second_kernel(
@@ -407,7 +415,9 @@
         plain_ref[...] = plain_in[...]
         slab_normals(me_ref[0], around_ref, lit_ref, normal_ref, slopes_ref, rows_ref)
 
-    sum_images(1, meta_ref, pixels_ref, normal_ref, sums_ref, plain_ref, work)
+    sum_images(
+        1, pl.program_id(0), STEPS[1], meta_ref, pixels_ref, normal_ref, sums_ref, plain_ref, work
+    )
 
     @pl.when(pl.program_id(0) == pl.num_programs(0) - 1)
     def finish():
@@ -473,6 +483,65 @@
     )[0]
 
 
+def both_kernel(
+    me_ref, meta_ref, pixels_ref, meta_rest, pixels_rest, around_ref, lit_ref,
+    reply_ref, sums_ref, plain_ref, normal_ref, slopes_ref, rows_ref, *work,
+):
+    step = pl.program_id(0)
+
+    @pl.when(step == 0)
+    def start():
+        sums_ref[...] = jnp.zeros_like(sums_ref)
+        plain_ref[...] = jnp.zeros_like(plain_ref)
+        slab_normals(me_ref[0], around_ref, lit_ref, normal_ref, slopes_ref, rows_ref)
+
+    @pl.when(step < STEPS[0])
+    def first():
+        sum_images(
+            0, step, STEPS[0], meta_ref, pixels_ref, normal_ref, sums_ref, plain_ref, work[:4]
+        )
+
+    @pl.when(step >= STEPS[0])
+    def second():
+        later = step - STEPS[0]
+        sum_images(
+            1, later, STEPS[1], meta_rest, pixels_rest, normal_ref, sums_ref, plain_ref, work[4:]
+        )
+
+    @pl.when(step == STEPS[0] + STEPS[1] - 1)
+    def finish():
+        slab_reply(me_ref[0], lit_ref, slopes_ref, sums_ref, plain_ref, reply_ref)
+
+
+def both_sums(me, metas, pixels, around, lit):
+    places = (
+        lambda s: jnp.minimum(s, STEPS[0] - 1),
+        lambda s: jnp.maximum(s - STEPS[0], 0),
+    )
+    specs, scratch = [pl.BlockSpec(memory_space=pltpu.SMEM)], []
+    for part in range(2):
+        count, sources, place = PARTS[part][1], SUM_SRC[part], places[part]
+        rows = QUARTERS * count + (EXTRA if part == 0 else 0)
+        specs.append(pl.BlockSpec((8, sources * count), lambda s, place=place: (0, place(s))))
+        specs.append(
+            pl.BlockSpec((sources, rows, LANES), lambda s, place=place: (place(s), 0, 0))
+        )
+        scratch += [pltpu.VMEM((sources * count // 2, 2 * SLAB), BF16)] * 2
+        scratch += [pltpu.VMEM((3 * DEVICES, sources * count // 2), BF16)] * 2
+    return pl.pallas_call(
+        both_kernel,
+        grid=(STEPS[0] + STEPS[1],),
+        in_specs=specs + [kept((DEVICES, 16, LANES)), kept((DEVICES, SLAB))],
+        out_specs=kept((DEVICES, REPLY, LANES)),
+        out_shape=jax.ShapeDtypeStruct((DEVICES, REPLY, LANES), BF16),
+        scratch_shapes=[
+            pltpu.VMEM(shape, dtype) for shape, dtype in (SUMS, PLAIN, NORMALS, SLOPES, ROWS)
+        ]
+        + scratch,
+        compiler_params=pltpu.CompilerParams(vmem_limit_bytes=44 * 1024 * 1024),
+    )(me, metas[0], pixels[0], metas[1], pixels[1], around, lit)
+
+
 def owner_kernel(final, *refs):
     got_ref, surface_ref, hits_ref, height_ref, ends_ref, sides_ref = refs[:6]
     outs, (model_ref, misfit_ref, scalar_ref, mixed_ref) = refs[6:-4], refs[-4:]
@@ -577,12 +646,16 @@
 
 def body(heights, shadow, image_tiles, image_dest, sun_gain, shot_dest, shot_pixel, shot_height):
     me = (lax.axis_index("row") * N_COL + lax.axis_index("col")).astype(jnp.int32)[None]
-    dest = image_dest[:, 0].astype(F32)
-    table = jnp.concatenate([dest, jnp.zeros_like(dest), sun_gain.astype(F32).T.reshape(-1)])
-    table = jnp.pad(table.reshape(3, LANES), ((0, 5), (0, 0)))
-    shots = jnp.stack([shot_dest[:, 0].astype(F32), shot_pixel.astype(F32), shot_height])
-    shots = jnp.pad(shots, ((0, 5), (0, 0)))
-    packed, surface = pack(image_tiles, heights, shadow, table, shots)
+    packed, surface = pack(
+        image_tiles,
+        heights,
+        shadow,
+        image_dest.T,
+        sun_gain.T,
+        shot_dest.T,
+        shot_pixel[None, :],
+        shot_height[None, :],
+    )
     rims = edges(surface)
     pixels = (exchange(packed), exchange(pack_rest(image_tiles)))
     extra = pixels[0][:, QUARTERS * PARTS[0][1] :, :]
@@ -598,16 +671,12 @@
     around = extra[:, 0:16, :]
     slots = extra[:, 23, : SHOT_CAP * 5].reshape(DEVICES * SHOT_CAP, 5).astype(F32)
     hits, height_sum = shot_sums(slots)
-
-    def slab_pass(around):
-        begun = first_sums(me, metas[0], pixels[0], around, slab_lit)
-        return second_sums(me, metas[1], pixels[1], around, slab_lit, *begun)
-
-    got = exchange(slab_pass(around))
+    begun = first_sums(me, metas[0], pixels[0], around, slab_lit)
+    got = exchange(second_sums(me, metas[1], pixels[1], around, slab_lit, *begun))
     surface, around = owner_update(False, got, surface, hits, height_sum, rims)
     around = exchange(around)
     rims = edges(surface)
-    got = exchange(slab_pass(around))
+    got = exchange(both_sums(me, metas, pixels, around, slab_lit))
     return owner_update(True, got, surface, hits, height_sum, rims)[0]
 
 

time: 261 us -> 256 us (0.981)
  other arithmetic: 6.85 us -> 2.8 us
    pallas_call x4 -> x2, Pallas kernels: 52.3 us -> 25.6 us  [sum_call(): pl.pallas_call(kernel, grid=(DEVICES // sources,), in_specs=[pl.BlockSpec...]
    pallas_call x0 -> x1, Pallas kernels: none -> 26.1 us  [both_sums(): pl.pallas_call(both_kernel, grid=(STEPS[0] + STEPS[1],), in_specs=specs +...]
    unnamed x29 -> x27, local copies, waits for them, and re-layouts: 6.02 us -> 5.83 us
where the time goes in v4:
time: 256 us; the launch traced here: 252 us
  waiting for transfers between devices  92.6 us (36%)
  Pallas kernels  68 us (27%)
  starting transfers between devices  55.2 us (22%)
  blocking collectives  17.8 us (7%)
  local copies, waits for them, and re-layouts  14.7 us (6%)
  other arithmetic  2.8 us (1%)
    ppermute x4, waiting for transfers between devices, edges(): out.append(lax.ppermute(first, axis, down))  70.8 us
    all_to_all x4, starting transfers between devices, exchange(): return lax.all_to_all(value, AXES, split_axis=0, concat_axis=0, tiled=True)  33.3 us
    pallas_call x1, Pallas kernels, both_sums(): pl.pallas_call(both_kernel, grid=(STEPS[0] + STEPS[1],), in_specs=specs +...  26.1 us
    pallas_call x2, Pallas kernels, sum_call(): pl.pallas_call(kernel, grid=(DEVICES // sources,), in_specs=[pl.BlockSpec...  25.6 us
    all_to_all x4, waiting for transfers between devices, exchange(): return lax.all_to_all(value, AXES, split_axis=0, concat_axis=0, tiled=True)  21.8 us
    all_to_all x1, blocking collectives, exchange(): return lax.all_to_all(value, AXES, split_axis=0, concat_axis=0, tiled=True)  17.8 us
    ppermute x4, starting transfers between devices, edges(): out.append(lax.ppermute(last, axis, up))  13.2 us
    ppermute x4, starting transfers between devices, edges(): out.append(lax.ppermute(first, axis, down))  8.74 us
  transfers between devices with their start and end apart: 12, of which 6 were waited for; matrix products, arithmetic and copies ran while one was open for 5% of the time, Pallas kernels for 9%

profile of v4, /device:TPU:1, one launch (start us, length us, event | category | flops | bytes accessed | tf_op | source)
XLA Modules:
  0.0 252.0 jit_solution(11612023394789786118)
XLA Ops:
  0.0 8.7 %shard_map.82 = (bf16[128,216,128]{2,1,0:T(8,128)(2,1)}, f32[256,256]{1,0:T(8,128)}) custom-call(bf16[64,256,256]{2,1,0:T(8,128)(2,1)} %images_ref.3, f32[256,256]{1,0:T(8,128)} %heights_ref.1, s32[256,256]{1,0:T(8,128)} %shadow_ref.1, s32[1,64]{1,0:T(1,128)} %bitcast.18, bf16[4,64]{1,0:T(4,128)(2,1)} %bitcast.14, s32[1,256]{1,0:T(1,128)} %bitcast.15, ...), custom_call_target="tpu_custom_call" | custom-call | tf_op jit(solution)/shard_map/pallas_call | solution.py:197
  8.7 11.9 %all-to-all-start = ((bf16[128,216,128]{2,1,0:T(8,128)(2,1)}), bf16[128,216,128]{2,1,0:T(8,128)(2,1)}, u32[]{:S(2)}, u32[]{:S(2)}) async-start(bf16[128,216,128]{2,1,0:T(8,128)(2,1)} %get-tuple-element.11), calls=%async_computation | async-start | bytes 14155776 | tf_op jit(solution)/shard_map/all_to_all | solution.py:33
  20.6 3.0 %collective-permute-start.1 = (f32[1,256]{1,0:T(1,128)S(1)}, f32[1,256]{1,0:T(1,128)S(1)}, u32[]{:S(2)}, u32[]{:S(2)}) collective-permute-start(f32[1,256]{1,0:T(1,128)S(1)} %get-tuple-element.41), channel_id=1, source_target_pairs={{16,0},{32,16},{48,32},{64,48},{80,64},{96,80},{112,96},{17,1},{33... | collective-permute-start | bytes 3080 | tf_op jit(solution)/shard_map/ppermute | solution.py:45
  23.6 2.5 %collective-permute-start = (f32[1,256]{1,0:T(1,128)S(1)}, f32[1,256]{1,0:T(1,128)S(1)}, u32[]{:S(2)}, u32[]{:S(2)}) collective-permute-start(f32[1,256]{1,0:T(1,128)S(1)} %get-tuple-element.40), channel_id=1, source_target_pairs={{0,16},{16,32},{32,48},{48,64},{64,80},{80,96},{96,112},{1,17},{17... | collective-permute-start | bytes 3080 | tf_op jit(solution)/shard_map/ppermute | solution.py:44
  26.2 0.1 fusion.22
  26.3 1.3 collective-permute-start.3
  27.6 4.0 %collective-permute-start.2 = (f32[256,1]{1,0:T(8,128)S(1)}, f32[256,1]{1,0:T(8,128)S(1)}, u32[]{:S(2)}, u32[]{:S(2)}) collective-permute-start(f32[256,1]{1,0:T(8,128)S(1)} %get-tuple-element.38), channel_id=1, source_target_pairs={{0,1},{1,2},{2,3},{3,4},{4,5},{5,6},{6,7},{7,8},{8,9},{9,10},{10,1... | collective-permute-start | bytes 3080 | tf_op jit(solution)/shard_map/ppermute | solution.py:44
  31.6 4.3 %shard_map.83 = bf16[128,64,128]{2,1,0:T(8,128)(2,1)} custom-call(bf16[64,256,256]{2,1,0:T(8,128)(2,1)} %images_ref.3), custom_call_target="tpu_custom_call" | custom-call | flops 536870912 | bytes 4194304 | tf_op jit(solution)/shard_map/pallas_call | solution.py:226
  36.0 66.3 %collective-permute-done.1 = f32[1,256]{1,0:T(1,128)S(1)} collective-permute-done((f32[1,256]{1,0:T(1,128)S(1)}, f32[1,256]{1,0:T(1,128)S(1)}, u32[]{:S(2)}, u32[]{:S(2)}) %collective-permute-start.1) | collective-permute-done | bytes 1056 | tf_op jit(solution)/shard_map/ppermute | solution.py:45
  102.3 0.0 collective-permute-done
  102.3 0.0 collective-permute-done.3
  102.3 0.0 collective-permute-done.2
  102.3 0.1 pad_maximum_fusion.refs_5_
  102.4 7.1 %all-to-all-done.pixels_ref = bf16[128,216,128]{2,1,0:T(8,128)(2,1)} async-done(((bf16[128,216,128]{2,1,0:T(8,128)(2,1)}), bf16[128,216,128]{2,1,0:T(8,128)(2,1)}, u32[]{:S(2)}, u32[]{:S(2)}) %all-to-all-start) | async-done | bytes 7077920 | tf_op jit(solution)/shard_map/all_to_all | solution.py:33
  109.5 7.8 %all-to-all-start.1 = ((bf16[128,64,128]{2,1,0:T(8,128)(2,1)}), bf16[128,64,128]{2,1,0:T(8,128)(2,1)S(1)}, u32[]{:S(2)}, u32[]{:S(2)}) async-start(bf16[128,64,128]{2,1,0:T(8,128)(2,1)} %shard_map.83), calls=%async_computation.1 | async-start | bytes 4194304 | tf_op jit(solution)/shard_map/all_to_all | solution.py:33
  117.3 2.7 %slice_reduce_fusion.10 = (bf16[128,48]{1,0:T(8,128)(2,1)S(1)}, bf16[128,48]{1,0:T(8,128)(2,1)S(1)}, bf16[128,48]{1,0:T(8,128)(2,1)S(1)}, bf16[128,48]{1,0:T(8,128)(2,1)S(1)}, bf16[128,48]{1,0:T(8,128)(2,1)S(1)}) fusion(bf16[128,216,128]{2,1,0:T(8,128)(2,1)} %all-to-all-done.pixels_ref), kind=kLoop, calls=%fused_computation.38 | loop fusion | bytes 122880 | tf_op jit(solution)/shard_map/slice | solution.py:665
  120.0 2.8 %slice_reduce_fusion.5 = (bf16[128,16]{1,0:T(8,128)(2,1)S(1)}, bf16[128,16]{1,0:T(8,128)(2,1)S(1)}, bf16[128,16]{1,0:T(8,128)(2,1)S(1)}, bf16[128,16]{1,0:T(8,128)(2,1)S(1)}, bf16[128,16]{1,0:T(8,128)(2,1)S(1)}) fusion(bf16[128,216,128]{2,1,0:T(8,128)(2,1)} %all-to-all-done.pixels_ref), kind=kLoop, calls=%fused_computation.33 | loop fusion | bytes 40960 | tf_op jit(solution)/shard_map/slice | solution.py:665
  122.8 0.1 stack.26
  122.9 0.1 stack.27
  123.0 0.1 stack.28
  123.1 0.1 stack.29
  123.2 0.1 stack.30
  123.3 0.1 stack.32
  123.4 0.1 stack.33
  123.5 0.1 stack.34
  123.6 0.1 stack.35
  123.7 0.1 stack.36
  123.8 1.0 slice_convert_fusion
  124.8 0.2 stack.31
  125.0 0.1 stack.37
  125.1 1.1 slice.141.around_ref
  126.2 18.2 %shard_map.84 = (f32[384,1024]{1,0:T(8,128)S(1)}, f32[8,1024]{1,0:T(8,128)S(1)}) custom-call(s32[1]{0:T(128)} %bitcast.me_ref, f32[8,6144]{1,0:T(8,128)S(1)} %pad_convert_fusion.meta_ref, bf16[128,216,128]{2,1,0:T(8,128)(2,1)} %all-to-all-done.pixels_ref, bf16[128,16,128]{2,1,0:T(8,128)(2,1)S(1)} %slice.141.around_ref, f32[128,512]{1,0:T(8,128)S(1)} %bitcast.10), custom_call_target="tpu_custom_call" | custom-call | flops 9663676416 | bytes 12582912 | tf_op jit(solution)/shard_map/pallas_call | solution.py:443
  144.5 0.7 copy-done.7
  145.2 1.2 copy-done.11
  146.3 0.4 all-to-all-done.1.pixels_ref.pixels_rest
  146.8 1.4 copy-done.12
  148.2 7.4 %shard_map.85 = bf16[128,24,128]{2,1,0:T(8,128)(2,1)S(1)} custom-call(s32[1]{0:T(128)} %bitcast.me_ref, f32[8,2048]{1,0:T(8,128)S(1)} %pad_convert_fusion.1.meta_ref.meta_rest, bf16[128,64,128]{2,1,0:T(8,128)(2,1)S(1)} %all-to-all-done.1.pixels_ref.pixels_rest, bf16[128,16,128]{2,1,0:T(8,128)(2,1)S(1)} %slice.141.around_ref, f32[128,512]{1,0:T(8,128)S(1)} %bitcast.11, ...), custom_call_target="tpu_custom_call" | custom-call | flops 3221225472 | bytes 4194304 | tf_op jit(solution)/shard_map/pallas_call | solution.py:443
  155.6 0.9 copy-done.6
  156.4 9.4 %all-to-all-start.2 = ((bf16[128,24,128]{2,1,0:T(8,128)(2,1)}), bf16[128,24,128]{2,1,0:T(8,128)(2,1)S(1)}, u32[]{:S(2)}, u32[]{:S(2)}) async-start(bf16[128,24,128]{2,1,0:T(8,128)(2,1)} %copy-done.6), calls=%async_computation.2 | async-start | bytes 1572864 | tf_op jit(solution)/shard_map/all_to_all | solution.py:33
  165.8 1.2 fusion.16
  167.0 0.1 reshape.33
  167.1 0.7 slice_reduce_fusion
  167.8 0.3 fusion.7
  168.2 0.5 fusion
  168.7 0.1 slice_add_fusion
  168.7 13.5 %all-to-all-done.2.refs_0_ = bf16[128,24,128]{2,1,0:T(8,128)(2,1)S(1)} async-done(((bf16[128,24,128]{2,1,0:T(8,128)(2,1)}), bf16[128,24,128]{2,1,0:T(8,128)(2,1)S(1)}, u32[]{:S(2)}, u32[]{:S(2)}) %all-to-all-start.2) | async-done | bytes 786464 | tf_op jit(solution)/shard_map/all_to_all | solution.py:33
  182.3 0.9 copy-done.3
  183.2 1.6 shard_map.86
  184.8 0.0 copy-start
  184.8 0.7 copy-done
  185.5 17.8 %all_to_all.25.around_ref = bf16[128,16,128]{2,1,0:T(8,128)(2,1)S(1)} all-to-all(bf16[128,16,128]{2,1,0:T(8,128)(2,1)S(1)} %get-tuple-element.15), channel_id=1, replica_groups=mesh['row'=8,'col'=16] {'row','col'}, dimensions={0} | all-to-all | bytes 1048576 | tf_op jit(solution)/shard_map/all_to_all | solution.py:33
  203.3 0.0 copy-start.1
  203.3 26.1 %shard_map.87 = bf16[128,24,128]{2,1,0:T(8,128)(2,1)} custom-call(s32[1]{0:T(128)} %bitcast.me_ref, f32[8,6144]{1,0:T(8,128)S(1)} %copy-done.8, bf16[128,216,128]{2,1,0:T(8,128)(2,1)} %all-to-all-done.pixels_ref, f32[8,2048]{1,0:T(8,128)S(1)} %copy-done.10, bf16[128,64,128]{2,1,0:T(8,128)(2,1)S(1)} %all-to-all-done.1.pixels_ref.pixels_rest, ...), custom_call_target="tpu_custom_call" | custom-call | tf_op jit(solution)/shard_map/pallas_call | solution.py:531
  229.3 4.2 %all-to-all-start.4 = ((bf16[128,24,128]{2,1,0:T(8,128)(2,1)}), bf16[128,24,128]{2,1,0:T(8,128)(2,1)S(1)}, u32[]{:S(2)}, u32[]{:S(2)}) async-start(bf16[128,24,128]{2,1,0:T(8,128)(2,1)} %shard_map.87), calls=%async_computation.4 | async-start | bytes 1572864 | tf_op jit(solution)/shard_map/all_to_all | solution.py:33
  233.6 3.1 %collective-permute-start.5 = (f32[1,256]{1,0:T(1,128)S(1)}, f32[1,256]{1,0:T(1,128)S(1)}, u32[]{:S(2)}, u32[]{:S(2)}) collective-permute-start(f32[1,256]{1,0:T(1,128)S(1)} %get-tuple-element.37), channel_id=1, source_target_pairs={{16,0},{32,16},{48,32},{64,48},{80,64},{96,80},{112,96},{17,1},{33... | collective-permute-start | bytes 3080 | tf_op jit(solution)/shard_map/ppermute | solution.py:45
  236.7 2.4 collective-permute-start.4
  239.2 0.1 fusion.20
  239.3 1.3 collective-permute-start.7
  240.6 4.2 %collective-permute-start.6 = (f32[256,1]{1,0:T(8,128)S(1)}, f32[256,1]{1,0:T(8,128)S(1)}, u32[]{:S(2)}, u32[]{:S(2)}) collective-permute-start(f32[256,1]{1,0:T(8,128)S(1)} %get-tuple-element.34), channel_id=1, source_target_pairs={{0,1},{1,2},{2,3},{3,4},{4,5},{5,6},{6,7},{7,8},{8,9},{9,10},{10,1... | collective-permute-start | bytes 3080 | tf_op jit(solution)/shard_map/ppermute | solution.py:44
  244.8 0.0 collective-permute-done.5
  244.8 4.5 %collective-permute-done.7 = f32[256,1]{1,0:T(8,128)S(1)} collective-permute-done((f32[256,1]{1,0:T(8,128)S(1)}, f32[256,1]{1,0:T(8,128)S(1)}, u32[]{:S(2)}, u32[]{:S(2)}) %collective-permute-start.7) | collective-permute-done | bytes 1056 | tf_op jit(solution)/shard_map/ppermute | solution.py:45
  249.3 0.1 pad_maximum_fusion.1.refs_5_
  249.4 0.8 all-to-all-done.4.refs_0_
  250.2 1.8 shard_map.88
  (28 shorter events, 0.1 us)
Async XLA Ops:
  8.7 11.9 %copy-start.2 = (f32[256,256]{1,0:T(8,128)S(1)}, f32[256,256]{1,0:T(8,128)}, u32[]{:S(2)}) copy-start(f32[256,256]{1,0:T(8,128)} %get-tuple-element.14.refs_1_) | copy-start | bytes 786436
  8.7 100.8 %all-to-all-start = ((bf16[128,216,128]{2,1,0:T(8,128)(2,1)}), bf16[128,216,128]{2,1,0:T(8,128)(2,1)}, u32[]{:S(2)}, u32[]{:S(2)}) async-start(bf16[128,216,128]{2,1,0:T(8,128)(2,1)} %get-tuple-element.11), calls=%async_computation | async-start | bytes 14155776 | tf_op jit(solution)/shard_map/all_to_all | solution.py:33
  20.6 81.7 %collective-permute-start.1 = (f32[1,256]{1,0:T(1,128)S(1)}, f32[1,256]{1,0:T(1,128)S(1)}, u32[]{:S(2)}, u32[]{:S(2)}) collective-permute-start(f32[1,256]{1,0:T(1,128)S(1)} %get-tuple-element.41), channel_id=1, source_target_pairs={{16,0},{32,16},{48,32},{64,48},{80,64},{96,80},{112,96},{17,1},{33... | collective-permute-start | bytes 3080 | tf_op jit(solution)/shard_map/ppermute | solution.py:45
  23.6 78.6 %collective-permute-start = (f32[1,256]{1,0:T(1,128)S(1)}, f32[1,256]{1,0:T(1,128)S(1)}, u32[]{:S(2)}, u32[]{:S(2)}) collective-permute-start(f32[1,256]{1,0:T(1,128)S(1)} %get-tuple-element.40), channel_id=1, source_target_pairs={{0,16},{16,32},{32,48},{48,64},{64,80},{80,96},{96,112},{1,17},{17... | collective-permute-start | bytes 3080 | tf_op jit(solution)/shard_map/ppermute | solution.py:44
  26.3 76.0 %collective-permute-start.3 = (f32[256,1]{1,0:T(8,128)S(1)}, f32[256,1]{1,0:T(8,128)S(1)}, u32[]{:S(2)}, u32[]{:S(2)}) collective-permute-start(f32[256,1]{1,0:T(8,128)S(1)} %get-tuple-element.39), channel_id=1, source_target_pairs={{1,0},{2,1},{3,2},{4,3},{5,4},{6,5},{7,6},{8,7},{9,8},{10,9},{11,1... | collective-permute-start | bytes 3080 | tf_op jit(solution)/shard_map/ppermute | solution.py:45
  27.6 74.7 %collective-permute-start.2 = (f32[256,1]{1,0:T(8,128)S(1)}, f32[256,1]{1,0:T(8,128)S(1)}, u32[]{:S(2)}, u32[]{:S(2)}) collective-permute-start(f32[256,1]{1,0:T(8,128)S(1)} %get-tuple-element.38), channel_id=1, source_target_pairs={{0,1},{1,2},{2,3},{3,4},{4,5},{5,6},{6,7},{7,8},{8,9},{9,10},{10,1... | collective-permute-start | bytes 3080 | tf_op jit(solution)/shard_map/ppermute | solution.py:44
  109.5 37.3 %all-to-all-start.1 = ((bf16[128,64,128]{2,1,0:T(8,128)(2,1)}), bf16[128,64,128]{2,1,0:T(8,128)(2,1)S(1)}, u32[]{:S(2)}, u32[]{:S(2)}) async-start(bf16[128,64,128]{2,1,0:T(8,128)(2,1)} %shard_map.83), calls=%async_computation.1 | async-start | bytes 4194304 | tf_op jit(solution)/shard_map/all_to_all | solution.py:33
  124.8 22.0 %copy-start.4 = (f32[16,8,4,128]{3,1,2,0:T(8,128)}, f32[16,8,4,128]{3,1,2,0:T(8,128)S(1)}, u32[]{:S(2)}) copy-start(f32[16,8,4,128]{3,1,2,0:T(8,128)S(1)} %copy.17) | copy-start | bytes 786436
  126.2 20.6 %copy-start.9 = (f32[8,2048]{1,0:T(8,128)}, f32[8,2048]{1,0:T(8,128)S(1)}, u32[]{:S(2)}) copy-start(f32[8,2048]{1,0:T(8,128)S(1)} %pad_convert_fusion.1.meta_ref.meta_rest) | copy-start | bytes 196612
  144.5 0.7 copy-start.7
  145.2 1.2 copy-start.11
  146.8 1.4 copy-start.12
  155.5 0.9 copy-start.6
  156.4 25.8 %all-to-all-start.2 = ((bf16[128,24,128]{2,1,0:T(8,128)(2,1)}), bf16[128,24,128]{2,1,0:T(8,128)(2,1)S(1)}, u32[]{:S(2)}, u32[]{:S(2)}) async-start(bf16[128,24,128]{2,1,0:T(8,128)(2,1)} %copy-done.6), calls=%async_computation.2 | async-start | bytes 1572864 | tf_op jit(solution)/shard_map/all_to_all | solution.py:33
  182.3 1.0 copy-start.3
  183.2 20.0 %copy-start.5 = (f32[16,8,4,128]{3,1,2,0:T(8,128)S(1)}, f32[16,8,4,128]{3,1,2,0:T(8,128)}, u32[]{:S(2)}) copy-start(f32[16,8,4,128]{3,1,2,0:T(8,128)} %copy-done.4) | copy-start | bytes 786436
  183.2 20.0 %copy-start.8 = (f32[8,6144]{1,0:T(8,128)S(1)}, f32[8,6144]{1,0:T(8,128)}, u32[]{:S(2)}) copy-start(f32[8,6144]{1,0:T(8,128)} %copy-done.7) | copy-start | bytes 589828
  183.2 20.0 %copy-start.10 = (f32[8,2048]{1,0:T(8,128)S(1)}, f32[8,2048]{1,0:T(8,128)}, u32[]{:S(2)}) copy-start(f32[8,2048]{1,0:T(8,128)} %copy-done.9) | copy-start | bytes 196612
  184.8 0.7 copy-start
  203.3 30.3 %copy-start.1 = (f32[256,256]{1,0:T(8,128)S(1)}, f32[256,256]{1,0:T(8,128)}, u32[]{:S(2)}) copy-start(f32[256,256]{1,0:T(8,128)} %copy-done) | copy-start | bytes 786436
  229.3 20.8 %all-to-all-start.4 = ((bf16[128,24,128]{2,1,0:T(8,128)(2,1)}), bf16[128,24,128]{2,1,0:T(8,128)(2,1)S(1)}, u32[]{:S(2)}, u32[]{:S(2)}) async-start(bf16[128,24,128]{2,1,0:T(8,128)(2,1)} %shard_map.87), calls=%async_computation.4 | async-start | bytes 1572864 | tf_op jit(solution)/shard_map/all_to_all | solution.py:33
  233.6 11.2 %collective-permute-start.5 = (f32[1,256]{1,0:T(1,128)S(1)}, f32[1,256]{1,0:T(1,128)S(1)}, u32[]{:S(2)}, u32[]{:S(2)}) collective-permute-start(f32[1,256]{1,0:T(1,128)S(1)} %get-tuple-element.37), channel_id=1, source_target_pairs={{16,0},{32,16},{48,32},{64,48},{80,64},{96,80},{112,96},{17,1},{33... | collective-permute-start | bytes 3080 | tf_op jit(solution)/shard_map/ppermute | solution.py:45
  236.7 8.1 %collective-permute-start.4 = (f32[1,256]{1,0:T(1,128)S(1)}, f32[1,256]{1,0:T(1,128)S(1)}, u32[]{:S(2)}, u32[]{:S(2)}) collective-permute-start(f32[1,256]{1,0:T(1,128)S(1)} %get-tuple-element.36), channel_id=1, source_target_pairs={{0,16},{16,32},{32,48},{48,64},{64,80},{80,96},{96,112},{1,17},{17... | collective-permute-start | bytes 3080 | tf_op jit(solution)/shard_map/ppermute | solution.py:44
  239.3 10.0 %collective-permute-start.7 = (f32[256,1]{1,0:T(8,128)S(1)}, f32[256,1]{1,0:T(8,128)S(1)}, u32[]{:S(2)}, u32[]{:S(2)}) collective-permute-start(f32[256,1]{1,0:T(8,128)S(1)} %get-tuple-element.35), channel_id=1, source_target_pairs={{1,0},{2,1},{3,2},{4,3},{5,4},{6,5},{7,6},{8,7},{9,8},{10,9},{11,1... | collective-permute-start | bytes 3080 | tf_op jit(solution)/shard_map/ppermute | solution.py:45
  240.6 8.7 %collective-permute-start.6 = (f32[256,1]{1,0:T(8,128)S(1)}, f32[256,1]{1,0:T(8,128)S(1)}, u32[]{:S(2)}, u32[]{:S(2)}) collective-permute-start(f32[256,1]{1,0:T(8,128)S(1)} %get-tuple-element.34), channel_id=1, source_target_pairs={{0,1},{1,2},{2,3},{3,4},{4,5},{5,6},{6,7},{7,8},{8,9},{9,10},{10,1... | collective-permute-start | bytes 3080 | tf_op jit(solution)/shard_map/ppermute | solution.py:44

commit v5 on v4

--- a/solution.py
+++ b/solution.py
@@ -676,6 +676,8 @@
     surface, around = owner_update(False, got, surface, hits, height_sum, rims)
     around = exchange(around)
     rims = edges(surface)
+    around, above, below = lax.optimization_barrier((around, rims[0], rims[1]))
+    rims = [above, below] + rims[2:]
     got = exchange(both_sums(me, metas, pixels, around, slab_lit))
     return owner_update(True, got, surface, hits, height_sum, rims)[0]
 

time: 256 us -> 257 us (level); the launches traced: 252 us -> 256 us
  blocking collectives: 17.8 us -> 0 us
  waiting for transfers between devices: 92.6 us -> 106 us
  starting transfers between devices: 55.2 us -> 59.7 us
  local copies, waits for them, and re-layouts: 14.7 us -> 18.9 us
    all_to_all x1 -> x0, blocking collectives: 17.8 us -> none  [exchange(): return lax.all_to_all(value, AXES, split_axis=0, concat_axis=0, tiled=True)]
    ppermute x4, waiting for transfers between devices: 70.8 us -> 78.5 us  [edges(): out.append(lax.ppermute(first, axis, down))]
    all_to_all x4 -> x5, waiting for transfers between devices: 21.8 us -> 27.4 us  [exchange(): return lax.all_to_all(value, AXES, split_axis=0, concat_axis=0, tiled=True)]
    all_to_all x4 -> x5, starting transfers between devices: 33.3 us -> 37.8 us  [exchange(): return lax.all_to_all(value, AXES, split_axis=0, concat_axis=0, tiled=True)]
    unnamed x27 -> x29, local copies, waits for them, and re-layouts: 5.83 us -> 9.33 us
  transfers between devices with their start and end apart: 12 -> 13, of which waited for: 6 -> 8; matrix products, arithmetic and copies ran while one was open for 5% -> 5% of each run, Pallas kernels for 9% -> 9%
where the time goes in v5:
time: 257 us; the launch traced here: 256 us
  waiting for transfers between devices  106 us (41%)
  Pallas kernels  67.9 us (26%)
  starting transfers between devices  59.7 us (23%)
  local copies, waits for them, and re-layouts  18.9 us (7%)
  other arithmetic  2.8 us (1%)
    ppermute x4, waiting for transfers between devices, edges(): out.append(lax.ppermute(first, axis, down))  78.5 us
    all_to_all x5, starting transfers between devices, exchange(): return lax.all_to_all(value, AXES, split_axis=0, concat_axis=0, tiled=True)  37.8 us
    all_to_all x5, waiting for transfers between devices, exchange(): return lax.all_to_all(value, AXES, split_axis=0, concat_axis=0, tiled=True)  27.4 us
    pallas_call x1, Pallas kernels, both_sums(): pl.pallas_call(both_kernel, grid=(STEPS[0] + STEPS[1],), in_specs=specs +...  26 us
    pallas_call x2, Pallas kernels, sum_call(): pl.pallas_call(kernel, grid=(DEVICES // sources,), in_specs=[pl.BlockSpec...  25.5 us
    ppermute x4, starting transfers between devices, edges(): out.append(lax.ppermute(last, axis, up))  14.2 us
    unnamed x29, local copies, waits for them, and re-layouts  9.33 us
    pallas_call x1, Pallas kernels, pack(): pl.pallas_call(pack_kernel, grid=(DEVICES // per_step,), in_specs=[pl.Blo...  8.66 us
  transfers between devices with their start and end apart: 13, of which 8 were waited for; matrix products, arithmetic and copies ran while one was open for 5% of the time, Pallas kernels for 9%

profile of v5, /device:TPU:1, one launch (start us, length us, event | category | flops | bytes accessed | tf_op | source)
XLA Modules:
  0.0 256.0 jit_solution(10736889588061444600)
XLA Ops:
  0.0 8.7 %shard_map.82 = (bf16[128,216,128]{2,1,0:T(8,128)(2,1)}, f32[256,256]{1,0:T(8,128)}) custom-call(bf16[64,256,256]{2,1,0:T(8,128)(2,1)} %images_ref.3, f32[256,256]{1,0:T(8,128)} %heights_ref.1, s32[256,256]{1,0:T(8,128)} %shadow_ref.1, s32[1,64]{1,0:T(1,128)} %bitcast.18, bf16[4,64]{1,0:T(4,128)(2,1)} %bitcast.14, s32[1,256]{1,0:T(1,128)} %bitcast.15, ...), custom_call_target="tpu_custom_call" | custom-call | tf_op jit(solution)/shard_map/pallas_call | solution.py:197
  8.7 11.9 %all-to-all-start = ((bf16[128,216,128]{2,1,0:T(8,128)(2,1)}), bf16[128,216,128]{2,1,0:T(8,128)(2,1)}, u32[]{:S(2)}, u32[]{:S(2)}) async-start(bf16[128,216,128]{2,1,0:T(8,128)(2,1)} %get-tuple-element.14), calls=%async_computation | async-start | bytes 14155776 | tf_op jit(solution)/shard_map/all_to_all | solution.py:33
  20.6 3.0 %collective-permute-start.1 = (f32[1,256]{1,0:T(1,128)S(1)}, f32[1,256]{1,0:T(1,128)S(1)}, u32[]{:S(2)}, u32[]{:S(2)}) collective-permute-start(f32[1,256]{1,0:T(1,128)S(1)} %get-tuple-element.47), channel_id=1, source_target_pairs={{16,0},{32,16},{48,32},{64,48},{80,64},{96,80},{112,96},{17,1},{33... | collective-permute-start | bytes 3080 | tf_op jit(solution)/shard_map/ppermute | solution.py:45
  23.6 2.5 collective-permute-start
  26.2 0.1 fusion.22
  26.3 1.3 collective-permute-start.3
  27.6 4.0 %collective-permute-start.2 = (f32[256,1]{1,0:T(8,128)S(1)}, f32[256,1]{1,0:T(8,128)S(1)}, u32[]{:S(2)}, u32[]{:S(2)}) collective-permute-start(f32[256,1]{1,0:T(8,128)S(1)} %get-tuple-element.44), channel_id=1, source_target_pairs={{0,1},{1,2},{2,3},{3,4},{4,5},{5,6},{6,7},{7,8},{8,9},{9,10},{10,1... | collective-permute-start | bytes 3080 | tf_op jit(solution)/shard_map/ppermute | solution.py:44
  31.6 4.3 %shard_map.83 = bf16[128,64,128]{2,1,0:T(8,128)(2,1)} custom-call(bf16[64,256,256]{2,1,0:T(8,128)(2,1)} %images_ref.3), custom_call_target="tpu_custom_call" | custom-call | flops 536870912 | bytes 4194304 | tf_op jit(solution)/shard_map/pallas_call | solution.py:226
  36.0 66.3 %collective-permute-done.1 = f32[1,256]{1,0:T(1,128)S(1)} collective-permute-done((f32[1,256]{1,0:T(1,128)S(1)}, f32[1,256]{1,0:T(1,128)S(1)}, u32[]{:S(2)}, u32[]{:S(2)}) %collective-permute-start.1) | collective-permute-done | bytes 1056 | tf_op jit(solution)/shard_map/ppermute | solution.py:45
  102.3 0.1 pad_maximum_fusion.refs_5_
  102.4 7.1 %all-to-all-done.pixels_ref = bf16[128,216,128]{2,1,0:T(8,128)(2,1)} async-done(((bf16[128,216,128]{2,1,0:T(8,128)(2,1)}), bf16[128,216,128]{2,1,0:T(8,128)(2,1)}, u32[]{:S(2)}, u32[]{:S(2)}) %all-to-all-start) | async-done | bytes 7077920 | tf_op jit(solution)/shard_map/all_to_all | solution.py:33
  109.5 7.8 %all-to-all-start.1 = ((bf16[128,64,128]{2,1,0:T(8,128)(2,1)}), bf16[128,64,128]{2,1,0:T(8,128)(2,1)S(1)}, u32[]{:S(2)}, u32[]{:S(2)}) async-start(bf16[128,64,128]{2,1,0:T(8,128)(2,1)} %shard_map.83), calls=%async_computation.1 | async-start | bytes 4194304 | tf_op jit(solution)/shard_map/all_to_all | solution.py:33
  117.3 2.7 %slice_reduce_fusion.10 = (bf16[128,48]{1,0:T(8,128)(2,1)S(1)}, bf16[128,48]{1,0:T(8,128)(2,1)S(1)}, bf16[128,48]{1,0:T(8,128)(2,1)S(1)}, bf16[128,48]{1,0:T(8,128)(2,1)S(1)}, bf16[128,48]{1,0:T(8,128)(2,1)S(1)}) fusion(bf16[128,216,128]{2,1,0:T(8,128)(2,1)} %all-to-all-done.pixels_ref), kind=kLoop, calls=%fused_computation.38 | loop fusion | bytes 122880 | tf_op jit(solution)/shard_map/slice | solution.py:665
  120.0 2.8 %slice_reduce_fusion.5 = (bf16[128,16]{1,0:T(8,128)(2,1)S(1)}, bf16[128,16]{1,0:T(8,128)(2,1)S(1)}, bf16[128,16]{1,0:T(8,128)(2,1)S(1)}, bf16[128,16]{1,0:T(8,128)(2,1)S(1)}, bf16[128,16]{1,0:T(8,128)(2,1)S(1)}) fusion(bf16[128,216,128]{2,1,0:T(8,128)(2,1)} %all-to-all-done.pixels_ref), kind=kLoop, calls=%fused_computation.33 | loop fusion | bytes 40960 | tf_op jit(solution)/shard_map/slice | solution.py:665
  122.8 0.1 stack.26
  122.9 0.1 stack.27
  123.0 0.1 stack.28
  123.1 0.1 stack.29
  123.2 0.1 stack.30
  123.3 0.1 stack.32
  123.4 0.1 stack.33
  123.5 0.1 stack.34
  123.6 0.1 stack.35
  123.7 0.1 stack.36
  123.8 1.0 slice_convert_fusion
  124.8 0.2 stack.31
  125.0 0.1 stack.37
  125.1 1.1 slice.141.around_ref
  126.2 18.2 %shard_map.84 = (f32[384,1024]{1,0:T(8,128)S(1)}, f32[8,1024]{1,0:T(8,128)S(1)}) custom-call(s32[1]{0:T(128)} %bitcast.me_ref, f32[8,6144]{1,0:T(8,128)S(1)} %pad_convert_fusion.meta_ref, bf16[128,216,128]{2,1,0:T(8,128)(2,1)} %all-to-all-done.pixels_ref, bf16[128,16,128]{2,1,0:T(8,128)(2,1)S(1)} %slice.141.around_ref, f32[128,512]{1,0:T(8,128)S(1)} %bitcast.10), custom_call_target="tpu_custom_call" | custom-call | flops 9663676416 | bytes 12582912 | tf_op jit(solution)/shard_map/pallas_call | solution.py:443
  144.5 0.7 copy-done.7
  145.2 1.2 copy-done.12
  146.3 0.4 all-to-all-done.1.pixels_ref.pixels_rest
  146.8 1.4 copy-done.13
  148.2 7.3 %shard_map.85 = bf16[128,24,128]{2,1,0:T(8,128)(2,1)S(1)} custom-call(s32[1]{0:T(128)} %bitcast.me_ref, f32[8,2048]{1,0:T(8,128)S(1)} %pad_convert_fusion.1.meta_ref.meta_rest, bf16[128,64,128]{2,1,0:T(8,128)(2,1)S(1)} %all-to-all-done.1.pixels_ref.pixels_rest, bf16[128,16,128]{2,1,0:T(8,128)(2,1)S(1)} %slice.141.around_ref, f32[128,512]{1,0:T(8,128)S(1)} %bitcast.11, ...), custom_call_target="tpu_custom_call" | custom-call | flops 3221225472 | bytes 4194304 | tf_op jit(solution)/shard_map/pallas_call | solution.py:443
  155.5 0.9 copy-done.6
  156.4 9.4 %all-to-all-start.2 = ((bf16[128,24,128]{2,1,0:T(8,128)(2,1)}), bf16[128,24,128]{2,1,0:T(8,128)(2,1)S(1)}, u32[]{:S(2)}, u32[]{:S(2)}) async-start(bf16[128,24,128]{2,1,0:T(8,128)(2,1)} %copy-done.6), calls=%async_computation.2 | async-start | bytes 1572864 | tf_op jit(solution)/shard_map/all_to_all | solution.py:33
  165.8 1.2 fusion.16
  167.0 0.1 reshape.33
  167.1 0.7 slice_reduce_fusion
  167.8 0.3 fusion.7
  168.1 0.5 fusion
  168.7 13.5 %all-to-all-done.2.refs_0_ = bf16[128,24,128]{2,1,0:T(8,128)(2,1)S(1)} async-done(((bf16[128,24,128]{2,1,0:T(8,128)(2,1)}), bf16[128,24,128]{2,1,0:T(8,128)(2,1)S(1)}, u32[]{:S(2)}, u32[]{:S(2)}) %all-to-all-start.2) | async-done | bytes 786464 | tf_op jit(solution)/shard_map/all_to_all | solution.py:33
  182.2 0.9 copy-done.3
  183.2 1.6 shard_map.86
  184.8 0.7 copy-done
  185.5 0.8 copy-done.9
  186.3 4.3 %all-to-all-start.3 = ((bf16[128,16,128]{2,1,0:T(8,128)(2,1)}), bf16[128,16,128]{2,1,0:T(8,128)(2,1)S(1)}, u32[]{:S(2)}, u32[]{:S(2)}) async-start(bf16[128,16,128]{2,1,0:T(8,128)(2,1)} %copy-done.9), calls=%async_computation.3 | async-start | bytes 1048576 | tf_op jit(solution)/shard_map/all_to_all | solution.py:33
  190.6 0.7 fusion.21
  191.3 3.5 %collective-permute-start.4 = (f32[1,256]{1,0:T(1,128)S(1)}, f32[1,256]{1,0:T(1,128)S(1)}, u32[]{:S(2)}, u32[]{:S(2)}) collective-permute-start(f32[1,256]{1,0:T(1,128)S(1)} %get-tuple-element.43), channel_id=1, source_target_pairs={{0,16},{16,32},{32,48},{48,64},{64,80},{80,96},{96,112},{1,17},{17... | collective-permute-start | bytes 3080 | tf_op jit(solution)/shard_map/ppermute | solution.py:44
  194.9 2.1 collective-permute-start.5
  197.0 3.2 %collective-permute-done.5 = f32[1,256]{1,0:T(1,128)S(1)} collective-permute-done((f32[1,256]{1,0:T(1,128)S(1)}, f32[1,256]{1,0:T(1,128)S(1)}, u32[]{:S(2)}, u32[]{:S(2)}) %collective-permute-start.5) | collective-permute-done | bytes 1056 | tf_op jit(solution)/shard_map/ppermute | solution.py:45
  200.2 4.4 %all-to-all-done.3.around_ref = bf16[128,16,128]{2,1,0:T(8,128)(2,1)S(1)} async-done(((bf16[128,16,128]{2,1,0:T(8,128)(2,1)}), bf16[128,16,128]{2,1,0:T(8,128)(2,1)S(1)}, u32[]{:S(2)}, u32[]{:S(2)}) %all-to-all-start.3) | async-done | bytes 524320 | tf_op jit(solution)/shard_map/all_to_all | solution.py:33
  204.6 0.9 copy-done.5
  205.6 0.9 copy-done.8
  206.5 0.8 copy-done.11
  207.3 26.0 %shard_map.87 = bf16[128,24,128]{2,1,0:T(8,128)(2,1)} custom-call(s32[1]{0:T(128)} %bitcast.me_ref, f32[8,6144]{1,0:T(8,128)S(1)} %copy-done.8, bf16[128,216,128]{2,1,0:T(8,128)(2,1)} %all-to-all-done.pixels_ref, f32[8,2048]{1,0:T(8,128)S(1)} %copy-done.11, bf16[128,64,128]{2,1,0:T(8,128)(2,1)S(1)} %all-to-all-done.1.pixels_ref.pixels_rest, ...), custom_call_target="tpu_custom_call" | custom-call | tf_op jit(solution)/shard_map/pallas_call | solution.py:531
  233.3 4.4 %all-to-all-start.4 = ((bf16[128,24,128]{2,1,0:T(8,128)(2,1)}), bf16[128,24,128]{2,1,0:T(8,128)(2,1)S(1)}, u32[]{:S(2)}, u32[]{:S(2)}) async-start(bf16[128,24,128]{2,1,0:T(8,128)(2,1)} %shard_map.87), calls=%async_computation.4 | async-start | bytes 1572864 | tf_op jit(solution)/shard_map/all_to_all | solution.py:33
  237.8 0.1 fusion.20
  237.9 1.3 collective-permute-start.7
  239.2 4.0 %collective-permute-start.6 = (f32[256,1]{1,0:T(8,128)S(1)}, f32[256,1]{1,0:T(8,128)S(1)}, u32[]{:S(2)}, u32[]{:S(2)}) collective-permute-start(f32[256,1]{1,0:T(8,128)S(1)} %get-tuple-element.40), channel_id=1, source_target_pairs={{0,1},{1,2},{2,3},{3,4},{4,5},{5,6},{6,7},{7,8},{8,9},{9,10},{10,1... | collective-permute-start | bytes 3080 | tf_op jit(solution)/shard_map/ppermute | solution.py:44
  243.2 8.9 %collective-permute-done.7 = f32[256,1]{1,0:T(8,128)S(1)} collective-permute-done((f32[256,1]{1,0:T(8,128)S(1)}, f32[256,1]{1,0:T(8,128)S(1)}, u32[]{:S(2)}, u32[]{:S(2)}) %collective-permute-start.7) | collective-permute-done | bytes 1056 | tf_op jit(solution)/shard_map/ppermute | solution.py:45
  252.1 0.1 pad_maximum_fusion.1.refs_5_
  252.3 2.0 all-to-all-done.4.refs_0_
  254.2 1.8 shard_map.88
  (31 shorter events, 0.2 us)
Async XLA Ops:
  8.7 11.9 %copy-start.2 = (f32[256,256]{1,0:T(8,128)S(1)}, f32[256,256]{1,0:T(8,128)}, u32[]{:S(2)}) copy-start(f32[256,256]{1,0:T(8,128)} %get-tuple-element.17.refs_1_) | copy-start | bytes 786436
  8.7 100.8 %all-to-all-start = ((bf16[128,216,128]{2,1,0:T(8,128)(2,1)}), bf16[128,216,128]{2,1,0:T(8,128)(2,1)}, u32[]{:S(2)}, u32[]{:S(2)}) async-start(bf16[128,216,128]{2,1,0:T(8,128)(2,1)} %get-tuple-element.14), calls=%async_computation | async-start | bytes 14155776 | tf_op jit(solution)/shard_map/all_to_all | solution.py:33
  20.6 81.7 %collective-permute-start.1 = (f32[1,256]{1,0:T(1,128)S(1)}, f32[1,256]{1,0:T(1,128)S(1)}, u32[]{:S(2)}, u32[]{:S(2)}) collective-permute-start(f32[1,256]{1,0:T(1,128)S(1)} %get-tuple-element.47), channel_id=1, source_target_pairs={{16,0},{32,16},{48,32},{64,48},{80,64},{96,80},{112,96},{17,1},{33... | collective-permute-start | bytes 3080 | tf_op jit(solution)/shard_map/ppermute | solution.py:45
  23.6 78.6 %collective-permute-start = (f32[1,256]{1,0:T(1,128)S(1)}, f32[1,256]{1,0:T(1,128)S(1)}, u32[]{:S(2)}, u32[]{:S(2)}) collective-permute-start(f32[1,256]{1,0:T(1,128)S(1)} %get-tuple-element.46), channel_id=1, source_target_pairs={{0,16},{16,32},{32,48},{48,64},{64,80},{80,96},{96,112},{1,17},{17... | collective-permute-start | bytes 3080 | tf_op jit(solution)/shard_map/ppermute | solution.py:44
  26.3 76.0 %collective-permute-start.3 = (f32[256,1]{1,0:T(8,128)S(1)}, f32[256,1]{1,0:T(8,128)S(1)}, u32[]{:S(2)}, u32[]{:S(2)}) collective-permute-start(f32[256,1]{1,0:T(8,128)S(1)} %get-tuple-element.45), channel_id=1, source_target_pairs={{1,0},{2,1},{3,2},{4,3},{5,4},{6,5},{7,6},{8,7},{9,8},{10,9},{11,1... | collective-permute-start | bytes 3080 | tf_op jit(solution)/shard_map/ppermute | solution.py:45
  27.6 74.7 %collective-permute-start.2 = (f32[256,1]{1,0:T(8,128)S(1)}, f32[256,1]{1,0:T(8,128)S(1)}, u32[]{:S(2)}, u32[]{:S(2)}) collective-permute-start(f32[256,1]{1,0:T(8,128)S(1)} %get-tuple-element.44), channel_id=1, source_target_pairs={{0,1},{1,2},{2,3},{3,4},{4,5},{5,6},{6,7},{7,8},{8,9},{9,10},{10,1... | collective-permute-start | bytes 3080 | tf_op jit(solution)/shard_map/ppermute | solution.py:44
  109.5 37.3 %all-to-all-start.1 = ((bf16[128,64,128]{2,1,0:T(8,128)(2,1)}), bf16[128,64,128]{2,1,0:T(8,128)(2,1)S(1)}, u32[]{:S(2)}, u32[]{:S(2)}) async-start(bf16[128,64,128]{2,1,0:T(8,128)(2,1)} %shard_map.83), calls=%async_computation.1 | async-start | bytes 4194304 | tf_op jit(solution)/shard_map/all_to_all | solution.py:33
  124.8 22.0 %copy-start.4 = (f32[16,8,4,128]{3,1,2,0:T(8,128)}, f32[16,8,4,128]{3,1,2,0:T(8,128)S(1)}, u32[]{:S(2)}) copy-start(f32[16,8,4,128]{3,1,2,0:T(8,128)S(1)} %copy.17) | copy-start | bytes 786436
  126.2 20.6 %copy-start.10 = (f32[8,2048]{1,0:T(8,128)}, f32[8,2048]{1,0:T(8,128)S(1)}, u32[]{:S(2)}) copy-start(f32[8,2048]{1,0:T(8,128)S(1)} %pad_convert_fusion.1.meta_ref.meta_rest) | copy-start | bytes 196612
  144.5 0.7 copy-start.7
  145.2 1.2 copy-start.12
  146.8 1.4 copy-start.13
  155.5 0.9 copy-start.6
  156.4 25.8 %all-to-all-start.2 = ((bf16[128,24,128]{2,1,0:T(8,128)(2,1)}), bf16[128,24,128]{2,1,0:T(8,128)(2,1)S(1)}, u32[]{:S(2)}, u32[]{:S(2)}) async-start(bf16[128,24,128]{2,1,0:T(8,128)(2,1)} %copy-done.6), calls=%async_computation.2 | async-start | bytes 1572864 | tf_op jit(solution)/shard_map/all_to_all | solution.py:33
  182.2 1.0 copy-start.3
  184.8 0.7 copy-start
  185.5 0.8 copy-start.9
  186.3 18.4 %all-to-all-start.3 = ((bf16[128,16,128]{2,1,0:T(8,128)(2,1)}), bf16[128,16,128]{2,1,0:T(8,128)(2,1)S(1)}, u32[]{:S(2)}, u32[]{:S(2)}) async-start(bf16[128,16,128]{2,1,0:T(8,128)(2,1)} %copy-done.9), calls=%async_computation.3 | async-start | bytes 1048576 | tf_op jit(solution)/shard_map/all_to_all | solution.py:33
  191.3 5.6 %collective-permute-start.4 = (f32[1,256]{1,0:T(1,128)S(1)}, f32[1,256]{1,0:T(1,128)S(1)}, u32[]{:S(2)}, u32[]{:S(2)}) collective-permute-start(f32[1,256]{1,0:T(1,128)S(1)} %get-tuple-element.43), channel_id=1, source_target_pairs={{0,16},{16,32},{32,48},{48,64},{64,80},{80,96},{96,112},{1,17},{17... | collective-permute-start | bytes 3080 | tf_op jit(solution)/shard_map/ppermute | solution.py:44
  194.9 42.9 %copy-start.1 = (f32[256,256]{1,0:T(8,128)S(1)}, f32[256,256]{1,0:T(8,128)}, u32[]{:S(2)}) copy-start(f32[256,256]{1,0:T(8,128)} %copy-done) | copy-start | bytes 786436
  194.9 5.3 %collective-permute-start.5 = (f32[1,256]{1,0:T(1,128)S(1)}, f32[1,256]{1,0:T(1,128)S(1)}, u32[]{:S(2)}, u32[]{:S(2)}) collective-permute-start(f32[1,256]{1,0:T(1,128)S(1)} %get-tuple-element.42), channel_id=1, source_target_pairs={{16,0},{32,16},{48,32},{64,48},{80,64},{96,80},{112,96},{17,1},{33... | collective-permute-start | bytes 3080 | tf_op jit(solution)/shard_map/ppermute | solution.py:45
  204.6 1.0 copy-start.5
  205.6 0.9 copy-start.8
  206.5 0.8 copy-start.11
  233.3 20.9 %all-to-all-start.4 = ((bf16[128,24,128]{2,1,0:T(8,128)(2,1)}), bf16[128,24,128]{2,1,0:T(8,128)(2,1)S(1)}, u32[]{:S(2)}, u32[]{:S(2)}) async-start(bf16[128,24,128]{2,1,0:T(8,128)(2,1)} %shard_map.87), calls=%async_computation.4 | async-start | bytes 1572864 | tf_op jit(solution)/shard_map/all_to_all | solution.py:33
  237.9 14.3 %collective-permute-start.7 = (f32[256,1]{1,0:T(8,128)S(1)}, f32[256,1]{1,0:T(8,128)S(1)}, u32[]{:S(2)}, u32[]{:S(2)}) collective-permute-start(f32[256,1]{1,0:T(8,128)S(1)} %get-tuple-element.41), channel_id=1, source_target_pairs={{1,0},{2,1},{3,2},{4,3},{5,4},{6,5},{7,6},{8,7},{9,8},{10,9},{11,1... | collective-permute-start | bytes 3080 | tf_op jit(solution)/shard_map/ppermute | solution.py:45
  239.2 13.0 %collective-permute-start.6 = (f32[256,1]{1,0:T(8,128)S(1)}, f32[256,1]{1,0:T(8,128)S(1)}, u32[]{:S(2)}, u32[]{:S(2)}) collective-permute-start(f32[256,1]{1,0:T(8,128)S(1)} %get-tuple-element.40), channel_id=1, source_target_pairs={{0,1},{1,2},{2,3},{3,4},{4,5},{5,6},{6,7},{7,8},{8,9},{9,10},{10,1... | collective-permute-start | bytes 3080 | tf_op jit(solution)/shard_map/ppermute | solution.py:44

commit v6 on v4

--- a/solution.py
+++ b/solution.py
@@ -454,7 +454,7 @@
         scratch_shapes=[pltpu.VMEM(shape, dtype) for shape, dtype in scratch]
         + [pltpu.VMEM((half, 2 * SLAB), BF16)] * 2
         + [pltpu.VMEM((3 * DEVICES, half), BF16)] * 2,
-        compiler_params=pltpu.CompilerParams(vmem_limit_bytes=44 * 1024 * 1024),
+        compiler_params=pltpu.CompilerParams(vmem_limit_bytes=26 * 1024 * 1024),
         cost_estimate=pl.CostEstimate(
             flops=2 * 12 * DEVICES * cells, bytes_accessed=4 * cells, transcendentals=2 * cells
         ),
@@ -538,7 +538,7 @@
             pltpu.VMEM(shape, dtype) for shape, dtype in (SUMS, PLAIN, NORMALS, SLOPES, ROWS)
         ]
         + scratch,
-        compiler_params=pltpu.CompilerParams(vmem_limit_bytes=44 * 1024 * 1024),
+        compiler_params=pltpu.CompilerParams(vmem_limit_bytes=26 * 1024 * 1024),
     )(me, metas[0], pixels[0], metas[1], pixels[1], around, lit)
 
 
@@ -628,7 +628,7 @@
             pltpu.VMEM((DEVICES, LANES), F32),
             pltpu.VMEM((2 * TILE, LANES), F32),
         ],
-        compiler_params=pltpu.CompilerParams(vmem_limit_bytes=32 * 1024 * 1024),
+        compiler_params=pltpu.CompilerParams(vmem_limit_bytes=16 * 1024 * 1024),
     )(got, surface, hits, height_sum, ends, sides)
 
 

time: 256 us -> 256 us (level)
  no operation moved by 1% of the time
where the time goes in v6:
time: 256 us; the launch traced here: 252 us
  waiting for transfers between devices  92.6 us (36%)
  Pallas kernels  68 us (27%)
  starting transfers between devices  55.2 us (22%)
  blocking collectives  17.8 us (7%)
  local copies, waits for them, and re-layouts  14.7 us (6%)
  other arithmetic  2.8 us (1%)
    ppermute x4, waiting for transfers between devices, edges(): out.append(lax.ppermute(first, axis, down))  70.8 us
    all_to_all x4, starting transfers between devices, exchange(): return lax.all_to_all(value, AXES, split_axis=0, concat_axis=0, tiled=True)  33.3 us
    pallas_call x1, Pallas kernels, both_sums(): pl.pallas_call(both_kernel, grid=(STEPS[0] + STEPS[1],), in_specs=specs +...  26.1 us
    pallas_call x2, Pallas kernels, sum_call(): pl.pallas_call(kernel, grid=(DEVICES // sources,), in_specs=[pl.BlockSpec...  25.6 us
    all_to_all x4, waiting for transfers between devices, exchange(): return lax.all_to_all(value, AXES, split_axis=0, concat_axis=0, tiled=True)  21.8 us
    all_to_all x1, blocking collectives, exchange(): return lax.all_to_all(value, AXES, split_axis=0, concat_axis=0, tiled=True)  17.8 us
    ppermute x4, starting transfers between devices, edges(): out.append(lax.ppermute(last, axis, up))  13.2 us
    ppermute x4, starting transfers between devices, edges(): out.append(lax.ppermute(first, axis, down))  8.74 us
  transfers between devices with their start and end apart: 12, of which 6 were waited for; matrix products, arithmetic and copies ran while one was open for 5% of the time, Pallas kernels for 9%

profile of v6, /device:TPU:1, one launch (start us, length us, event | category | flops | bytes accessed | tf_op | source)
XLA Modules:
  0.0 252.0 jit_solution(15742566984476419590)
XLA Ops:
  0.0 8.7 %shard_map.82 = (bf16[128,216,128]{2,1,0:T(8,128)(2,1)}, f32[256,256]{1,0:T(8,128)}) custom-call(bf16[64,256,256]{2,1,0:T(8,128)(2,1)} %images_ref.3, f32[256,256]{1,0:T(8,128)} %heights_ref.1, s32[256,256]{1,0:T(8,128)} %shadow_ref.1, s32[1,64]{1,0:T(1,128)} %bitcast.18, bf16[4,64]{1,0:T(4,128)(2,1)} %bitcast.14, s32[1,256]{1,0:T(1,128)} %bitcast.15, ...), custom_call_target="tpu_custom_call" | custom-call | tf_op jit(solution)/shard_map/pallas_call | solution.py:197
  8.7 11.9 %all-to-all-start = ((bf16[128,216,128]{2,1,0:T(8,128)(2,1)}), bf16[128,216,128]{2,1,0:T(8,128)(2,1)}, u32[]{:S(2)}, u32[]{:S(2)}) async-start(bf16[128,216,128]{2,1,0:T(8,128)(2,1)} %get-tuple-element.11), calls=%async_computation | async-start | bytes 14155776 | tf_op jit(solution)/shard_map/all_to_all | solution.py:33
  20.6 3.0 %collective-permute-start.1 = (f32[1,256]{1,0:T(1,128)S(1)}, f32[1,256]{1,0:T(1,128)S(1)}, u32[]{:S(2)}, u32[]{:S(2)}) collective-permute-start(f32[1,256]{1,0:T(1,128)S(1)} %get-tuple-element.41), channel_id=1, source_target_pairs={{16,0},{32,16},{48,32},{64,48},{80,64},{96,80},{112,96},{17,1},{33... | collective-permute-start | bytes 3080 | tf_op jit(solution)/shard_map/ppermute | solution.py:45
  23.6 2.5 %collective-permute-start = (f32[1,256]{1,0:T(1,128)S(1)}, f32[1,256]{1,0:T(1,128)S(1)}, u32[]{:S(2)}, u32[]{:S(2)}) collective-permute-start(f32[1,256]{1,0:T(1,128)S(1)} %get-tuple-element.40), channel_id=1, source_target_pairs={{0,16},{16,32},{32,48},{48,64},{64,80},{80,96},{96,112},{1,17},{17... | collective-permute-start | bytes 3080 | tf_op jit(solution)/shard_map/ppermute | solution.py:44
  26.2 0.1 fusion.22
  26.3 1.3 collective-permute-start.3
  27.6 4.0 %collective-permute-start.2 = (f32[256,1]{1,0:T(8,128)S(1)}, f32[256,1]{1,0:T(8,128)S(1)}, u32[]{:S(2)}, u32[]{:S(2)}) collective-permute-start(f32[256,1]{1,0:T(8,128)S(1)} %get-tuple-element.38), channel_id=1, source_target_pairs={{0,1},{1,2},{2,3},{3,4},{4,5},{5,6},{6,7},{7,8},{8,9},{9,10},{10,1... | collective-permute-start | bytes 3080 | tf_op jit(solution)/shard_map/ppermute | solution.py:44
  31.6 4.3 %shard_map.83 = bf16[128,64,128]{2,1,0:T(8,128)(2,1)} custom-call(bf16[64,256,256]{2,1,0:T(8,128)(2,1)} %images_ref.3), custom_call_target="tpu_custom_call" | custom-call | flops 536870912 | bytes 4194304 | tf_op jit(solution)/shard_map/pallas_call | solution.py:226
  36.0 66.3 %collective-permute-done.1 = f32[1,256]{1,0:T(1,128)S(1)} collective-permute-done((f32[1,256]{1,0:T(1,128)S(1)}, f32[1,256]{1,0:T(1,128)S(1)}, u32[]{:S(2)}, u32[]{:S(2)}) %collective-permute-start.1) | collective-permute-done | bytes 1056 | tf_op jit(solution)/shard_map/ppermute | solution.py:45
  102.3 0.0 collective-permute-done
  102.3 0.0 collective-permute-done.3
  102.3 0.0 collective-permute-done.2
  102.3 0.1 pad_maximum_fusion.refs_5_
  102.4 7.1 %all-to-all-done.pixels_ref = bf16[128,216,128]{2,1,0:T(8,128)(2,1)} async-done(((bf16[128,216,128]{2,1,0:T(8,128)(2,1)}), bf16[128,216,128]{2,1,0:T(8,128)(2,1)}, u32[]{:S(2)}, u32[]{:S(2)}) %all-to-all-start) | async-done | bytes 7077920 | tf_op jit(solution)/shard_map/all_to_all | solution.py:33
  109.5 7.8 %all-to-all-start.1 = ((bf16[128,64,128]{2,1,0:T(8,128)(2,1)}), bf16[128,64,128]{2,1,0:T(8,128)(2,1)S(1)}, u32[]{:S(2)}, u32[]{:S(2)}) async-start(bf16[128,64,128]{2,1,0:T(8,128)(2,1)} %shard_map.83), calls=%async_computation.1 | async-start | bytes 4194304 | tf_op jit(solution)/shard_map/all_to_all | solution.py:33
  117.3 2.7 %slice_reduce_fusion.10 = (bf16[128,48]{1,0:T(8,128)(2,1)S(1)}, bf16[128,48]{1,0:T(8,128)(2,1)S(1)}, bf16[128,48]{1,0:T(8,128)(2,1)S(1)}, bf16[128,48]{1,0:T(8,128)(2,1)S(1)}, bf16[128,48]{1,0:T(8,128)(2,1)S(1)}) fusion(bf16[128,216,128]{2,1,0:T(8,128)(2,1)} %all-to-all-done.pixels_ref), kind=kLoop, calls=%fused_computation.38 | loop fusion | bytes 122880 | tf_op jit(solution)/shard_map/slice | solution.py:665
  120.0 2.8 %slice_reduce_fusion.5 = (bf16[128,16]{1,0:T(8,128)(2,1)S(1)}, bf16[128,16]{1,0:T(8,128)(2,1)S(1)}, bf16[128,16]{1,0:T(8,128)(2,1)S(1)}, bf16[128,16]{1,0:T(8,128)(2,1)S(1)}, bf16[128,16]{1,0:T(8,128)(2,1)S(1)}) fusion(bf16[128,216,128]{2,1,0:T(8,128)(2,1)} %all-to-all-done.pixels_ref), kind=kLoop, calls=%fused_computation.33 | loop fusion | bytes 40960 | tf_op jit(solution)/shard_map/slice | solution.py:665
  122.8 0.1 stack.26
  122.9 0.1 stack.27
  123.0 0.1 stack.28
  123.1 0.1 stack.29
  123.2 0.1 stack.30
  123.3 0.1 stack.32
  123.4 0.1 stack.33
  123.5 0.1 stack.34
  123.6 0.1 stack.35
  123.7 0.1 stack.36
  123.8 1.0 slice_convert_fusion
  124.8 0.2 stack.31
  125.0 0.1 stack.37
  125.1 1.1 slice.141.around_ref
  126.2 18.2 %shard_map.84 = (f32[384,1024]{1,0:T(8,128)S(1)}, f32[8,1024]{1,0:T(8,128)S(1)}) custom-call(s32[1]{0:T(128)} %bitcast.me_ref, f32[8,6144]{1,0:T(8,128)S(1)} %pad_convert_fusion.meta_ref, bf16[128,216,128]{2,1,0:T(8,128)(2,1)} %all-to-all-done.pixels_ref, bf16[128,16,128]{2,1,0:T(8,128)(2,1)S(1)} %slice.141.around_ref, f32[128,512]{1,0:T(8,128)S(1)} %bitcast.10), custom_call_target="tpu_custom_call" | custom-call | flops 9663676416 | bytes 12582912 | tf_op jit(solution)/shard_map/pallas_call | solution.py:443
  144.5 0.7 copy-done.7
  145.2 1.2 copy-done.11
  146.3 0.4 all-to-all-done.1.pixels_ref.pixels_rest
  146.8 1.4 copy-done.12
  148.2 7.4 %shard_map.85 = bf16[128,24,128]{2,1,0:T(8,128)(2,1)S(1)} custom-call(s32[1]{0:T(128)} %bitcast.me_ref, f32[8,2048]{1,0:T(8,128)S(1)} %pad_convert_fusion.1.meta_ref.meta_rest, bf16[128,64,128]{2,1,0:T(8,128)(2,1)S(1)} %all-to-all-done.1.pixels_ref.pixels_rest, bf16[128,16,128]{2,1,0:T(8,128)(2,1)S(1)} %slice.141.around_ref, f32[128,512]{1,0:T(8,128)S(1)} %bitcast.11, ...), custom_call_target="tpu_custom_call" | custom-call | flops 3221225472 | bytes 4194304 | tf_op jit(solution)/shard_map/pallas_call | solution.py:443
  155.6 0.9 copy-done.6
  156.4 9.4 %all-to-all-start.2 = ((bf16[128,24,128]{2,1,0:T(8,128)(2,1)}), bf16[128,24,128]{2,1,0:T(8,128)(2,1)S(1)}, u32[]{:S(2)}, u32[]{:S(2)}) async-start(bf16[128,24,128]{2,1,0:T(8,128)(2,1)} %copy-done.6), calls=%async_computation.2 | async-start | bytes 1572864 | tf_op jit(solution)/shard_map/all_to_all | solution.py:33
  165.8 1.2 fusion.16
  167.0 0.1 reshape.33
  167.1 0.7 slice_reduce_fusion
  167.8 0.3 fusion.7
  168.2 0.5 fusion
  168.7 0.1 slice_add_fusion
  168.7 13.5 %all-to-all-done.2.refs_0_ = bf16[128,24,128]{2,1,0:T(8,128)(2,1)S(1)} async-done(((bf16[128,24,128]{2,1,0:T(8,128)(2,1)}), bf16[128,24,128]{2,1,0:T(8,128)(2,1)S(1)}, u32[]{:S(2)}, u32[]{:S(2)}) %all-to-all-start.2) | async-done | bytes 786464 | tf_op jit(solution)/shard_map/all_to_all | solution.py:33
  182.3 0.9 copy-done.3
  183.2 1.6 shard_map.86
  184.8 0.0 copy-start
  184.8 0.7 copy-done
  185.5 17.8 %all_to_all.25.around_ref = bf16[128,16,128]{2,1,0:T(8,128)(2,1)S(1)} all-to-all(bf16[128,16,128]{2,1,0:T(8,128)(2,1)S(1)} %get-tuple-element.15), channel_id=1, replica_groups=mesh['row'=8,'col'=16] {'row','col'}, dimensions={0} | all-to-all | bytes 1048576 | tf_op jit(solution)/shard_map/all_to_all | solution.py:33
  203.3 0.0 copy-start.1
  203.3 26.1 %shard_map.87 = bf16[128,24,128]{2,1,0:T(8,128)(2,1)} custom-call(s32[1]{0:T(128)} %bitcast.me_ref, f32[8,6144]{1,0:T(8,128)S(1)} %copy-done.8, bf16[128,216,128]{2,1,0:T(8,128)(2,1)} %all-to-all-done.pixels_ref, f32[8,2048]{1,0:T(8,128)S(1)} %copy-done.10, bf16[128,64,128]{2,1,0:T(8,128)(2,1)S(1)} %all-to-all-done.1.pixels_ref.pixels_rest, ...), custom_call_target="tpu_custom_call" | custom-call | tf_op jit(solution)/shard_map/pallas_call | solution.py:531
  229.3 4.2 %all-to-all-start.4 = ((bf16[128,24,128]{2,1,0:T(8,128)(2,1)}), bf16[128,24,128]{2,1,0:T(8,128)(2,1)S(1)}, u32[]{:S(2)}, u32[]{:S(2)}) async-start(bf16[128,24,128]{2,1,0:T(8,128)(2,1)} %shard_map.87), calls=%async_computation.4 | async-start | bytes 1572864 | tf_op jit(solution)/shard_map/all_to_all | solution.py:33
  233.6 3.1 %collective-permute-start.5 = (f32[1,256]{1,0:T(1,128)S(1)}, f32[1,256]{1,0:T(1,128)S(1)}, u32[]{:S(2)}, u32[]{:S(2)}) collective-permute-start(f32[1,256]{1,0:T(1,128)S(1)} %get-tuple-element.37), channel_id=1, source_target_pairs={{16,0},{32,16},{48,32},{64,48},{80,64},{96,80},{112,96},{17,1},{33... | collective-permute-start | bytes 3080 | tf_op jit(solution)/shard_map/ppermute | solution.py:45
  236.7 2.4 collective-permute-start.4
  239.2 0.1 fusion.20
  239.3 1.3 collective-permute-start.7
  240.6 4.2 %collective-permute-start.6 = (f32[256,1]{1,0:T(8,128)S(1)}, f32[256,1]{1,0:T(8,128)S(1)}, u32[]{:S(2)}, u32[]{:S(2)}) collective-permute-start(f32[256,1]{1,0:T(8,128)S(1)} %get-tuple-element.34), channel_id=1, source_target_pairs={{0,1},{1,2},{2,3},{3,4},{4,5},{5,6},{6,7},{7,8},{8,9},{9,10},{10,1... | collective-permute-start | bytes 3080 | tf_op jit(solution)/shard_map/ppermute | solution.py:44
  244.8 0.0 collective-permute-done.5
  244.8 4.5 %collective-permute-done.7 = f32[256,1]{1,0:T(8,128)S(1)} collective-permute-done((f32[256,1]{1,0:T(8,128)S(1)}, f32[256,1]{1,0:T(8,128)S(1)}, u32[]{:S(2)}, u32[]{:S(2)}) %collective-permute-start.7) | collective-permute-done | bytes 1056 | tf_op jit(solution)/shard_map/ppermute | solution.py:45
  249.3 0.1 pad_maximum_fusion.1.refs_5_
  249.4 0.8 all-to-all-done.4.refs_0_
  250.2 1.8 shard_map.88
  (28 shorter events, 0.1 us)
Async XLA Ops:
  8.7 11.9 %copy-start.2 = (f32[256,256]{1,0:T(8,128)S(1)}, f32[256,256]{1,0:T(8,128)}, u32[]{:S(2)}) copy-start(f32[256,256]{1,0:T(8,128)} %get-tuple-element.14.refs_1_) | copy-start | bytes 786436
  8.7 100.8 %all-to-all-start = ((bf16[128,216,128]{2,1,0:T(8,128)(2,1)}), bf16[128,216,128]{2,1,0:T(8,128)(2,1)}, u32[]{:S(2)}, u32[]{:S(2)}) async-start(bf16[128,216,128]{2,1,0:T(8,128)(2,1)} %get-tuple-element.11), calls=%async_computation | async-start | bytes 14155776 | tf_op jit(solution)/shard_map/all_to_all | solution.py:33
  20.6 81.7 %collective-permute-start.1 = (f32[1,256]{1,0:T(1,128)S(1)}, f32[1,256]{1,0:T(1,128)S(1)}, u32[]{:S(2)}, u32[]{:S(2)}) collective-permute-start(f32[1,256]{1,0:T(1,128)S(1)} %get-tuple-element.41), channel_id=1, source_target_pairs={{16,0},{32,16},{48,32},{64,48},{80,64},{96,80},{112,96},{17,1},{33... | collective-permute-start | bytes 3080 | tf_op jit(solution)/shard_map/ppermute | solution.py:45
  23.6 78.6 %collective-permute-start = (f32[1,256]{1,0:T(1,128)S(1)}, f32[1,256]{1,0:T(1,128)S(1)}, u32[]{:S(2)}, u32[]{:S(2)}) collective-permute-start(f32[1,256]{1,0:T(1,128)S(1)} %get-tuple-element.40), channel_id=1, source_target_pairs={{0,16},{16,32},{32,48},{48,64},{64,80},{80,96},{96,112},{1,17},{17... | collective-permute-start | bytes 3080 | tf_op jit(solution)/shard_map/ppermute | solution.py:44
  26.3 76.0 %collective-permute-start.3 = (f32[256,1]{1,0:T(8,128)S(1)}, f32[256,1]{1,0:T(8,128)S(1)}, u32[]{:S(2)}, u32[]{:S(2)}) collective-permute-start(f32[256,1]{1,0:T(8,128)S(1)} %get-tuple-element.39), channel_id=1, source_target_pairs={{1,0},{2,1},{3,2},{4,3},{5,4},{6,5},{7,6},{8,7},{9,8},{10,9},{11,1... | collective-permute-start | bytes 3080 | tf_op jit(solution)/shard_map/ppermute | solution.py:45
  27.6 74.7 %collective-permute-start.2 = (f32[256,1]{1,0:T(8,128)S(1)}, f32[256,1]{1,0:T(8,128)S(1)}, u32[]{:S(2)}, u32[]{:S(2)}) collective-permute-start(f32[256,1]{1,0:T(8,128)S(1)} %get-tuple-element.38), channel_id=1, source_target_pairs={{0,1},{1,2},{2,3},{3,4},{4,5},{5,6},{6,7},{7,8},{8,9},{9,10},{10,1... | collective-permute-start | bytes 3080 | tf_op jit(solution)/shard_map/ppermute | solution.py:44
  109.5 37.3 %all-to-all-start.1 = ((bf16[128,64,128]{2,1,0:T(8,128)(2,1)}), bf16[128,64,128]{2,1,0:T(8,128)(2,1)S(1)}, u32[]{:S(2)}, u32[]{:S(2)}) async-start(bf16[128,64,128]{2,1,0:T(8,128)(2,1)} %shard_map.83), calls=%async_computation.1 | async-start | bytes 4194304 | tf_op jit(solution)/shard_map/all_to_all | solution.py:33
  124.8 22.0 %copy-start.4 = (f32[16,8,4,128]{3,1,2,0:T(8,128)}, f32[16,8,4,128]{3,1,2,0:T(8,128)S(1)}, u32[]{:S(2)}) copy-start(f32[16,8,4,128]{3,1,2,0:T(8,128)S(1)} %copy.17) | copy-start | bytes 786436
  126.2 20.6 %copy-start.9 = (f32[8,2048]{1,0:T(8,128)}, f32[8,2048]{1,0:T(8,128)S(1)}, u32[]{:S(2)}) copy-start(f32[8,2048]{1,0:T(8,128)S(1)} %pad_convert_fusion.1.meta_ref.meta_rest) | copy-start | bytes 196612
  144.5 0.7 copy-start.7
  145.2 1.2 copy-start.11
  146.8 1.4 copy-start.12
  155.5 0.9 copy-start.6
  156.4 25.8 %all-to-all-start.2 = ((bf16[128,24,128]{2,1,0:T(8,128)(2,1)}), bf16[128,24,128]{2,1,0:T(8,128)(2,1)S(1)}, u32[]{:S(2)}, u32[]{:S(2)}) async-start(bf16[128,24,128]{2,1,0:T(8,128)(2,1)} %copy-done.6), calls=%async_computation.2 | async-start | bytes 1572864 | tf_op jit(solution)/shard_map/all_to_all | solution.py:33
  182.3 1.0 copy-start.3
  183.2 20.0 %copy-start.5 = (f32[16,8,4,128]{3,1,2,0:T(8,128)S(1)}, f32[16,8,4,128]{3,1,2,0:T(8,128)}, u32[]{:S(2)}) copy-start(f32[16,8,4,128]{3,1,2,0:T(8,128)} %copy-done.4) | copy-start | bytes 786436
  183.2 20.0 %copy-start.8 = (f32[8,6144]{1,0:T(8,128)S(1)}, f32[8,6144]{1,0:T(8,128)}, u32[]{:S(2)}) copy-start(f32[8,6144]{1,0:T(8,128)} %copy-done.7) | copy-start | bytes 589828
  183.2 20.0 %copy-start.10 = (f32[8,2048]{1,0:T(8,128)S(1)}, f32[8,2048]{1,0:T(8,128)}, u32[]{:S(2)}) copy-start(f32[8,2048]{1,0:T(8,128)} %copy-done.9) | copy-start | bytes 196612
  184.8 0.7 copy-start
  203.3 30.3 %copy-start.1 = (f32[256,256]{1,0:T(8,128)S(1)}, f32[256,256]{1,0:T(8,128)}, u32[]{:S(2)}) copy-start(f32[256,256]{1,0:T(8,128)} %copy-done) | copy-start | bytes 786436
  229.3 20.8 %all-to-all-start.4 = ((bf16[128,24,128]{2,1,0:T(8,128)(2,1)}), bf16[128,24,128]{2,1,0:T(8,128)(2,1)S(1)}, u32[]{:S(2)}, u32[]{:S(2)}) async-start(bf16[128,24,128]{2,1,0:T(8,128)(2,1)} %shard_map.87), calls=%async_computation.4 | async-start | bytes 1572864 | tf_op jit(solution)/shard_map/all_to_all | solution.py:33
  233.6 11.2 %collective-permute-start.5 = (f32[1,256]{1,0:T(1,128)S(1)}, f32[1,256]{1,0:T(1,128)S(1)}, u32[]{:S(2)}, u32[]{:S(2)}) collective-permute-start(f32[1,256]{1,0:T(1,128)S(1)} %get-tuple-element.37), channel_id=1, source_target_pairs={{16,0},{32,16},{48,32},{64,48},{80,64},{96,80},{112,96},{17,1},{33... | collective-permute-start | bytes 3080 | tf_op jit(solution)/shard_map/ppermute | solution.py:45
  236.7 8.1 %collective-permute-start.4 = (f32[1,256]{1,0:T(1,128)S(1)}, f32[1,256]{1,0:T(1,128)S(1)}, u32[]{:S(2)}, u32[]{:S(2)}) collective-permute-start(f32[1,256]{1,0:T(1,128)S(1)} %get-tuple-element.36), channel_id=1, source_target_pairs={{0,16},{16,32},{32,48},{48,64},{64,80},{80,96},{96,112},{1,17},{17... | collective-permute-start | bytes 3080 | tf_op jit(solution)/shard_map/ppermute | solution.py:44
  239.3 10.0 %collective-permute-start.7 = (f32[256,1]{1,0:T(8,128)S(1)}, f32[256,1]{1,0:T(8,128)S(1)}, u32[]{:S(2)}, u32[]{:S(2)}) collective-permute-start(f32[256,1]{1,0:T(8,128)S(1)} %get-tuple-element.35), channel_id=1, source_target_pairs={{1,0},{2,1},{3,2},{4,3},{5,4},{6,5},{7,6},{8,7},{9,8},{10,9},{11,1... | collective-permute-start | bytes 3080 | tf_op jit(solution)/shard_map/ppermute | solution.py:45
  240.6 8.7 %collective-permute-start.6 = (f32[256,1]{1,0:T(8,128)S(1)}, f32[256,1]{1,0:T(8,128)S(1)}, u32[]{:S(2)}, u32[]{:S(2)}) collective-permute-start(f32[256,1]{1,0:T(8,128)S(1)} %get-tuple-element.34), channel_id=1, source_target_pairs={{0,1},{1,2},{2,3},{3,4},{4,5},{5,6},{6,7},{7,8},{8,9},{9,10},{10,1... | collective-permute-start | bytes 3080 | tf_op jit(solution)/shard_map/ppermute | solution.py:44
